TPU v7x, 32 devices: a whole 2x2x4 slice. The times are simulated.
32 devices in a mesh: dp: 2 (over x), seq: 8 (over z, y), mp: 2 (over core).
Axes of the slice: x: 2, y: 2, z: 4, core: 2. Of those that a mesh axis runs over, the one named last changes fastest.
Arguments:
- hidden_in: bfloat16 [4, 1024, 2048], P('dp', 'seq'), may hold values from -6 to 6
- doc_lengths: int32 [4, 4], P('dp'), may hold values from 1 to 1020, as said below
- attn_gain: bfloat16 [2048], P(('dp', 'seq')), may hold values from 0.5 to 1.5
- query_weight: bfloat16 [2048, 2048], P(('dp', 'seq'), 'mp'), may hold values from -0.125 to 0.125
- key_weight: bfloat16 [2048, 512], P(('dp', 'seq'), 'mp'), may hold values from -0.125 to 0.125
- value_weight: bfloat16 [2048, 512], P(('dp', 'seq'), 'mp'), may hold values from -0.125 to 0.125
- output_weight: bfloat16 [2048, 2048], P('mp', ('dp', 'seq')), may hold values from -2 to 2
- ffn_gain: bfloat16 [2048], P(('dp', 'seq')), may hold values from 0.5 to 1.5
- gate_weight: bfloat16 [2048, 8192], P(('dp', 'seq'), 'mp'), may hold values from -0.125 to 0.125
- up_weight: bfloat16 [2048, 8192], P(('dp', 'seq'), 'mp'), may hold values from -0.125 to 0.125
- down_weight: bfloat16 [8192, 2048], P('mp', ('dp', 'seq')), may hold values from -0.0625 to 0.0625
- out_grad: bfloat16 [4, 1024, 2048], P('dp', 'seq'), may hold values from -6 to 6
Outputs:
- layer_out: bfloat16 [4, 1024, 2048], P('dp', 'seq')
- input_grad: bfloat16 [4, 1024, 2048], P('dp', 'seq')
- attn_gain_grad: float32 [2048], P(('dp', 'seq'))
- query_grad: float32 [2048, 2048], P(('dp', 'seq'), 'mp')
- key_grad: float32 [2048, 512], P(('dp', 'seq'), 'mp')
- value_grad: float32 [2048, 512], P(('dp', 'seq'), 'mp')
- output_grad: float32 [2048, 2048], P('mp', ('dp', 'seq'))
- ffn_gain_grad: float32 [2048], P(('dp', 'seq'))
- gate_grad: float32 [2048, 8192], P(('dp', 'seq'), 'mp')
- up_grad: float32 [2048, 8192], P(('dp', 'seq'), 'mp')
- down_grad: float32 [8192, 2048], P('mp', ('dp', 'seq'))
Inputs may be any that keep to these rules, and one draw needn't show every extreme that they name: `doc_lengths`: in each row the lengths sum to less than 1024; the positions after the last document are padding. In each row one document starts within the first 128 positions and ends within the last 128.
All inputs are finite; a program needn't handle non-finite values.
Results may differ from a plain program's by a relative error of at most 0.018.
Values may be sent and summed in bfloat16 or wider, within the bound.
A program may use at most 256 MiB of HBM per device.

v0:
```python
import math

import jax
import jax.numpy as jnp
from jax import lax
from jax.sharding import PartitionSpec as P

H = 32
KVH = 8
HD = 64


EPSILON = 1e-05
MASKED = -1e30
ROPE_THETA = 500000.0
ROPE_FACTOR = 32.0
LOW_FACTOR = 1.0
HIGH_FACTOR = 4.0
PRIOR_CONTEXT = 8192.0


def inverse_freqs(head_dim):
    ladder = jnp.arange(head_dim // 2, dtype=jnp.float32)
    base = ROPE_THETA ** (-2.0 * ladder / head_dim)
    wavelen = 2.0 * math.pi / base
    smooth = (PRIOR_CONTEXT / wavelen - LOW_FACTOR) / (HIGH_FACTOR - LOW_FACTOR)
    blended = (1.0 - smooth) * base / ROPE_FACTOR + smooth * base
    low_limit = PRIOR_CONTEXT / LOW_FACTOR
    high_limit = PRIOR_CONTEXT / HIGH_FACTOR
    return jnp.where(
        wavelen < high_limit, base, jnp.where(wavelen > low_limit, base / ROPE_FACTOR, blended)
    )


def rope_tables(position, head_dim):
    angles = position[..., None] * inverse_freqs(head_dim)
    angles = jnp.concatenate([angles, angles], axis=-1)
    return (jnp.cos(angles)[..., None, :], jnp.sin(angles)[..., None, :])


def rotate(values, cosine, sine):
    middle = values.shape[-1] // 2
    turned = jnp.concatenate([-values[..., middle:], values[..., :middle]], axis=-1)
    return values * cosine + turned * sine


def unrotate(grads, cosine, sine):
    middle = grads.shape[-1] // 2
    scaled = grads * sine
    turned = jnp.concatenate([scaled[..., middle:], -scaled[..., :middle]], axis=-1)
    return grads * cosine + turned


def doc_tables(lengths, total_len):
    ends = jnp.cumsum(lengths, axis=-1)
    starts = ends - lengths
    places = jnp.arange(total_len, dtype=jnp.int32)
    doc_count = lengths.shape[-1]
    doc_index = jnp.sum((places[None, :, None] >= ends[:, None, :]).astype(jnp.int32), axis=-1)
    segment = jnp.where(doc_index < doc_count, doc_index + 1, 0)
    bounds = jnp.concatenate([starts, ends[:, -1:]], axis=-1)
    chosen = doc_index[:, :, None] == jnp.arange(doc_count + 1, dtype=jnp.int32)[None, None, :]
    begin = jnp.sum(jnp.where(chosen, bounds[:, None, :], 0), axis=-1)
    position = (places[None, :] - begin).astype(jnp.float32)
    return (segment, position)


def contract_rows(left, right):
    return lax.dot_general(
        left, right, (((0,), (0,)), ((), ())), preferred_element_type=jnp.float32
    )


def contract_cols(left, right):
    return lax.dot_general(
        left, right, (((1,), (1,)), ((), ())), preferred_element_type=jnp.float32
    )


def norm_back(values, scale, gain, grad):
    weighted = grad * gain
    gain_grad = jnp.sum(grad * values * scale, axis=0)
    inner = jnp.mean(weighted * values, axis=-1, keepdims=True)
    return (weighted * scale - values * scale**3 * inner, gain_grad)


def shards(
    hidden_in,
    doc_lengths,
    attn_gain,
    query_weight,
    key_weight,
    value_weight,
    output_weight,
    ffn_gain,
    gate_weight,
    up_weight,
    down_weight,
    out_grad,
):
    row_count, local_len, model_width = hidden_in.shape
    head_dim = HD
    key_heads = key_weight.shape[1] // head_dim
    group_size = H // KVH
    query_heads = key_heads * group_size
    full_len = local_len * lax.axis_size("seq")
    offset = lax.axis_index("seq") * local_len
    tokens = row_count * local_len
    last_query = offset + local_len - 1
    key_block = min(512, full_len)
    block_count = full_len // key_block
    score_scale = head_dim ** (-0.5)
    segment_all, position_all = doc_tables(doc_lengths, full_len)
    query_segment = lax.dynamic_slice_in_dim(segment_all, offset, local_len, 1)
    query_position = lax.dynamic_slice_in_dim(position_all, offset, local_len, 1)
    query_places = offset + jnp.arange(local_len, dtype=jnp.int32)
    cosine, sine = rope_tables(query_position, head_dim)
    gain_one, query_full, key_full, value_full, output_full = (
        lax.all_gather(attn_gain, ("dp", "seq"), axis=0, tiled=True),
        lax.all_gather(query_weight, ("dp", "seq"), axis=0, tiled=True),
        lax.all_gather(key_weight, ("dp", "seq"), axis=0, tiled=True),
        lax.all_gather(value_weight, ("dp", "seq"), axis=0, tiled=True),
        lax.all_gather(output_weight, ("dp", "seq"), axis=1, tiled=True),
    )
    inputs = hidden_in.reshape(tokens, model_width).astype(jnp.float32)
    scale_one = lax.rsqrt(jnp.mean(inputs * inputs, axis=-1, keepdims=True) + EPSILON)
    normed_one = (inputs * scale_one * gain_one).astype(jnp.bfloat16)
    query_pre = jnp.dot(normed_one, query_full, preferred_element_type=jnp.float32)
    key_pre = jnp.dot(normed_one, key_full, preferred_element_type=jnp.float32)
    value_pre = jnp.dot(normed_one, value_full, preferred_element_type=jnp.float32)
    queries = rotate(query_pre.reshape(row_count, local_len, query_heads, head_dim), cosine, sine)
    queries = queries.astype(jnp.bfloat16).reshape(
        row_count, local_len, key_heads, group_size, head_dim
    )
    keys_local = rotate(key_pre.reshape(row_count, local_len, key_heads, head_dim), cosine, sine)
    keys_local = keys_local.astype(jnp.bfloat16).reshape(row_count, local_len, key_heads * head_dim)
    values_local = value_pre.astype(jnp.bfloat16).reshape(
        row_count, local_len, key_heads * head_dim
    )
    keys_all, values_all = (
        lax.all_gather(keys_local, "seq", axis=1, tiled=True),
        lax.all_gather(values_local, "seq", axis=1, tiled=True),
    )

    def score_block(start):
        keys_block = lax.dynamic_slice_in_dim(keys_all, start, key_block, 1).reshape(
            row_count, key_block, key_heads, head_dim
        )
        values_block = lax.dynamic_slice_in_dim(values_all, start, key_block, 1).reshape(
            row_count, key_block, key_heads, head_dim
        )
        key_segment = lax.dynamic_slice_in_dim(segment_all, start, key_block, 1)
        key_places = start + jnp.arange(key_block, dtype=jnp.int32)
        allowed = (query_segment[:, :, None] == key_segment[:, None, :]) & (
            query_places[None, :, None] >= key_places[None, None, :]
        )
        allowed = allowed[:, None, None, :, :]
        scores = (
            jnp.einsum("rikgd,rjkd->rkgij", queries, keys_block, preferred_element_type=jnp.float32)
            * score_scale
        )
        return (jnp.where(allowed, scores, MASKED), allowed, keys_block, values_block)

    def stats_step(index, carry):
        start = index * key_block

        def stats_update(state):
            run_max, run_sum = state
            masked, allowed, keys_block, values_block = score_block(start)
            new_max = jnp.maximum(run_max, jnp.max(masked, axis=-1))
            fresh = jnp.where(allowed, jnp.exp(masked - new_max[..., None]), 0.0)
            return (new_max, run_sum * jnp.exp(run_max - new_max) + jnp.sum(fresh, axis=-1))

        return lax.cond(start <= last_query, stats_update, lambda state: state, carry)

    stat_shape = (row_count, key_heads, group_size, local_len)
    run_max, run_sum = lax.fori_loop(
        0,
        block_count,
        stats_step,
        (jnp.full(stat_shape, MASKED, jnp.float32), jnp.zeros(stat_shape, jnp.float32)),
    )
    log_total = run_max + jnp.log(run_sum)

    def output_step(index, carry):
        start = index * key_block

        def output_update(summed):
            masked, allowed, keys_block, values_block = score_block(start)
            attn_probs = jnp.exp(masked - log_total[..., None]).astype(jnp.bfloat16)
            return summed + jnp.einsum(
                "rkgij,rjkd->rikgd", attn_probs, values_block, preferred_element_type=jnp.float32
            )

        return lax.cond(start <= last_query, output_update, lambda summed: summed, carry)

    out_shape = (row_count, local_len, key_heads, group_size, head_dim)
    attn_five = lax.fori_loop(0, block_count, output_step, jnp.zeros(out_shape, jnp.float32))
    attn_low = attn_five.reshape(tokens, query_heads * head_dim).astype(jnp.bfloat16)
    attn_branch = lax.psum(
        jnp.dot(attn_low, output_full, preferred_element_type=jnp.float32).astype(jnp.bfloat16),
        "mp",
    ).astype(jnp.float32)
    residual = inputs + attn_branch
    gain_two, gate_full, up_full, down_full = (
        lax.all_gather(ffn_gain, ("dp", "seq"), axis=0, tiled=True),
        lax.all_gather(gate_weight, ("dp", "seq"), axis=0, tiled=True),
        lax.all_gather(up_weight, ("dp", "seq"), axis=0, tiled=True),
        lax.all_gather(down_weight, ("dp", "seq"), axis=1, tiled=True),
    )
    scale_two = lax.rsqrt(jnp.mean(residual * residual, axis=-1, keepdims=True) + EPSILON)
    normed_two = (residual * scale_two * gain_two).astype(jnp.bfloat16)
    gate_proj = jnp.dot(normed_two, gate_full, preferred_element_type=jnp.float32)
    up_proj = jnp.dot(normed_two, up_full, preferred_element_type=jnp.float32)
    silu_gate = jax.nn.silu(gate_proj)
    hidden_units = (silu_gate * up_proj).astype(jnp.bfloat16)
    ffn_branch = lax.psum(
        jnp.dot(hidden_units, down_full, preferred_element_type=jnp.float32).astype(jnp.bfloat16),
        "mp",
    ).astype(jnp.float32)
    layer_out = (
        (residual + ffn_branch).astype(jnp.bfloat16).reshape(row_count, local_len, model_width)
    )
    gain_two_back, gate_back, up_back, down_back = (gain_two, gate_full, up_full, down_full)
    grad_low = out_grad.reshape(tokens, model_width)
    down_grad = contract_rows(hidden_units, grad_low)
    hidden_grad = contract_cols(grad_low, down_back)
    sigmoid_gate = jax.nn.sigmoid(gate_proj)
    gate_act = (
        hidden_grad * up_proj * sigmoid_gate * (1.0 + gate_proj * (1.0 - sigmoid_gate))
    ).astype(jnp.bfloat16)
    up_act = (hidden_grad * silu_gate).astype(jnp.bfloat16)
    gate_grad = contract_rows(normed_two, gate_act)
    up_grad = contract_rows(normed_two, up_act)
    normed_two_grad = lax.psum(
        (contract_cols(gate_act, gate_back) + contract_cols(up_act, up_back)).astype(jnp.bfloat16),
        "mp",
    ).astype(jnp.float32)
    residual_part, ffn_gain_grad = norm_back(residual, scale_two, gain_two_back, normed_two_grad)
    residual_grad = grad_low.astype(jnp.float32) + residual_part
    ffn_gain_grad, gate_grad, up_grad, down_grad = (
        lax.psum_scatter(ffn_gain_grad, ("dp", "seq"), scatter_dimension=0, tiled=True),
        lax.psum_scatter(gate_grad, ("dp", "seq"), scatter_dimension=0, tiled=True),
        lax.psum_scatter(up_grad, ("dp", "seq"), scatter_dimension=0, tiled=True),
        lax.psum_scatter(down_grad, ("dp", "seq"), scatter_dimension=1, tiled=True),
    )
    gain_one_back, query_back, key_back, value_back, output_back = (
        gain_one,
        query_full,
        key_full,
        value_full,
        output_full,
    )
    residual_low = residual_grad.astype(jnp.bfloat16)
    output_grad = contract_rows(attn_low, residual_low)
    attn_grad = contract_cols(residual_low, output_back).astype(jnp.bfloat16).reshape(out_shape)
    delta_rows = jnp.transpose(jnp.sum(attn_grad * attn_five, axis=-1), (0, 2, 3, 1))

    def back_step(index, carry):
        start = index * key_block

        def back_update(state):
            query_acc, key_acc, value_acc = state
            masked, allowed, keys_block, values_block = score_block(start)
            attn_probs = jnp.exp(masked - log_total[..., None])
            probs_low = attn_probs.astype(jnp.bfloat16)
            value_part = jnp.einsum(
                "rkgij,rikgd->rjkd", probs_low, attn_grad, preferred_element_type=jnp.float32
            )
            prob_grad = jnp.einsum(
                "rikgd,rjkd->rkgij", attn_grad, values_block, preferred_element_type=jnp.float32
            )
            score_grad = (attn_probs * (prob_grad - delta_rows[..., None])).astype(jnp.bfloat16)
            query_acc = (
                query_acc
                + jnp.einsum(
                    "rkgij,rjkd->rikgd", score_grad, keys_block, preferred_element_type=jnp.float32
                )
                * score_scale
            )
            key_part = (
                jnp.einsum(
                    "rkgij,rikgd->rjkd", score_grad, queries, preferred_element_type=jnp.float32
                )
                * score_scale
            )
            key_acc = lax.dynamic_update_slice_in_dim(key_acc, key_part, start, 1)
            value_acc = lax.dynamic_update_slice_in_dim(value_acc, value_part, start, 1)
            return (query_acc, key_acc, value_acc)

        return lax.cond(start <= last_query, back_update, lambda state: state, carry)

    whole_shape = (row_count, full_len, key_heads, head_dim)
    query_acc, key_acc, value_acc = lax.fori_loop(
        0,
        block_count,
        back_step,
        (
            jnp.zeros(out_shape, jnp.float32),
            jnp.zeros(whole_shape, jnp.float32),
            jnp.zeros(whole_shape, jnp.float32),
        ),
    )
    key_sum, value_sum = (
        lax.psum_scatter(
            key_acc.reshape(row_count, full_len, key_heads * head_dim).astype(jnp.bfloat16),
            "seq",
            scatter_dimension=1,
            tiled=True,
        ).astype(jnp.float32),
        lax.psum_scatter(
            value_acc.reshape(row_count, full_len, key_heads * head_dim).astype(jnp.bfloat16),
            "seq",
            scatter_dimension=1,
            tiled=True,
        ).astype(jnp.float32),
    )
    query_pre_grad = unrotate(
        query_acc.reshape(row_count, local_len, query_heads, head_dim), cosine, sine
    )
    query_pre_grad = query_pre_grad.astype(jnp.bfloat16).reshape(tokens, query_heads * head_dim)
    key_pre_grad = unrotate(
        key_sum.reshape(row_count, local_len, key_heads, head_dim), cosine, sine
    )
    key_pre_grad = key_pre_grad.astype(jnp.bfloat16).reshape(tokens, key_heads * head_dim)
    value_pre_grad = value_sum.astype(jnp.bfloat16).reshape(tokens, key_heads * head_dim)
    query_grad = contract_rows(normed_one, query_pre_grad)
    key_grad = contract_rows(normed_one, key_pre_grad)
    value_grad = contract_rows(normed_one, value_pre_grad)
    normed_one_grad = lax.psum(
        (
            contract_cols(query_pre_grad, query_back)
            + contract_cols(key_pre_grad, key_back)
            + contract_cols(value_pre_grad, value_back)
        ).astype(jnp.bfloat16),
        "mp",
    ).astype(jnp.float32)
    input_part, attn_gain_grad = norm_back(inputs, scale_one, gain_one_back, normed_one_grad)
    input_grad = (
        (residual_grad + input_part).astype(jnp.bfloat16).reshape(row_count, local_len, model_width)
    )
    attn_gain_grad, query_grad, key_grad, value_grad, output_grad = (
        lax.psum_scatter(attn_gain_grad, ("dp", "seq"), scatter_dimension=0, tiled=True),
        lax.psum_scatter(query_grad, ("dp", "seq"), scatter_dimension=0, tiled=True),
        lax.psum_scatter(key_grad, ("dp", "seq"), scatter_dimension=0, tiled=True),
        lax.psum_scatter(value_grad, ("dp", "seq"), scatter_dimension=0, tiled=True),
        lax.psum_scatter(output_grad, ("dp", "seq"), scatter_dimension=1, tiled=True),
    )
    return (
        layer_out,
        input_grad,
        attn_gain_grad,
        query_grad,
        key_grad,
        value_grad,
        output_grad,
        ffn_gain_grad,
        gate_grad,
        up_grad,
        down_grad,
    )


def solution(mesh):
    return jax.shard_map(
        shards,
        mesh=mesh,
        in_specs=(
            P("dp", "seq", None),
            P("dp", None),
            P(("dp", "seq")),
            P(("dp", "seq"), "mp"),
            P(("dp", "seq"), "mp"),
            P(("dp", "seq"), "mp"),
            P("mp", ("dp", "seq")),
            P(("dp", "seq")),
            P(("dp", "seq"), "mp"),
            P(("dp", "seq"), "mp"),
            P("mp", ("dp", "seq")),
            P("dp", "seq", None),
        ),
        out_specs=(
            P("dp", "seq", None),
            P("dp", "seq", None),
            P(("dp", "seq")),
            P(("dp", "seq"), "mp"),
            P(("dp", "seq"), "mp"),
            P(("dp", "seq"), "mp"),
            P("mp", ("dp", "seq")),
            P(("dp", "seq")),
            P(("dp", "seq"), "mp"),
            P(("dp", "seq"), "mp"),
            P("mp", ("dp", "seq")),
        ),
        check_vma=False,
    )
```

profile of v0, /device:TPU:0, one launch (start us, length us, event | category | flops | bytes accessed | tf_op | source)
XLA Modules:
  0.0 3879.3 jit_solution(7548772751389506490)
XLA Ops:
  11.1 42.3 %all-gather = bf16[16,1,128]{2,1,0:T(2,128)(2,1)S(1)} all-gather(bf16[1,1,128]{2,1,0:T(2,128)(2,1)} %bitcast.326), channel_id=1, replica_groups=mesh['dp'=2,'seq'=8,'mp'=2] {'dp','seq'}, dimensions={0}, use_global_device_ids=true | all-gather | bytes 4352 | tf_op jit(solution)/shard_map/all_gather | solution.py:119
  54.2 1.7 fusion.62
  56.3 12.7 all-gather.16.cloned.1.call-done
  69.0 2.3 copy.112
  71.2 1.7 fusion.73
  74.1 51.9 %all-gather.12.cloned.1.call-done = bf16[2048,256]{1,0:T(8,128)(2,1)} async-done(((bf16[128,256]{1,0:T(8,128)(2,1)}), bf16[2048,256]{1,0:T(8,128)(2,1)}) %all-gather.12.cloned.1.call-update) | async-done | bytes 1048592 | tf_op jit(solution)/shard_map/all_gather | solution.py:122
  126.0 1.7 convolution_convert_fusion.3
  129.3 74.1 %all-gather.20.cloned.1.call-done = bf16[2048,1024]{1,0:T(8,128)(2,1)} async-done(((bf16[128,1024]{1,0:T(8,128)(2,1)}), bf16[2048,1024]{1,0:T(8,128)(2,1)}) %all-gather.20.cloned.1.call-update) | async-done | bytes 4194320 | tf_op jit(solution)/shard_map/all_gather | solution.py:120
  203.4 6.5 copy.114
  209.9 3.5 fusion.71
  213.7 30.3 all-gather.18.cloned.1.call-done
  244.0 5.0 while.51
  244.0 4.9 conditional.9
  246.9 2.0 select_reduce_fusion
  249.0 35.9 all-gather.14.cloned.1.call-done
  286.0 6.6 while.52
  286.0 6.6 conditional.10
  287.7 4.9 fusion.18
  294.5 81.1 %all-gather.22.cloned.1.call-done = bf16[1024,2048]{1,0:T(8,128)(2,1)} async-done(((bf16[1024,128]{1,0:T(8,128)(2,1)}), bf16[1024,2048]{1,0:T(8,128)(2,1)}) %all-gather.22.cloned.1.call-update) | async-done | bytes 4194320 | tf_op jit(solution)/shard_map/all_gather | solution.py:123
  375.6 4.4 convolution_convert_fusion.1
  382.2 38.0 all-gather.1
  420.2 1.7 multiply_reduce_fusion
  422.0 1.5 multiply_convert_fusion.3
  423.4 170.6 %all-gather.24.cloned.1.call-done = bf16[2048,4096]{1,0:T(8,128)(2,1)} async-done(((bf16[128,4096]{1,0:T(8,128)(2,1)}), bf16[2048,4096]{1,0:T(8,128)(2,1)}) %all-gather.24.cloned.1.call-update) | async-done | bytes 16777232 | tf_op jit(solution)/shard_map/all_gather | solution.py:207
  594.1 12.6 fusion.103
  606.7 180.4 %all-gather.26.cloned.1.call-done = bf16[2048,4096]{1,0:T(8,128)(2,1)} async-done(((bf16[128,4096]{1,0:T(8,128)(2,1)}), bf16[2048,4096]{1,0:T(8,128)(2,1)}) %all-gather.26.cloned.1.call-update) | async-done | bytes 16777232 | tf_op jit(solution)/shard_map/all_gather | solution.py:208
  787.1 12.6 fusion.104
  799.6 238.2 %all-gather.28.cloned.1.call-done = bf16[4096,2048]{1,0:T(8,128)(2,1)} async-done(((bf16[4096,128]{1,0:T(8,128)(2,1)}), bf16[4096,2048]{1,0:T(8,128)(2,1)}) %all-gather.28.cloned.1.call-update) | async-done | bytes 16777232 | tf_op jit(solution)/shard_map/all_gather | solution.py:209
  1037.8 13.8 multiply_convert_fusion
  1051.6 12.3 fusion.105
  1063.9 12.5 fusion.45
  1076.6 17.7 all-reduce.10.cloned.1.call-done
  1094.4 2.7 fusion.59
  1101.8 3.0 fusion.75
  1107.1 12.2 while.53
  1107.1 12.2 conditional.11
  1109.9 2.8 fusion.24
  1113.9 1.4 fusion.41
  1116.3 2.0 fusion.34
  1119.3 2.5 copy.148
  1123.9 11.9 convolution_convert_fusion
  1140.7 2.7 fusion.76
  1143.4 56.6 %reduce-scatter.28.cloned.1.call-done = bf16[128,512]{1,0:T(8,128)(2,1)} async-done(((bf16[1024,512]{1,0:T(8,128)(2,1)}), bf16[128,512]{1,0:T(8,128)(2,1)}) %reduce-scatter.28.cloned.1.call-update) | async-done | bytes 131088
  1202.4 2.1 convolution_add_fusion.1
  1204.5 61.7 %reduce-scatter.12.cloned.1.call-done = bf16[2,128,256]{2,1,0:T(8,128)(2,1)} async-done(((bf16[2,1024,256]{2,1,0:T(8,128)(2,1)}), bf16[2,128,256]{2,1,0:T(8,128)(2,1)}) %reduce-scatter.12.cloned.1.call-update) | async-done | bytes 131088 | tf_op jit(solution)/shard_map/reduce_scatter | solution.py:311
  1266.2 2.8 fusion.46
  1270.2 1.8 fusion.92
  1272.1 1.8 convolution_bitcast_fusion.1
  1274.8 4.6 fusion.78
  1279.5 1.5 copy-done.8
  1281.1 4.6 fusion.81
  1287.9 13.3 fusion.106
  1301.2 1.5 copy-done.26
  1302.7 13.3 fusion.107
  1318.0 13.4 fusion.108
  1333.3 2.0 fusion.61
  1335.3 74.8 %all-reduce.2 = (f32[2048]{0:T(1024)S(1)}, f32[2048]{0:T(1024)S(1)}) all-reduce(f32[2048]{0:T(1024)S(1)} %get-tuple-element.876, f32[2048]{0:T(1024)S(1)} %copy-done.34), channel_id=4, replica_groups=mesh['dp'=2,'seq'=8,'mp'=2] {'dp','seq'}, use_global_device_ids=true, to_apply=%region_29.30.clone | all-reduce | flops 4096 | bytes 32768
  1411.3 4.1 fusion.53
  1415.4 39.3 %reduce-scatter.18.cloned.1.call-done = f32[128,256]{1,0:T(8,128)} async-done(((f32[2048,256]{1,0:T(8,128)}), f32[128,256]{1,0:T(8,128)}) %reduce-scatter.18.cloned.1.call-update) | async-done | bytes 131088 | tf_op jit(solution)/shard_map/reduce_scatter | solution.py:346
  1454.8 177.7 %reduce-scatter.14.cloned.1.call-done = f32[128,1024]{1,0:T(8,128)} async-done(((f32[2048,1024]{1,0:T(8,128)}), f32[128,1024]{1,0:T(8,128)}) %reduce-scatter.14.cloned.1.call-update) | async-done | bytes 524304 | tf_op jit(solution)/shard_map/reduce_scatter | solution.py:344
  1632.5 180.4 %reduce-scatter.20.cloned.1.call-done = f32[1024,128]{1,0:T(8,128)} async-done(((f32[1024,2048]{1,0:T(8,128)}), f32[1024,128]{1,0:T(8,128)}) %reduce-scatter.20.cloned.1.call-update) | async-done | bytes 524304 | tf_op jit(solution)/shard_map/reduce_scatter | solution.py:347
  1812.9 686.2 %reduce-scatter.22.cloned.1.call-done = f32[128,4096]{1,0:T(8,128)} async-done(((f32[2048,4096]{1,0:T(8,128)}), f32[128,4096]{1,0:T(8,128)}) %reduce-scatter.22.cloned.1.call-update) | async-done | bytes 2097168 | tf_op jit(solution)/shard_map/reduce_scatter | solution.py:243
  2499.1 686.4 %reduce-scatter.24.cloned.1.call-done = f32[128,4096]{1,0:T(8,128)} async-done(((f32[2048,4096]{1,0:T(8,128)}), f32[128,4096]{1,0:T(8,128)}) %reduce-scatter.24.cloned.1.call-update) | async-done | bytes 2097168 | tf_op jit(solution)/shard_map/reduce_scatter | solution.py:244
  3185.5 686.5 %reduce-scatter.26.cloned.1.call-done = f32[4096,128]{1,0:T(8,128)} async-done(((f32[4096,2048]{1,0:T(8,128)}), f32[4096,128]{1,0:T(8,128)}) %reduce-scatter.26.cloned.1.call-update) | async-done | bytes 2097168 | tf_op jit(solution)/shard_map/reduce_scatter | solution.py:245
  (228 shorter events, 48.6 us)
Async XLA Ops:
  7.2 48.7 %copy-start = (bf16[2,128,2048]{2,1,0:T(8,128)(2,1)S(1)}, bf16[2,128,2048]{2,1,0:T(8,128)(2,1)}, u32[]{:S(2)}) copy-start(bf16[2,128,2048]{2,1,0:T(8,128)(2,1)} %param.24) | copy-start | bytes 3145732
  7.2 61.8 %all-gather.16.cloned.1.call-start = ((), (), s32[]{:S(2)}) async-start(), calls=%async_computation.11 | async-start | bytes 1114112 | tf_op jit(solution)/shard_map/all_gather | solution.py:121
  7.9 118.0 %all-gather.12.cloned.1.call-start = ((), (), s32[]{:S(2)}) async-start(), calls=%async_computation.9 | async-start | bytes 1114112 | tf_op jit(solution)/shard_map/all_gather | solution.py:122
  8.7 194.7 %all-gather.20.cloned.1.call-start = ((), (), s32[]{:S(2)}) async-start(), calls=%async_computation.13 | async-start | bytes 4456448 | tf_op jit(solution)/shard_map/all_gather | solution.py:120
  9.4 234.6 %all-gather.18.cloned.1.call-start = ((), (), s32[]{:S(2)}) async-start(), calls=%async_computation.12 | async-start | bytes 1179648 | tf_op jit(solution)/shard_map/all_gather | solution.py:141
  53.4 20.3 copy-start.32
  54.2 159.3 %copy-start.22 = (f32[2,128,64]{1,2,0:T(8,128)}, f32[2,128,64]{1,2,0:T(8,128)S(1)}, u32[]{:S(2)}) copy-start(f32[2,128,64]{1,2,0:T(8,128)S(1)} %get-tuple-element.971) | copy-start | bytes 196612
  54.2 159.3 %copy-start.29 = (f32[2,128,64]{1,2,0:T(8,128)}, f32[2,128,64]{1,2,0:T(8,128)S(1)}, u32[]{:S(2)}) copy-start(f32[2,128,64]{1,2,0:T(8,128)S(1)} %get-tuple-element.972) | copy-start | bytes 196612
  55.9 15.4 copy-start.37
  55.9 17.8 copy-start.35
  56.2 153.6 %copy-start.5 = (bf16[2,128,2048]{2,1,0:T(8,128)(2,1)}, bf16[2,128,2048]{2,1,0:T(8,128)(2,1)S(1)}, u32[]{:S(2)}) copy-start(bf16[2,128,2048]{2,1,0:T(8,128)(2,1)S(1)} %fusion.64) | copy-start | bytes 3145732
  73.7 211.2 %all-gather.14.cloned.1.call-start = ((), (), s32[]{:S(2)}) async-start(), calls=%async_computation.10 | async-start | bytes 1179648 | tf_op jit(solution)/shard_map/all_gather | solution.py:142
  128.4 247.2 %all-gather.22.cloned.1.call-start = ((), (), s32[]{:S(2)}) async-start(), calls=%async_computation.14 | async-start | bytes 4456448 | tf_op jit(solution)/shard_map/all_gather | solution.py:123
  129.0 291.2 %all-reduce.8.cloned.1.call-start = ((), (), s32[]{:S(2)}) async-start(), calls=%async_computation.15 | async-start | bytes 2097152 | tf_op jit(solution)/shard_map/psum | solution.py:200
  294.5 85.5 %copy-start.24 = (bf16[2,128,4,4,64]{1,0,4,3,2:T(2,128)(2,1)}, bf16[2,128,4,4,64]{1,0,4,3,2:T(2,128)(2,1)S(1)}, u32[]{:S(2)}) copy-start(bf16[2,128,4,4,64]{1,0,4,3,2:T(2,128)(2,1)S(1)} %copy.115) | copy-start | bytes 1572868
  380.0 2.1 copy-start.39
  380.1 214.0 %all-gather.24.cloned.1.call-start = ((), (), s32[]{:S(2)}) async-start(), calls=%async_computation.16 | async-start | bytes 17825792 | tf_op jit(solution)/shard_map/all_gather | solution.py:207
  380.8 406.3 %all-gather.26.cloned.1.call-start = ((), (), s32[]{:S(2)}) async-start(), calls=%async_computation.17 | async-start | bytes 17825792 | tf_op jit(solution)/shard_map/all_gather | solution.py:208
  381.5 656.3 %all-gather.28.cloned.1.call-start = ((), (), s32[]{:S(2)}) async-start(), calls=%async_computation.18 | async-start | bytes 17825792 | tf_op jit(solution)/shard_map/all_gather | solution.py:209
  382.1 712.2 %all-reduce.10.cloned.1.call-start = ((), (), s32[]{:S(2)}) async-start(), calls=%async_computation.19 | async-start | bytes 2097152 | tf_op jit(solution)/shard_map/psum | solution.py:235
  420.2 1.8 copy-start.3
  1076.4 123.6 %reduce-scatter.28.cloned.1.call-start = ((), (), s32[]{:S(2)}) async-start(), calls=%async_computation.28 | async-start | bytes 1179648
  1094.4 2.7 copy-start.11
  1094.4 2.7 copy-start.13
  1097.1 2.9 copy-start.40
  1098.0 1.3 copy-start.7
  1101.8 5.3 copy-start.2
  1112.7 1.2 copy-start.14
  1113.9 2.4 copy-start.16
  1115.3 1.0 copy-start.15
  1118.3 1.0 copy-start.17
  1121.8 1.5 copy-start.23
  1123.0 143.2 %reduce-scatter.12.cloned.1.call-start = ((), (), s32[]{:S(2)}) async-start(), calls=%async_computation.20 | async-start | bytes 1179648 | tf_op jit(solution)/shard_map/reduce_scatter | solution.py:311
  1123.9 12.0 copy-start.18
  1135.9 1.3 copy-start.30
  1137.5 195.8 %all-reduce.12.cloned.1.call-start = ((), (), s32[]{:S(2)}) async-start(), calls=%async_computation.29 | async-start | bytes 4194304 | tf_op jit(solution)/shard_map/psum | solution.py:217
  1138.5 2.2 copy-start.9
  1201.2 1.2 copy-start.19
  1269.0 1.2 copy-start.6
  1269.0 146.4 %reduce-scatter.16.cloned.1.call-start = ((), (), s32[]{:S(2)}) async-start(), calls=%async_computation.22 | async-start | bytes 2228224 | tf_op jit(solution)/shard_map/reduce_scatter | solution.py:345
  1270.2 1.9 copy-start.31
  1272.1 2.2 copy-start.28
  1272.1 182.7 %reduce-scatter.18.cloned.1.call-start = ((), (), s32[]{:S(2)}) async-start(), calls=%async_computation.23 | async-start | bytes 2228224 | tf_op jit(solution)/shard_map/reduce_scatter | solution.py:346
  1274.0 358.5 %reduce-scatter.14.cloned.1.call-start = ((), (), s32[]{:S(2)}) async-start(), calls=%async_computation.21 | async-start | bytes 8912896 | tf_op jit(solution)/shard_map/reduce_scatter | solution.py:344
  1279.4 1.6 copy-start.8
  1279.4 1.7 copy-start.25
  1279.5 533.4 %reduce-scatter.20.cloned.1.call-start = ((), (), s32[]{:S(2)}) async-start(), calls=%async_computation.24 | async-start | bytes 8912896 | tf_op jit(solution)/shard_map/reduce_scatter | solution.py:347
  1285.7 1.3 copy-start.10
  1285.7 2.2 copy-start.27
  1285.7 1213.4 %reduce-scatter.22.cloned.1.call-start = ((), (), s32[]{:S(2)}) async-start(), calls=%async_computation.25 | async-start | bytes 35651584 | tf_op jit(solution)/shard_map/reduce_scatter | solution.py:243
  1301.1 1.6 copy-start.26
  1301.2 1884.3 %reduce-scatter.24.cloned.1.call-start = ((), (), s32[]{:S(2)}) async-start(), calls=%async_computation.26 | async-start | bytes 35651584 | tf_op jit(solution)/shard_map/reduce_scatter | solution.py:244
  1316.0 1.2 copy-start.12
  1316.0 1.9 copy-start.21
  1316.1 2555.9 %reduce-scatter.26.cloned.1.call-start = ((), (), s32[]{:S(2)}) async-start(), calls=%async_computation.27 | async-start | bytes 35651584 | tf_op jit(solution)/shard_map/reduce_scatter | solution.py:245
  1331.4 0.7 copy-start.41
  1331.4 1.9 copy-start.38
  1331.4 2.0 copy-start.1
  1331.4 2.0 copy-start.33
  1331.4 2.0 copy-start.36
  1331.4 3.9 copy-start.34
  1331.4 79.9 %copy-start.4 = (bf16[256,2048]{1,0:T(8,128)(2,1)S(1)}, bf16[256,2048]{1,0:T(8,128)(2,1)}, u32[]{:S(2)}) copy-start(bf16[256,2048]{1,0:T(8,128)(2,1)} %all-reduce.8.cloned.1.call-done) | copy-start | bytes 3145732
  1333.3 78.0 %copy-start.20 = (bf16[256,2048]{1,0:T(8,128)(2,1)S(1)}, bf16[256,2048]{1,0:T(8,128)(2,1)}, u32[]{:S(2)}) copy-start(bf16[256,2048]{1,0:T(8,128)(2,1)} %get-tuple-element.947) | copy-start | bytes 3145732
Sparse Core Ops, SparseCore 0:
  10.8 58.1 all-gather.15
  71.8 54.1 all-gather.11
  128.8 74.5 all-gather.19
  205.8 38.1 all-gather.17
  246.5 38.4 all-gather.13
  287.5 88.0 all-gather.21
  380.2 17.7 all-reduce.7
  401.2 192.8 all-gather.23
  597.2 189.7 all-gather.25
  790.0 247.7 all-gather.27
  1076.5 17.7 all-reduce.9
  1123.2 76.8 reduce-scatter.27
  1203.8 62.3 reduce-scatter.11
  1269.1 20.2 all-reduce.11
  1292.3 82.2 reduce-scatter.15
  1377.3 77.4 reduce-scatter.17
  1457.6 174.8 reduce-scatter.13
  1635.3 177.5 reduce-scatter.19
  1816.0 683.1 reduce-scatter.21
  2502.0 683.4 reduce-scatter.23
  3188.5 683.4 reduce-scatter.25
where the time goes:
time: 3880 us
  waiting for transfers between devices  3470 us (89%)
  matrix products  163 us (4%)
  blocking collectives  155 us (4%)
  local copies, waits for them, and re-layouts  43.1 us (1%)
    reduce_scatter x1, waiting for transfers between devices, shards(): lax.psum_scatter(down_grad, ('dp', 'seq'), scatter_dimension=1, tiled=True)  687 us
    reduce_scatter x1, waiting for transfers between devices, shards(): lax.psum_scatter(up_grad, ('dp', 'seq'), scatter_dimension=0, tiled=True)  686 us
    reduce_scatter x1, waiting for transfers between devices, shards(): lax.psum_scatter(gate_grad, ('dp', 'seq'), scatter_dimension=0, tiled=True)  686 us
    all_gather x1, waiting for transfers between devices, shards(): lax.all_gather(down_weight, ('dp', 'seq'), axis=1, tiled=True)  238 us
    reduce_scatter x1, waiting for transfers between devices, shards(): lax.psum_scatter(output_grad, ('dp', 'seq'), scatter_dimension=1, tiled=T...  180 us
    all_gather x1, waiting for transfers between devices, shards(): lax.all_gather(up_weight, ('dp', 'seq'), axis=0, tiled=True)  180 us
    reduce_scatter x1, waiting for transfers between devices, shards(): lax.psum_scatter(query_grad, ('dp', 'seq'), scatter_dimension=0, tiled=True)  178 us
    all_gather x1, waiting for transfers between devices, shards(): lax.all_gather(gate_weight, ('dp', 'seq'), axis=0, tiled=True)  171 us
  transfers between devices with their start and end apart: 21, of which 18 were waited for; matrix products, arithmetic and copies ran while one was open for 4% of the time, Pallas kernels for 0%

commit v1 on v0

v1 whole, which is shorter than its diff:
```python
import functools
import math

import jax
import jax.numpy as jnp
from jax import lax
from jax.experimental import pallas as pl
from jax.experimental.pallas import tpu as pltpu
from jax.sharding import PartitionSpec as P

H = 32
KVH = 8
HD = 64
SQUARE = 4

EPSILON = 1e-05
MASKED = -1e30
ROPE_THETA = 500000.0
ROPE_FACTOR = 32.0
LOW_FACTOR = 1.0
HIGH_FACTOR = 4.0
PRIOR_CONTEXT = 8192.0
VMEM = 56 * 1024 * 1024


def inverse_freqs(head_dim):
    ladder = jnp.arange(head_dim // 2, dtype=jnp.float32)
    base = ROPE_THETA ** (-2.0 * ladder / head_dim)
    wavelen = 2.0 * math.pi / base
    smooth = (PRIOR_CONTEXT / wavelen - LOW_FACTOR) / (HIGH_FACTOR - LOW_FACTOR)
    blended = (1.0 - smooth) * base / ROPE_FACTOR + smooth * base
    low_limit = PRIOR_CONTEXT / LOW_FACTOR
    high_limit = PRIOR_CONTEXT / HIGH_FACTOR
    return jnp.where(
        wavelen < high_limit, base, jnp.where(wavelen > low_limit, base / ROPE_FACTOR, blended)
    )


def rope_tables(position, head_dim):
    angles = position[..., None] * inverse_freqs(head_dim)
    angles = jnp.concatenate([angles, angles], axis=-1)
    return (jnp.cos(angles)[..., None, :], jnp.sin(angles)[..., None, :])


def rotate(values, cosine, sine):
    middle = values.shape[-1] // 2
    turned = jnp.concatenate([-values[..., middle:], values[..., :middle]], axis=-1)
    return values * cosine + turned * sine


def unrotate(grads, cosine, sine):
    middle = grads.shape[-1] // 2
    scaled = grads * sine
    turned = jnp.concatenate([scaled[..., middle:], -scaled[..., :middle]], axis=-1)
    return grads * cosine + turned


def dot(left, right, dims=((1,), (0,))):
    return lax.dot_general(left, right, (dims, ((), ())), preferred_element_type=jnp.float32)


def swap(value, axis, mask):
    size = lax.axis_size(axis)
    return lax.ppermute(value, axis, [(i, i ^ mask) for i in range(size)])


def cut(value, start, length, axis):
    return lax.dynamic_slice_in_dim(value, start, length, axis)


def put(whole, part, start, axis):
    return lax.dynamic_update_slice_in_dim(whole, part, start, axis)


def mask_of(info, row, row_count, local, keys):
    span = SQUARE * local
    low, high = info[0], info[1]

    def place_of(index):
        block = (index // local) % SQUARE
        part = index // span
        return (high ^ part) * span + (low ^ block) * local + index % local

    def segment_of(place):
        total = jnp.zeros_like(place)
        for doc in range(4):
            total = total + (place >= info[2 + row * 4 + doc]).astype(jnp.int32)
        return total

    query = place_of(lax.broadcasted_iota(jnp.int32, (span, 1), 0))
    key = place_of(lax.broadcasted_iota(jnp.int32, (1, keys), 1))
    return (segment_of(query) == segment_of(key)) & (query >= key)


def attend_kernel(local, keys, group, info, q_ref, kv_ref, out_ref, lse_ref):
    row = pl.program_id(0)
    span = SQUARE * local
    allowed = mask_of(info, row, None, local, keys)
    kv = kv_ref[...].reshape(keys, 2 * HD)
    k, v = kv[:, :HD], kv[:, HD:]
    q_all = q_ref[...].reshape(span, group * HD)
    outs, sums = [], []
    for head in range(group):
        q = q_all[:, head * HD : (head + 1) * HD]
        score = dot(q, k, ((1,), (1,))) * HD ** (-0.5)
        score = jnp.where(allowed, score, MASKED)
        top = jnp.max(score, axis=1, keepdims=True)
        grown = jnp.exp(score - top)
        total = jnp.sum(grown, axis=1, keepdims=True)
        lse = top + jnp.log(total)
        probs = (grown * (1.0 / total)).astype(jnp.bfloat16)
        outs.append(dot(probs, v))
        sums.append(lse)
    out_ref[...] = jnp.concatenate(outs, axis=1).reshape(out_ref.shape)
    lse_ref[...] = jnp.concatenate(sums, axis=1).reshape(lse_ref.shape)


def attend(info, queries, kv):
    blocks, rows, local, width = queries.shape
    parts = kv.shape[0]
    keys = parts * blocks * local
    group = width // HD
    return pl.pallas_call(
        functools.partial(attend_kernel, local, keys, group),
        grid=(rows,),
        out_shape=(
            jax.ShapeDtypeStruct((blocks, rows, local, width), jnp.float32),
            jax.ShapeDtypeStruct((blocks, rows, local, group), jnp.float32),
        ),
        in_specs=[
            pl.BlockSpec(memory_space=pltpu.SMEM),
            pl.BlockSpec((blocks, 1, local, width), lambda r: (0, r, 0, 0)),
            pl.BlockSpec((parts, blocks, 1, local, 2 * HD), lambda r: (0, 0, r, 0, 0)),
        ],
        out_specs=(
            pl.BlockSpec((blocks, 1, local, width), lambda r: (0, r, 0, 0)),
            pl.BlockSpec((blocks, 1, local, group), lambda r: (0, r, 0, 0)),
        ),
        compiler_params=pltpu.CompilerParams(vmem_limit_bytes=VMEM),
        cost_estimate=pl.CostEstimate(
            flops=8 * rows * blocks * local * keys * width,
            bytes_accessed=rows * blocks * local * width * 8,
            transcendentals=rows * blocks * local * keys * group,
        ),
        name="attend",
    )(info, queries, kv)


def attend_back_kernel(
    local, keys, group, info, q_ref, kv_ref, go_ref, out_ref, lse_ref, dq_ref, dkv_ref
):
    row = pl.program_id(0)
    span = SQUARE * local
    allowed = mask_of(info, row, None, local, keys)
    kv = kv_ref[...].reshape(keys, 2 * HD)
    k, v = kv[:, :HD], kv[:, HD:]
    q_all = q_ref[...].reshape(span, group * HD)
    go_all = go_ref[...].reshape(span, group * HD)
    out_all = out_ref[...].reshape(span, group * HD)
    lse_all = lse_ref[...].reshape(span, group)
    dq = []
    dk = jnp.zeros((keys, HD), jnp.float32)
    dv = jnp.zeros((keys, HD), jnp.float32)
    scale = HD ** (-0.5)
    for head in range(group):
        q = q_all[:, head * HD : (head + 1) * HD]
        go = go_all[:, head * HD : (head + 1) * HD]
        out = out_all[:, head * HD : (head + 1) * HD]
        delta = jnp.sum(go.astype(jnp.float32) * out, axis=1, keepdims=True)
        score = dot(q, k, ((1,), (1,))) * scale
        probs = jnp.exp(jnp.where(allowed, score, MASKED) - lse_all[:, head : head + 1])
        dv = dv + dot(probs.astype(jnp.bfloat16), go, ((0,), (0,)))
        prob_grad = dot(go, v, ((1,), (1,)))
        score_grad = (probs * (prob_grad - delta)).astype(jnp.bfloat16)
        dq.append(dot(score_grad, k) * scale)
        dk = dk + dot(score_grad, q, ((0,), (0,)))
    dq_ref[...] = jnp.concatenate(dq, axis=1).reshape(dq_ref.shape)
    dkv_ref[...] = jnp.concatenate([dk * scale, dv], axis=1).reshape(dkv_ref.shape)


def attend_back(info, queries, kv, out_grads, out, lse):
    blocks, rows, local, width = queries.shape
    parts = kv.shape[0]
    keys = parts * blocks * local
    group = width // HD
    wide = pl.BlockSpec((blocks, 1, local, width), lambda r: (0, r, 0, 0))
    kv_spec = pl.BlockSpec((parts, blocks, 1, local, 2 * HD), lambda r: (0, 0, r, 0, 0))
    return pl.pallas_call(
        functools.partial(attend_back_kernel, local, keys, group),
        grid=(rows,),
        out_shape=(
            jax.ShapeDtypeStruct(queries.shape, jnp.float32),
            jax.ShapeDtypeStruct(kv.shape, jnp.float32),
        ),
        in_specs=[
            pl.BlockSpec(memory_space=pltpu.SMEM),
            wide,
            kv_spec,
            wide,
            wide,
            pl.BlockSpec((blocks, 1, local, group), lambda r: (0, r, 0, 0)),
        ],
        out_specs=(wide, kv_spec),
        compiler_params=pltpu.CompilerParams(vmem_limit_bytes=VMEM),
        cost_estimate=pl.CostEstimate(
            flops=20 * rows * blocks * local * keys * width,
            bytes_accessed=rows * blocks * local * width * 16,
            transcendentals=rows * blocks * local * keys * group,
        ),
        name="attend_back",
    )(info, queries, kv, out_grads, out, lse)


def bits_of(size):
    return [1 << b for b in range(size.bit_length() - 1)]


def spread_weight(shard, axis, place):
    dp, high, low, dp_size, high_size = place
    other = 1 - axis
    block = shard.shape[axis]
    width = shard.shape[other] // SQUARE
    pieces = [cut(shard, low * width, width, other)]
    for mask in range(1, SQUARE):
        pieces.append(swap(cut(shard, (low ^ mask) * width, width, other), "seq", mask))
    shape = [0, 0]
    shape[axis], shape[other] = SQUARE * block, width
    square = jnp.zeros(shape, shard.dtype)
    for mask in range(SQUARE):
        square = put(square, pieces[mask], (low ^ mask) * block, axis)
    parts = {(0, 0): square}
    for bit in bits_of(high_size):
        for (a, b) in list(parts):
            parts[a, b ^ bit] = swap(parts[a, b], "seq", SQUARE * bit)
    for bit in bits_of(dp_size):
        for (a, b) in list(parts):
            parts[a ^ bit, b] = swap(parts[a, b], "dp", bit)
    shape[axis] = SQUARE * block * high_size * dp_size
    whole = jnp.zeros(shape, shard.dtype)
    for (a, b), part in parts.items():
        index = (dp ^ a) * high_size + (high ^ b)
        whole = put(whole, part, index * SQUARE * block, axis)
    return whole


def settle_grad(grad, axis, place):
    dp, high, low, dp_size, high_size = place
    other = 1 - axis
    width = grad.shape[other]
    kept = grad
    for index, size, name, unit in ((dp, dp_size, "dp", 1), (high, high_size, "seq", SQUARE)):
        for bit in reversed(bits_of(size)):
            half = kept.shape[axis] // 2
            mine = (index // bit) % 2
            sent = cut(kept, (1 - mine) * half, half, axis).astype(jnp.bfloat16)
            kept = cut(kept, mine * half, half, axis) + swap(sent, name, unit * bit).astype(
                jnp.float32
            )
    block = kept.shape[axis] // SQUARE
    shape = [0, 0]
    shape[axis], shape[other] = block, SQUARE * width
    whole = jnp.zeros(shape, jnp.float32)
    whole = put(whole, cut(kept, low * block, block, axis), low * width, other)
    for mask in range(1, SQUARE):
        sent = cut(kept, (low ^ mask) * block, block, axis).astype(jnp.bfloat16)
        got = swap(sent, "seq", mask).astype(jnp.float32)
        whole = put(whole, got, (low ^ mask) * width, other)
    return whole


def gather_square(own, core):
    tokens, width = own.shape
    half = width // 2
    mine = cut(own, core * half, half, 1)
    got = jnp.concatenate([swap(mine, "seq", mask) for mask in range(1, SQUARE)], axis=0)
    across = swap(got, "mp", 1)
    first = jnp.where(core == 0, got, across)
    second = jnp.where(core == 0, across, got)
    return jnp.concatenate([own, jnp.concatenate([first, second], axis=1)], axis=0)


def scatter_square(partial, core):
    tokens, width = partial.shape[0] // SQUARE, partial.shape[1]
    half = width // 2
    kept = cut(partial, core * half, half, 1)
    sent = cut(partial, (1 - core) * half, half, 1).astype(jnp.bfloat16)
    kept = kept + swap(sent, "mp", 1).astype(jnp.float32)
    total = kept[:tokens]
    for mask in range(1, SQUARE):
        part = kept[mask * tokens : (mask + 1) * tokens].astype(jnp.bfloat16)
        total = total + swap(part, "seq", mask).astype(jnp.float32)
    mine = total.astype(jnp.bfloat16)
    across = swap(mine, "mp", 1)
    return jnp.concatenate(
        [jnp.where(core == 0, mine, across), jnp.where(core == 0, across, mine)], axis=1
    ).astype(jnp.float32)


def norm_back(values, scale, gain, grad):
    weighted = grad * gain
    gain_grad = jnp.sum(grad * values * scale, axis=0)
    inner = jnp.mean(weighted * values, axis=-1, keepdims=True)
    return (weighted * scale - values * scale**3 * inner, gain_grad)


def shards(
    hidden_in,
    doc_lengths,
    attn_gain,
    query_weight,
    key_weight,
    value_weight,
    output_weight,
    ffn_gain,
    gate_weight,
    up_weight,
    down_weight,
    out_grad,
):
    rows, local, model = hidden_in.shape
    tokens = rows * local
    seq = lax.axis_index("seq")
    core = lax.axis_index("mp")
    low, high = seq % SQUARE, seq // SQUARE
    high_size = lax.axis_size("seq") // SQUARE
    place = (lax.axis_index("dp"), high, low, lax.axis_size("dp"), high_size)
    group = H // KVH
    span = SQUARE * local

    ends = jnp.cumsum(doc_lengths, axis=-1)
    info = jnp.concatenate([jnp.stack([low, high]), ends.reshape(-1)]).astype(jnp.int32)

    gains = lax.all_gather(jnp.stack([attn_gain, ffn_gain]), ("dp", "seq"), axis=1, tiled=True)
    gain_one, gain_two = gains[0].astype(jnp.float32), gains[1].astype(jnp.float32)

    own_in = hidden_in.reshape(tokens, model)
    all_in = gather_square(own_in, core).astype(jnp.float32)
    query_own = spread_weight(query_weight, 0, place)
    key_own = spread_weight(key_weight, 0, place)
    value_own = spread_weight(value_weight, 0, place)
    output_own = spread_weight(output_weight, 1, place)
    gate_own = spread_weight(gate_weight, 0, place)
    up_own = spread_weight(up_weight, 0, place)
    down_own = spread_weight(down_weight, 1, place)
    all_grad = gather_square(out_grad.reshape(tokens, model), core)

    blocks = low ^ jnp.arange(SQUARE, dtype=jnp.int32)
    spots = (high * span + blocks[:, None] * local + jnp.arange(local, dtype=jnp.int32)[None, :])
    reached = spots[:, None, :, None] >= ends[None, :, None, :]
    begin = jnp.max(jnp.where(reached, ends[None, :, None, :], 0), axis=-1)
    position = (spots[:, None, :] - begin).astype(jnp.float32)
    cosine, sine = rope_tables(position, HD)

    scale_one = lax.rsqrt(jnp.mean(all_in * all_in, axis=-1, keepdims=True) + EPSILON)
    normed_one = (all_in * scale_one * gain_one).astype(jnp.bfloat16)
    query_pre = dot(normed_one, query_own).reshape(SQUARE, rows, local, group, HD)
    key_pre = dot(normed_one, key_own).reshape(SQUARE, rows, local, 1, HD)
    value_pre = dot(normed_one, value_own).reshape(SQUARE, rows, local, HD)
    queries = rotate(query_pre, cosine, sine).astype(jnp.bfloat16)
    queries = queries.reshape(SQUARE, rows, local, group * HD)
    keys = rotate(key_pre, cosine, sine).astype(jnp.bfloat16).reshape(value_pre.shape)
    kv = jnp.concatenate([keys, value_pre.astype(jnp.bfloat16)], axis=-1)[None]
    for bit in bits_of(high_size):
        kv = jnp.concatenate([kv, swap(kv, "seq", SQUARE * bit)], axis=0)
    attn, lse = attend(info, queries, kv)
    attn_low = attn.reshape(SQUARE * tokens, group * HD).astype(jnp.bfloat16)
    residual = own_in.astype(jnp.float32) + scatter_square(dot(attn_low, output_own), core)

    scale_two = lax.rsqrt(jnp.mean(residual * residual, axis=-1, keepdims=True) + EPSILON)
    normed_two = (residual * scale_two * gain_two).astype(jnp.bfloat16)
    normed_two = gather_square(normed_two, core)
    gate_proj = dot(normed_two, gate_own)
    up_proj = dot(normed_two, up_own)
    sigmoid_gate = jax.nn.sigmoid(gate_proj)
    silu_gate = gate_proj * sigmoid_gate
    hidden_units = (silu_gate * up_proj).astype(jnp.bfloat16)
    hidden_grad = dot(all_grad, down_own, ((1,), (1,)))
    gate_act = (
        hidden_grad * up_proj * sigmoid_gate * (1.0 + gate_proj * (1.0 - sigmoid_gate))
    ).astype(jnp.bfloat16)
    up_act = (hidden_grad * silu_gate).astype(jnp.bfloat16)
    down_grad = settle_grad(dot(hidden_units, all_grad, ((0,), (0,))), 1, place)
    normed_two_grad = scatter_square(
        dot(gate_act, gate_own, ((1,), (1,))) + dot(up_act, up_own, ((1,), (1,))), core
    )
    layer_out = residual + scatter_square(dot(hidden_units, down_own), core)
    layer_out = layer_out.astype(jnp.bfloat16).reshape(hidden_in.shape)
    gate_grad = settle_grad(dot(normed_two, gate_act, ((0,), (0,))), 0, place)
    up_grad = settle_grad(dot(normed_two, up_act, ((0,), (0,))), 0, place)

    residual_part, ffn_gain_grad = norm_back(residual, scale_two, gain_two, normed_two_grad)
    residual_grad = out_grad.reshape(tokens, model).astype(jnp.float32) + residual_part
    residual_low = gather_square(residual_grad.astype(jnp.bfloat16), core)
    output_grad = settle_grad(dot(attn_low, residual_low, ((0,), (0,))), 1, place)
    attn_grad = dot(residual_low, output_own, ((1,), (1,))).astype(jnp.bfloat16)
    attn_grad = attn_grad.reshape(queries.shape)
    query_acc, kv_acc = attend_back(info, queries, kv, attn_grad, attn, lse)
    for bit in reversed(bits_of(high_size)):
        sent = kv_acc[bit:].astype(jnp.bfloat16)
        kv_acc = kv_acc[:bit] + swap(sent, "seq", SQUARE * bit).astype(jnp.float32)
    kv_acc = kv_acc[0]
    query_back = unrotate(query_acc.reshape(query_pre.shape), cosine, sine).astype(jnp.bfloat16)
    key_back = unrotate(kv_acc[..., :HD].reshape(key_pre.shape), cosine, sine)
    key_back = key_back.astype(jnp.bfloat16).reshape(SQUARE * tokens, HD)
    value_back = kv_acc[..., HD:].astype(jnp.bfloat16).reshape(SQUARE * tokens, HD)
    query_back = query_back.reshape(SQUARE * tokens, group * HD)
    normed_one_grad = scatter_square(
        dot(query_back, query_own, ((1,), (1,)))
        + dot(key_back, key_own, ((1,), (1,)))
        + dot(value_back, value_own, ((1,), (1,))),
        core,
    )
    query_grad = settle_grad(dot(normed_one, query_back, ((0,), (0,))), 0, place)
    key_grad = settle_grad(dot(normed_one, key_back, ((0,), (0,))), 0, place)
    value_grad = settle_grad(dot(normed_one, value_back, ((0,), (0,))), 0, place)
    own_32 = own_in.astype(jnp.float32)
    own_scale = lax.rsqrt(jnp.mean(own_32 * own_32, axis=-1, keepdims=True) + EPSILON)
    input_part, attn_gain_grad = norm_back(own_32, own_scale, gain_one, normed_one_grad)
    input_grad = (residual_grad + input_part).astype(jnp.bfloat16).reshape(hidden_in.shape)
    gain_grads = lax.psum_scatter(
        jnp.stack([attn_gain_grad, ffn_gain_grad]), ("dp", "seq"), scatter_dimension=1, tiled=True
    )
    return (
        layer_out,
        input_grad,
        gain_grads[0],
        query_grad,
        key_grad,
        value_grad,
        output_grad,
        gain_grads[1],
        gate_grad,
        up_grad,
        down_grad,
    )


def solution(mesh):
    return jax.shard_map(
        shards,
        mesh=mesh,
        in_specs=(
            P("dp", "seq", None),
            P("dp", None),
            P(("dp", "seq")),
            P(("dp", "seq"), "mp"),
            P(("dp", "seq"), "mp"),
            P(("dp", "seq"), "mp"),
            P("mp", ("dp", "seq")),
            P(("dp", "seq")),
            P(("dp", "seq"), "mp"),
            P(("dp", "seq"), "mp"),
            P("mp", ("dp", "seq")),
            P("dp", "seq", None),
        ),
        out_specs=(
            P("dp", "seq", None),
            P("dp", "seq", None),
            P(("dp", "seq")),
            P(("dp", "seq"), "mp"),
            P(("dp", "seq"), "mp"),
            P(("dp", "seq"), "mp"),
            P("mp", ("dp", "seq")),
            P(("dp", "seq")),
            P(("dp", "seq"), "mp"),
            P(("dp", "seq"), "mp"),
            P("mp", ("dp", "seq")),
        ),
        check_vma=False,
    )
```

time: 3880 us -> 1150 us (0.30)
  waiting for transfers between devices: 3470 us -> 596 us
  starting transfers between devices: 1.69 us -> 130 us
  blocking collectives: 155 us -> 53 us
  local copies, waits for them, and re-layouts: 43.1 us -> 134 us
  matrix products: 163 us -> 103 us
  other arithmetic: 27.1 us -> 79.3 us
    reduce_scatter x8 -> x0, waiting for transfers between devices: 2520 us -> none  [the longest x1 687 us: shards(): lax.psum_scatter(down_grad, ('dp', 'seq'), scatter_dimension=1, tiled=True)]
    all_gather x9 -> x0, waiting for transfers between devices: 875 us -> none  [the longest x1 238 us: shards(): lax.all_gather(down_weight, ('dp', 'seq'), axis=1, tiled=True)]
    ppermute x0 -> x115, waiting for transfers between devices: none -> 523 us  [swap(): return lax.ppermute(value, axis, [(i, i ^ mask) for i in range(size)])]
    ppermute x0 -> x115, starting transfers between devices: none -> 130 us  [swap(): return lax.ppermute(value, axis, [(i, i ^ mask) for i in range(size)])]
    unnamed x1 -> x0, blocking collectives: 74.8 us -> none
    dot_general x28 -> x21, matrix products: 163 us -> 103 us  [dot(): lax.dot_general(left, right, (dims, ((), ())), preferred_element_type=jnp...]
    all_gather x2 -> x1, blocking collectives: 80.3 us -> 53 us  [shards(): lax.all_gather(jnp.stack([attn_gain, ffn_gain]), ('dp', 'seq'), axis=1, t...]
  transfers between devices with their start and end apart: 21 -> 116, of which waited for: 18 -> 58; matrix products, arithmetic and copies ran while one was open for 4% -> 15% of each run, Pallas kernels for 0% -> 0%
where the time goes in v1:
time: 1150 us; the launch traced here: 1140 us
  waiting for transfers between devices  596 us (52%)
  local copies, waits for them, and re-layouts  134 us (12%)
  starting transfers between devices  130 us (11%)
  matrix products  103 us (9%)
  other arithmetic  79.3 us (7%)
  blocking collectives  53 us (5%)
  Pallas kernels  29.1 us (3%)
  between operations  16.8 us (1%)
    ppermute x115, waiting for transfers between devices, swap(): return lax.ppermute(value, axis, [(i, i ^ mask) for i in range(size)])  523 us
    ppermute x115, starting transfers between devices, swap(): return lax.ppermute(value, axis, [(i, i ^ mask) for i in range(size)])  130 us
    dot_general x21, matrix products, dot(): lax.dot_general(left, right, (dims, ((), ())), preferred_element_type=jnp...  103 us
    unnamed x2, waiting for transfers between devices  72.9 us
    all_gather x1, blocking collectives, shards(): lax.all_gather(jnp.stack([attn_gain, ffn_gain]), ('dp', 'seq'), axis=1, t...  53 us
    dynamic_update_slice x62, local copies, waits for them, and re-layouts, put(): return lax.dynamic_update_slice_in_dim(whole, part, start, axis)  35.4 us
    unnamed x168, local copies, waits for them, and re-layouts  32.9 us
  transfers between devices with their start and end apart: 116, of which 58 were waited for; matrix products, arithmetic and copies ran while one was open for 15% of the time, Pallas kernels for 0%

profile of v1, /device:TPU:0, one launch (start us, length us, event | category | flops | bytes accessed | tf_op | source)
XLA Modules:
  0.0 1141.4 jit_solution(15148229594024123045)
XLA Ops:
  18.0 53.0 %all_gather.3 = bf16[2,2048]{1,0:T(2,128)(2,1)S(1)} all-gather(bf16[2,128]{1,0:T(2,128)(2,1)S(1)} %pad_maximum_fusion.8), channel_id=1, replica_groups=mesh['dp'=2,'seq'=8,'mp'=2] {'dp','seq'}, dimensions={1}, use_global_device_ids=true | all-gather | bytes 8704 | tf_op jit(solution)/shard_map/all_gather | solution.py:333
  73.1 3.9 collective-permute-done.11
  77.0 4.8 collective-permute-done.12
  81.9 3.8 collective-permute-done.16
  90.0 5.0 collective-permute-done.18
  119.2 6.1 collective-permute-done.15
  125.6 4.9 collective-permute-done.21
  132.6 7.5 collective-permute-done.26
  142.2 5.6 collective-permute-done.28
  149.7 4.4 fusion
  154.1 6.0 fusion.2
  185.7 3.7 convolution_convert_fusion
  198.6 11.5 %attend.1 = (f32[4,2,128,256]{3,2,1,0:T(8,128)}, f32[4,2,128,4]{3,2,1,0:T(8,128)}) custom-call(s32[10]{0:T(128)} %pad_add_fusion.info, bf16[4,2,128,256]{3,2,1,0:T(8,128)(2,1)} %add_convert_fusion.3.q_ref, bf16[2,4,2,128,128]{4,3,2,1,0:T(8,128)(2,1)} %pad_maximum_fusion.6.kv_ref), custom_call_target="tpu_custom_call" | custom-call | flops 2147483648 | bytes 2097152 | tf_op jit(solution)/shard_map/attend/pallas_call | solution.py:123
  222.8 8.0 collective-permute-start.51
  246.7 16.6 %collective-permute-done.44 = bf16[128,1024]{1,0:T(8,128)(2,1)S(1)} collective-permute-done((bf16[128,1024]{1,0:T(8,128)(2,1)}, bf16[128,1024]{1,0:T(8,128)(2,1)S(1)}, u32[]{:S(2)}, u32[]{:S(2)}) %collective-permute-start.44) | collective-permute-done | bytes 262176 | tf_op jit(solution)/shard_map/ppermute | solution.py:64
  264.6 3.8 collective-permute-start.39
  271.6 3.7 fusion.63
  288.8 20.7 %collective-permute-done.32 = bf16[256,1024]{1,0:T(8,128)(2,1)S(1)} collective-permute-done((bf16[256,1024]{1,0:T(8,128)(2,1)S(1)}, bf16[256,1024]{1,0:T(8,128)(2,1)S(1)}, u32[]{:S(2)}, u32[]{:S(2)}) %collective-permute-start.32) | collective-permute-done | bytes 524320 | tf_op jit(solution)/shard_map/ppermute | solution.py:64
  314.3 4.0 collective-permute-done.31
  321.4 5.3 collective-permute-start.47
  327.0 25.1 %collective-permute-done.62 = bf16[256,1024]{1,0:T(8,128)(2,1)S(1)} collective-permute-done((bf16[256,1024]{1,0:T(8,128)(2,1)}, bf16[256,1024]{1,0:T(8,128)(2,1)S(1)}, u32[]{:S(2)}, u32[]{:S(2)}) %collective-permute-start.62) | collective-permute-done | bytes 524320 | tf_op jit(solution)/shard_map/ppermute | solution.py:64
  352.1 12.2 %collective-permute-done.63 = bf16[256,1024]{1,0:T(8,128)(2,1)S(1)} collective-permute-done((bf16[256,1024]{1,0:T(8,128)(2,1)}, bf16[256,1024]{1,0:T(8,128)(2,1)S(1)}, u32[]{:S(2)}, u32[]{:S(2)}) %collective-permute-start.63) | collective-permute-done | bytes 524320 | tf_op jit(solution)/shard_map/ppermute | solution.py:64
  372.8 29.5 %collective-permute-done.47 = bf16[512,1024]{1,0:T(8,128)(2,1)} collective-permute-done((bf16[512,1024]{1,0:T(8,128)(2,1)}, bf16[512,1024]{1,0:T(8,128)(2,1)}, u32[]{:S(2)}, u32[]{:S(2)}) %collective-permute-start.47) | collective-permute-done | bytes 1048608 | tf_op jit(solution)/shard_map/ppermute | solution.py:64
  407.0 15.0 %collective-permute-done.41 = bf16[512,1024]{1,0:T(8,128)(2,1)} collective-permute-done((bf16[512,1024]{1,0:T(8,128)(2,1)}, bf16[512,1024]{1,0:T(8,128)(2,1)}, u32[]{:S(2)}, u32[]{:S(2)}) %collective-permute-start.41) | collective-permute-done | bytes 1048608 | tf_op jit(solution)/shard_map/ppermute | solution.py:64
  443.7 5.9 collective-permute-done.36
  451.1 7.1 collective-permute-done.49
  460.4 18.3 %collective-permute-done.43 = bf16[512,1024]{1,0:T(8,128)(2,1)} collective-permute-done((bf16[512,1024]{1,0:T(8,128)(2,1)}, bf16[512,1024]{1,0:T(8,128)(2,1)}, u32[]{:S(2)}, u32[]{:S(2)}) %collective-permute-start.43) | collective-permute-done | bytes 1048608 | tf_op jit(solution)/shard_map/ppermute | solution.py:64
  481.1 4.7 fusion.21
  487.2 6.7 fusion.58
  493.9 12.8 %multiply_convert_fusion.1 = (bf16[1024,1024]{1,0:T(8,128)(2,1)S(1)}, bf16[1024,1024]{1,0:T(8,128)(2,1)S(1)}, bf16[1024,1024]{1,0:T(8,128)(2,1)}) fusion(f32[1024,1024]{1,0:T(8,128)S(1)} %fusion.21, f32[1024,1024]{1,0:T(8,128)S(1)} %fusion.58, bf16[2048,1024]{1,0:T(8,128)(2,1)} %constant_dynamic-update-slice_fusion.14, ...), kind=kOutput, calls=%fused_computation.21 | convolution fusion | flops 4323278848 | bytes 23068672 | tf_op jit(solution)/shard_map/dot_general | solution.py:59
  506.7 10.9 fusion.74
  517.7 4.7 fusion.57
  522.3 9.9 convolution_add_fusion
  534.0 3.6 copy-done.25
  537.6 4.5 fusion.73
  545.9 7.5 fusion.56
  557.9 7.2 fusion.20
  569.0 3.7 fusion.61
  578.2 24.1 %collective-permute-done.100 = bf16[1024,1024]{1,0:T(8,128)(2,1)} collective-permute-done((bf16[1024,1024]{1,0:T(8,128)(2,1)S(1)}, bf16[1024,1024]{1,0:T(8,128)(2,1)}, u32[]{:S(2)}, u32[]{:S(2)}) %collective-permute-start.100) | collective-permute-done | bytes 2097184 | tf_op jit(solution)/shard_map/ppermute | solution.py:64
  605.2 42.1 %collective-permute-done.105 = bf16[1024,1024]{1,0:T(8,128)(2,1)} collective-permute-done((bf16[1024,1024]{1,0:T(8,128)(2,1)}, bf16[1024,1024]{1,0:T(8,128)(2,1)}, u32[]{:S(2)}, u32[]{:S(2)}) %collective-permute-start.105) | collective-permute-done | bytes 2097184 | tf_op jit(solution)/shard_map/ppermute | solution.py:64
  647.3 3.5 convert_add_fusion.1
  651.0 40.8 %collective-permute-done.110 = bf16[1024,1024]{1,0:T(8,128)(2,1)S(1)} collective-permute-done((bf16[1024,1024]{1,0:T(8,128)(2,1)}, bf16[1024,1024]{1,0:T(8,128)(2,1)S(1)}, u32[]{:S(2)}, u32[]{:S(2)}) %collective-permute-start.110) | collective-permute-done | bytes 2097184 | tf_op jit(solution)/shard_map/ppermute | solution.py:64
  693.1 3.5 convert_add_fusion
  696.6 4.0 collective-permute-start.58
  705.5 22.4 %collective-permute-done.58 = bf16[256,1024]{1,0:T(8,128)(2,1)S(1)} collective-permute-done((bf16[256,1024]{1,0:T(8,128)(2,1)S(1)}, bf16[256,1024]{1,0:T(8,128)(2,1)S(1)}, u32[]{:S(2)}, u32[]{:S(2)}) %collective-permute-start.58) | collective-permute-done | bytes 524320 | tf_op jit(solution)/shard_map/ppermute | solution.py:64
  728.8 58.2 %collective-permute-done.101 = bf16[512,1024]{1,0:T(8,128)(2,1)S(1)} collective-permute-done((bf16[512,1024]{1,0:T(8,128)(2,1)S(1)}, bf16[512,1024]{1,0:T(8,128)(2,1)S(1)}, u32[]{:S(2)}, u32[]{:S(2)}) %collective-permute-start.101) | collective-permute-done | bytes 1048608 | tf_op jit(solution)/shard_map/ppermute | solution.py:64
  787.9 21.5 %collective-permute-done.106 = bf16[512,1024]{1,0:T(8,128)(2,1)S(1)} collective-permute-done((bf16[512,1024]{1,0:T(8,128)(2,1)S(1)}, bf16[512,1024]{1,0:T(8,128)(2,1)S(1)}, u32[]{:S(2)}, u32[]{:S(2)}) %collective-permute-start.106) | collective-permute-done | bytes 1048608 | tf_op jit(solution)/shard_map/ppermute | solution.py:64
  809.8 21.4 %collective-permute-done.111 = bf16[1024,512]{1,0:T(8,128)(2,1)S(1)} collective-permute-done((bf16[1024,512]{1,0:T(8,128)(2,1)S(1)}, bf16[1024,512]{1,0:T(8,128)(2,1)S(1)}, u32[]{:S(2)}, u32[]{:S(2)}) %collective-permute-start.111) | collective-permute-done | bytes 1048608 | tf_op jit(solution)/shard_map/ppermute | solution.py:64
  836.0 3.5 collective-permute-start.71
  841.7 11.2 collective-permute-done.70
  852.9 9.1 collective-permute-start.108
  866.6 4.1 collective-permute-done.107
  876.5 5.8 collective-permute-done.112
  882.4 4.2 collective-permute-done.114
  888.0 6.5 fusion.24
  894.4 7.0 fusion.22
  901.4 17.6 %attend_back.1 = (f32[4,2,128,256]{3,2,1,0:T(8,128)}, f32[2,4,2,128,128]{4,3,2,1,0:T(8,128)}) custom-call(s32[10]{0:T(128)} %pad_add_fusion.info, bf16[4,2,128,256]{3,2,1,0:T(8,128)(2,1)} %add_convert_fusion.3.q_ref, bf16[2,4,2,128,128]{4,3,2,1,0:T(8,128)(2,1)} %pad_maximum_fusion.6.kv_ref, bf16[4,2,128,256]{3,2,1,0:T(8,128)(2,1)} %bitcast.147, ...), custom_call_target="tpu_custom_call" | custom-call | flops 5368709120 | bytes 4194304 | tf_op jit(solution)/shard_map/attend_back/pallas_call | solution.py:188
  970.1 4.2 collective-permute-start.87
  1000.0 15.0 %collective-permute-done.81 = bf16[512,256]{1,0:T(8,128)(2,1)S(1)} collective-permute-done((bf16[512,256]{1,0:T(8,128)(2,1)S(1)}, bf16[512,256]{1,0:T(8,128)(2,1)S(1)}, u32[]{:S(2)}, u32[]{:S(2)}) %collective-permute-start.81) | collective-permute-done | bytes 262176 | tf_op jit(solution)/shard_map/ppermute | solution.py:64
  1019.6 3.7 fusion.60
  1028.3 11.0 collective-permute-done.78
  1039.3 10.6 collective-permute-done.77
  1055.5 3.7 fusion.9
  1059.2 72.9 %reduce-scatter.4.cloned.1.call-done = f32[128,2]{1,0:T(8,128)} async-done(((f32[2048,2]{1,0:T(8,128)}), f32[128,2]{1,0:T(8,128)}) %reduce-scatter.4.cloned.1.call-update) | async-done | bytes 1040
  (600 shorter events, 321.7 us)
Async XLA Ops:
  7.2 1124.8 %reduce-scatter.4.cloned.1.call-start = ((), (), s32[]{:S(2)}) async-start(), calls=%async_computation.1 | async-start | bytes 1114112
  9.2 96.2 %collective-permute-start = (bf16[256,1024]{1,0:T(8,128)(2,1)}, bf16[256,1024]{1,0:T(8,128)(2,1)}, u32[]{:S(2)}, u32[]{:S(2)}) collective-permute-start(bf16[256,1024]{1,0:T(8,128)(2,1)} %constant_dynamic-slice_fusion.34), channel_id=1, source_target_pairs={{0,2},{2,0},{4,6},{6,4},{8,10},{10,8},{12,14},{14,12},{1,3},{3,1},... | collective-permute-start | bytes 1572872 | tf_op jit(solution)/shard_map/ppermute | solution.py:64
  12.2 94.4 %collective-permute-start.1 = (bf16[256,1024]{1,0:T(8,128)(2,1)}, bf16[256,1024]{1,0:T(8,128)(2,1)S(1)}, u32[]{:S(2)}, u32[]{:S(2)}) collective-permute-start(bf16[256,1024]{1,0:T(8,128)(2,1)} %constant_dynamic-slice_fusion.34), channel_id=1, source_target_pairs={{0,4},{2,6},{4,0},{6,2},{8,12},{10,14},{12,8},{14,10},{1,5},{3,7},... | collective-permute-start | bytes 1572872 | tf_op jit(solution)/shard_map/ppermute | solution.py:64
  13.8 95.8 %collective-permute-start.2 = (bf16[256,1024]{1,0:T(8,128)(2,1)}, bf16[256,1024]{1,0:T(8,128)(2,1)S(1)}, u32[]{:S(2)}, u32[]{:S(2)}) collective-permute-start(bf16[256,1024]{1,0:T(8,128)(2,1)} %constant_dynamic-slice_fusion.34), channel_id=1, source_target_pairs={{0,6},{2,4},{4,2},{6,0},{8,14},{10,12},{12,10},{14,8},{1,7},{3,5},... | collective-permute-start | bytes 1572872 | tf_op jit(solution)/shard_map/ppermute | solution.py:64
  15.4 80.3 %collective-permute-start.4 = (bf16[128,256]{1,0:T(8,128)(2,1)}, bf16[128,256]{1,0:T(8,128)(2,1)}, u32[]{:S(2)}, u32[]{:S(2)}) collective-permute-start(bf16[128,256]{1,0:T(8,128)(2,1)} %get-tuple-element.107), channel_id=1, source_target_pairs={{0,2},{2,0},{4,6},{6,4},{8,10},{10,8},{12,14},{14,12},{1,3},{3,1},... | collective-permute-start | bytes 196616 | tf_op jit(solution)/shard_map/ppermute | solution.py:64
  17.5 55.5 %collective-permute-start.10 = (bf16[128,64]{1,0:T(8,128)(2,1)S(1)}, bf16[128,64]{1,0:T(8,128)(2,1)S(1)}, u32[]{:S(2)}, u32[]{:S(2)}) collective-permute-start(bf16[128,64]{1,0:T(8,128)(2,1)S(1)} %get-tuple-element.119), channel_id=1, source_target_pairs={{0,2},{2,0},{4,6},{6,4},{8,10},{10,8},{12,14},{14,12},{1,3},{3,1},... | collective-permute-start | bytes 49160 | tf_op jit(solution)/shard_map/ppermute | solution.py:64
  111.7 36.8 %collective-permute-start.3 = (bf16[768,1024]{1,0:T(8,128)(2,1)S(1)}, bf16[768,1024]{1,0:T(8,128)(2,1)S(1)}, u32[]{:S(2)}, u32[]{:S(2)}) collective-permute-start(bf16[768,1024]{1,0:T(8,128)(2,1)S(1)} %constant_dynamic-update-slice_fusion.51), channel_id=1, source_target_pairs={{0,1},{1,0},{2,3},{3,2},{4,5},{5,4},{6,7},{7,6},{8,9},{9,8},{10,11... | collective-permute-start | bytes 4718600 | tf_op jit(solution)/shard_map/ppermute | solution.py:64
  115.3 25.6 %collective-permute-start.8 = (bf16[512,256]{1,0:T(8,128)(2,1)S(1)}, bf16[512,256]{1,0:T(8,128)(2,1)S(1)}, u32[]{:S(2)}, u32[]{:S(2)}) collective-permute-start(bf16[512,256]{1,0:T(8,128)(2,1)S(1)} %constant_dynamic-update-slice_fusion.48), channel_id=1, source_target_pairs={{0,16},{16,0},{1,17},{17,1},{2,18},{18,2},{3,19},{19,3},{4,20},{20... | collective-permute-start | bytes 786440 | tf_op jit(solution)/shard_map/ppermute | solution.py:64
  116.0 24.2 %collective-permute-start.26 = (bf16[256,512]{1,0:T(8,128)(2,1)S(1)}, bf16[256,512]{1,0:T(8,128)(2,1)S(1)}, u32[]{:S(2)}, u32[]{:S(2)}) collective-permute-start(bf16[256,512]{1,0:T(8,128)(2,1)S(1)} %constant_dynamic-update-slice_fusion.25), channel_id=1, source_target_pairs={{0,8},{2,10},{4,12},{6,14},{8,0},{10,2},{12,4},{14,6},{1,9},{3,11}... | collective-permute-start | bytes 786440 | tf_op jit(solution)/shard_map/ppermute | solution.py:64
  219.7 50.1 %collective-permute-start.29 = (bf16[1024,1024]{1,0:T(8,128)(2,1)}, bf16[1024,1024]{1,0:T(8,128)(2,1)}, u32[]{:S(2)}, u32[]{:S(2)}) collective-permute-start(bf16[1024,1024]{1,0:T(8,128)(2,1)} %dynamic-slice_convert_fusion.6), channel_id=1, source_target_pairs={{0,1},{1,0},{2,3},{3,2},{4,5},{5,4},{6,7},{7,6},{8,9},{9,8},{10,11... | collective-permute-start | bytes 6291464 | tf_op jit(solution)/shard_map/ppermute | solution.py:64
  232.6 53.5 %collective-permute-start.61 = (bf16[256,1024]{1,0:T(8,128)(2,1)}, bf16[256,1024]{1,0:T(8,128)(2,1)}, u32[]{:S(2)}, u32[]{:S(2)}) collective-permute-start(bf16[256,1024]{1,0:T(8,128)(2,1)} %constant_dynamic-slice_fusion.9), channel_id=1, source_target_pairs={{0,2},{2,0},{4,6},{6,4},{8,10},{10,8},{12,14},{14,12},{1,3},{3,1},... | collective-permute-start | bytes 1572872 | tf_op jit(solution)/shard_map/ppermute | solution.py:64
  237.3 26.1 %collective-permute-start.44 = (bf16[128,1024]{1,0:T(8,128)(2,1)}, bf16[128,1024]{1,0:T(8,128)(2,1)S(1)}, u32[]{:S(2)}, u32[]{:S(2)}) collective-permute-start(bf16[128,1024]{1,0:T(8,128)(2,1)} %get-tuple-element.86), channel_id=1, source_target_pairs={{0,2},{2,0},{4,6},{6,4},{8,10},{10,8},{12,14},{14,12},{1,3},{3,1},... | collective-permute-start | bytes 786440 | tf_op jit(solution)/shard_map/ppermute | solution.py:64
  239.8 24.9 %collective-permute-start.45 = (bf16[128,1024]{1,0:T(8,128)(2,1)}, bf16[128,1024]{1,0:T(8,128)(2,1)S(1)}, u32[]{:S(2)}, u32[]{:S(2)}) collective-permute-start(bf16[128,1024]{1,0:T(8,128)(2,1)} %get-tuple-element.88), channel_id=1, source_target_pairs={{0,4},{2,6},{4,0},{6,2},{8,12},{10,14},{12,8},{14,10},{1,5},{3,7},... | collective-permute-start | bytes 786440 | tf_op jit(solution)/shard_map/ppermute | solution.py:64
  244.7 30.8 %collective-permute-start.46 = (bf16[128,1024]{1,0:T(8,128)(2,1)}, bf16[128,1024]{1,0:T(8,128)(2,1)S(1)}, u32[]{:S(2)}, u32[]{:S(2)}) collective-permute-start(bf16[128,1024]{1,0:T(8,128)(2,1)} %get-tuple-element.85), channel_id=1, source_target_pairs={{0,6},{2,4},{4,2},{6,0},{8,14},{10,12},{12,10},{14,8},{1,7},{3,5},... | collective-permute-start | bytes 786440 | tf_op jit(solution)/shard_map/ppermute | solution.py:64
  275.4 34.0 %collective-permute-start.32 = (bf16[256,1024]{1,0:T(8,128)(2,1)S(1)}, bf16[256,1024]{1,0:T(8,128)(2,1)S(1)}, u32[]{:S(2)}, u32[]{:S(2)}) collective-permute-start(bf16[256,1024]{1,0:T(8,128)(2,1)S(1)} %get-tuple-element.63), channel_id=1, source_target_pairs={{0,6},{2,4},{4,2},{6,0},{8,14},{10,12},{12,10},{14,8},{1,7},{3,5},... | collective-permute-start | bytes 1572872 | tf_op jit(solution)/shard_map/ppermute | solution.py:64
  278.2 40.2 %collective-permute-start.31 = (bf16[256,1024]{1,0:T(8,128)(2,1)S(1)}, bf16[256,1024]{1,0:T(8,128)(2,1)S(1)}, u32[]{:S(2)}, u32[]{:S(2)}) collective-permute-start(bf16[256,1024]{1,0:T(8,128)(2,1)S(1)} %get-tuple-element.64), channel_id=1, source_target_pairs={{0,4},{2,6},{4,0},{6,2},{8,12},{10,14},{12,8},{14,10},{1,5},{3,7},... | collective-permute-start | bytes 1572872 | tf_op jit(solution)/shard_map/ppermute | solution.py:64
  283.0 38.3 %collective-permute-start.30 = (bf16[256,1024]{1,0:T(8,128)(2,1)S(1)}, bf16[256,1024]{1,0:T(8,128)(2,1)S(1)}, u32[]{:S(2)}, u32[]{:S(2)}) collective-permute-start(bf16[256,1024]{1,0:T(8,128)(2,1)S(1)} %get-tuple-element.62), channel_id=1, source_target_pairs={{0,2},{2,0},{4,6},{6,4},{8,10},{10,8},{12,14},{14,12},{1,3},{3,1},... | collective-permute-start | bytes 1572872 | tf_op jit(solution)/shard_map/ppermute | solution.py:64
  285.2 81.2 %collective-permute-start.53 = (bf16[1024,512]{1,0:T(8,128)(2,1)S(1)}, bf16[1024,512]{1,0:T(8,128)(2,1)}, u32[]{:S(2)}, u32[]{:S(2)}) collective-permute-start(bf16[1024,512]{1,0:T(8,128)(2,1)S(1)} %constant_dynamic-update-slice_fusion.4), channel_id=1, source_target_pairs={{0,8},{2,10},{4,12},{6,14},{8,0},{10,2},{12,4},{14,6},{1,9},{3,11}... | collective-permute-start | bytes 3145736 | tf_op jit(solution)/shard_map/ppermute | solution.py:64
  286.1 82.3 %collective-permute-start.54 = (bf16[1024,512]{1,0:T(8,128)(2,1)S(1)}, bf16[1024,512]{1,0:T(8,128)(2,1)S(1)}, u32[]{:S(2)}, u32[]{:S(2)}) collective-permute-start(bf16[1024,512]{1,0:T(8,128)(2,1)S(1)} %constant_dynamic-update-slice_fusion.4), channel_id=1, source_target_pairs={{0,16},{16,0},{1,17},{17,1},{2,18},{18,2},{3,19},{19,3},{4,20},{20... | collective-permute-start | bytes 3145736 | tf_op jit(solution)/shard_map/ppermute | solution.py:64
  309.5 42.6 %collective-permute-start.62 = (bf16[256,1024]{1,0:T(8,128)(2,1)}, bf16[256,1024]{1,0:T(8,128)(2,1)S(1)}, u32[]{:S(2)}, u32[]{:S(2)}) collective-permute-start(bf16[256,1024]{1,0:T(8,128)(2,1)} %constant_dynamic-slice_fusion.9), channel_id=1, source_target_pairs={{0,4},{2,6},{4,0},{6,2},{8,12},{10,14},{12,8},{14,10},{1,5},{3,7},... | collective-permute-start | bytes 1572872 | tf_op jit(solution)/shard_map/ppermute | solution.py:64
  318.4 46.0 %collective-permute-start.63 = (bf16[256,1024]{1,0:T(8,128)(2,1)}, bf16[256,1024]{1,0:T(8,128)(2,1)S(1)}, u32[]{:S(2)}, u32[]{:S(2)}) collective-permute-start(bf16[256,1024]{1,0:T(8,128)(2,1)} %constant_dynamic-slice_fusion.9), channel_id=1, source_target_pairs={{0,6},{2,4},{4,2},{6,0},{8,14},{10,12},{12,10},{14,8},{1,7},{3,5},... | collective-permute-start | bytes 1572872 | tf_op jit(solution)/shard_map/ppermute | solution.py:64
  321.4 80.9 %collective-permute-start.47 = (bf16[512,1024]{1,0:T(8,128)(2,1)}, bf16[512,1024]{1,0:T(8,128)(2,1)}, u32[]{:S(2)}, u32[]{:S(2)}) collective-permute-start(bf16[512,1024]{1,0:T(8,128)(2,1)} %constant_dynamic-update-slice_fusion.11), channel_id=1, source_target_pairs={{0,8},{2,10},{4,12},{6,14},{8,0},{10,2},{12,4},{14,6},{1,9},{3,11}... | collective-permute-start | bytes 3145736 | tf_op jit(solution)/shard_map/ppermute | solution.py:64
  364.3 40.8 %collective-permute-start.48 = (bf16[512,1024]{1,0:T(8,128)(2,1)}, bf16[512,1024]{1,0:T(8,128)(2,1)S(1)}, u32[]{:S(2)}, u32[]{:S(2)}) collective-permute-start(bf16[512,1024]{1,0:T(8,128)(2,1)} %constant_dynamic-update-slice_fusion.11), channel_id=1, source_target_pairs={{0,16},{16,0},{1,17},{17,1},{2,18},{18,2},{3,19},{19,3},{4,20},{20... | collective-permute-start | bytes 3145736 | tf_op jit(solution)/shard_map/ppermute | solution.py:64
  366.4 55.6 %collective-permute-start.41 = (bf16[512,1024]{1,0:T(8,128)(2,1)}, bf16[512,1024]{1,0:T(8,128)(2,1)}, u32[]{:S(2)}, u32[]{:S(2)}) collective-permute-start(bf16[512,1024]{1,0:T(8,128)(2,1)} %constant_dynamic-update-slice_fusion.18), channel_id=1, source_target_pairs={{0,8},{2,10},{4,12},{6,14},{8,0},{10,2},{12,4},{14,6},{1,9},{3,11}... | collective-permute-start | bytes 3145736 | tf_op jit(solution)/shard_map/ppermute | solution.py:64
  368.4 56.7 %collective-permute-start.42 = (bf16[512,1024]{1,0:T(8,128)(2,1)}, bf16[512,1024]{1,0:T(8,128)(2,1)S(1)}, u32[]{:S(2)}, u32[]{:S(2)}) collective-permute-start(bf16[512,1024]{1,0:T(8,128)(2,1)} %constant_dynamic-update-slice_fusion.18), channel_id=1, source_target_pairs={{0,16},{16,0},{1,17},{17,1},{2,18},{18,2},{3,19},{19,3},{4,20},{20... | collective-permute-start | bytes 3145736 | tf_op jit(solution)/shard_map/ppermute | solution.py:64
  368.7 57.7 %collective-permute-start.64 = (bf16[768,1024]{1,0:T(8,128)(2,1)S(1)}, bf16[768,1024]{1,0:T(8,128)(2,1)S(1)}, u32[]{:S(2)}, u32[]{:S(2)}) collective-permute-start(bf16[768,1024]{1,0:T(8,128)(2,1)S(1)} %constant_dynamic-update-slice_fusion.57), channel_id=1, source_target_pairs={{0,1},{1,0},{2,3},{3,2},{4,5},{5,4},{6,7},{7,6},{8,9},{9,8},{10,11... | collective-permute-start | bytes 4718600 | tf_op jit(solution)/shard_map/ppermute | solution.py:64
  402.2 31.9 %collective-permute-start.34 = (bf16[256,1024]{1,0:T(8,128)(2,1)}, bf16[256,1024]{1,0:T(8,128)(2,1)}, u32[]{:S(2)}, u32[]{:S(2)}) collective-permute-start(bf16[256,1024]{1,0:T(8,128)(2,1)} %constant_dynamic-slice_fusion.19), channel_id=1, source_target_pairs={{0,2},{2,0},{4,6},{6,4},{8,10},{10,8},{12,14},{14,12},{1,3},{3,1},... | collective-permute-start | bytes 1572872 | tf_op jit(solution)/shard_map/ppermute | solution.py:64
  405.1 44.6 %collective-permute-start.55 = (bf16[1024,512]{1,0:T(8,128)(2,1)}, bf16[1024,512]{1,0:T(8,128)(2,1)}, u32[]{:S(2)}, u32[]{:S(2)}) collective-permute-start(bf16[1024,512]{1,0:T(8,128)(2,1)} %collective-permute-done.53), channel_id=1, source_target_pairs={{0,16},{16,0},{1,17},{17,1},{2,18},{18,2},{3,19},{19,3},{4,20},{20... | collective-permute-start | bytes 3145736 | tf_op jit(solution)/shard_map/ppermute | solution.py:64
  422.0 36.2 %collective-permute-start.49 = (bf16[512,1024]{1,0:T(8,128)(2,1)}, bf16[512,1024]{1,0:T(8,128)(2,1)}, u32[]{:S(2)}, u32[]{:S(2)}) collective-permute-start(bf16[512,1024]{1,0:T(8,128)(2,1)} %collective-permute-done.47), channel_id=1, source_target_pairs={{0,16},{16,0},{1,17},{17,1},{2,18},{18,2},{3,19},{19,3},{4,20},{20... | collective-permute-start | bytes 3145736 | tf_op jit(solution)/shard_map/ppermute | solution.py:64
  425.1 53.7 %collective-permute-start.43 = (bf16[512,1024]{1,0:T(8,128)(2,1)}, bf16[512,1024]{1,0:T(8,128)(2,1)}, u32[]{:S(2)}, u32[]{:S(2)}) collective-permute-start(bf16[512,1024]{1,0:T(8,128)(2,1)} %collective-permute-done.41), channel_id=1, source_target_pairs={{0,16},{16,0},{1,17},{17,1},{2,18},{18,2},{3,19},{19,3},{4,20},{20... | collective-permute-start | bytes 3145736 | tf_op jit(solution)/shard_map/ppermute | solution.py:64
  449.6 36.2 %collective-permute-start.37 = (bf16[768,1024]{1,0:T(8,128)(2,1)S(1)}, bf16[768,1024]{1,0:T(8,128)(2,1)S(1)}, u32[]{:S(2)}, u32[]{:S(2)}) collective-permute-start(bf16[768,1024]{1,0:T(8,128)(2,1)S(1)} %constant_dynamic-update-slice_fusion.54), channel_id=1, source_target_pairs={{0,1},{1,0},{2,3},{3,2},{4,5},{5,4},{6,7},{7,6},{8,9},{9,8},{10,11... | collective-permute-start | bytes 4718600 | tf_op jit(solution)/shard_map/ppermute | solution.py:64
  534.0 35.1 %collective-permute-start.65 = (bf16[1024,1024]{1,0:T(8,128)(2,1)}, bf16[1024,1024]{1,0:T(8,128)(2,1)}, u32[]{:S(2)}, u32[]{:S(2)}) collective-permute-start(bf16[1024,1024]{1,0:T(8,128)(2,1)} %dynamic-slice_convert_fusion.4), channel_id=1, source_target_pairs={{0,1},{1,0},{2,3},{3,2},{4,5},{5,4},{6,7},{7,6},{8,9},{9,8},{10,11... | collective-permute-start | bytes 6291464 | tf_op jit(solution)/shard_map/ppermute | solution.py:64
  545.9 27.9 %collective-permute-start.56 = (bf16[1024,1024]{1,0:T(8,128)(2,1)}, bf16[1024,1024]{1,0:T(8,128)(2,1)S(1)}, u32[]{:S(2)}, u32[]{:S(2)}) collective-permute-start(bf16[1024,1024]{1,0:T(8,128)(2,1)} %dynamic-slice_convert_fusion.5), channel_id=1, source_target_pairs={{0,1},{1,0},{2,3},{3,2},{4,5},{5,4},{6,7},{7,6},{8,9},{9,8},{10,11... | collective-permute-start | bytes 6291464 | tf_op jit(solution)/shard_map/ppermute | solution.py:64
  553.7 48.6 %collective-permute-start.100 = (bf16[1024,1024]{1,0:T(8,128)(2,1)S(1)}, bf16[1024,1024]{1,0:T(8,128)(2,1)}, u32[]{:S(2)}, u32[]{:S(2)}) collective-permute-start(bf16[1024,1024]{1,0:T(8,128)(2,1)S(1)} %dynamic-slice_convert_fusion.2), channel_id=1, source_target_pairs={{0,16},{16,0},{1,17},{17,1},{2,18},{18,2},{3,19},{19,3},{4,20},{20... | collective-permute-start | bytes 6291464 | tf_op jit(solution)/shard_map/ppermute | solution.py:64
  557.4 89.9 %collective-permute-start.105 = (bf16[1024,1024]{1,0:T(8,128)(2,1)}, bf16[1024,1024]{1,0:T(8,128)(2,1)}, u32[]{:S(2)}, u32[]{:S(2)}) collective-permute-start(bf16[1024,1024]{1,0:T(8,128)(2,1)} %dynamic-slice_convert_fusion.1), channel_id=1, source_target_pairs={{0,16},{16,0},{1,17},{17,1},{2,18},{18,2},{3,19},{19,3},{4,20},{20... | collective-permute-start | bytes 6291464 | tf_op jit(solution)/shard_map/ppermute | solution.py:64
  567.1 124.7 %collective-permute-start.110 = (bf16[1024,1024]{1,0:T(8,128)(2,1)}, bf16[1024,1024]{1,0:T(8,128)(2,1)S(1)}, u32[]{:S(2)}, u32[]{:S(2)}) collective-permute-start(bf16[1024,1024]{1,0:T(8,128)(2,1)} %dynamic-slice_convert_fusion), channel_id=1, source_target_pairs={{0,16},{16,0},{1,17},{17,1},{2,18},{18,2},{3,19},{19,3},{4,20},{20... | collective-permute-start | bytes 6291464 | tf_op jit(solution)/shard_map/ppermute | solution.py:64
  573.8 122.8 %collective-permute-start.68 = (bf16[256,1024]{1,0:T(8,128)(2,1)}, bf16[256,1024]{1,0:T(8,128)(2,1)S(1)}, u32[]{:S(2)}, u32[]{:S(2)}) collective-permute-start(bf16[256,1024]{1,0:T(8,128)(2,1)} %get-tuple-element.57), channel_id=1, source_target_pairs={{0,6},{2,4},{4,2},{6,0},{8,14},{10,12},{12,10},{14,8},{1,7},{3,5},... | collective-permute-start | bytes 1572872 | tf_op jit(solution)/shard_map/ppermute | solution.py:64
  573.8 126.8 %collective-permute-start.67 = (bf16[256,1024]{1,0:T(8,128)(2,1)}, bf16[256,1024]{1,0:T(8,128)(2,1)}, u32[]{:S(2)}, u32[]{:S(2)}) collective-permute-start(bf16[256,1024]{1,0:T(8,128)(2,1)} %get-tuple-element.58), channel_id=1, source_target_pairs={{0,4},{2,6},{4,0},{6,2},{8,12},{10,14},{12,8},{14,10},{1,5},{3,7},... | collective-permute-start | bytes 1572872 | tf_op jit(solution)/shard_map/ppermute | solution.py:64
  602.3 98.6 %collective-permute-start.66 = (bf16[256,1024]{1,0:T(8,128)(2,1)S(1)}, bf16[256,1024]{1,0:T(8,128)(2,1)}, u32[]{:S(2)}, u32[]{:S(2)}) collective-permute-start(bf16[256,1024]{1,0:T(8,128)(2,1)S(1)} %get-tuple-element.56), channel_id=1, source_target_pairs={{0,2},{2,0},{4,6},{6,4},{8,10},{10,8},{12,14},{14,12},{1,3},{3,1},... | collective-permute-start | bytes 1572872 | tf_op jit(solution)/shard_map/ppermute | solution.py:64
  647.3 55.3 %collective-permute-start.59 = (bf16[256,1024]{1,0:T(8,128)(2,1)S(1)}, bf16[256,1024]{1,0:T(8,128)(2,1)S(1)}, u32[]{:S(2)}, u32[]{:S(2)}) collective-permute-start(bf16[256,1024]{1,0:T(8,128)(2,1)S(1)} %get-tuple-element.60), channel_id=1, source_target_pairs={{0,6},{2,4},{4,2},{6,0},{8,14},{10,12},{12,10},{14,8},{1,7},{3,5},... | collective-permute-start | bytes 1572872 | tf_op jit(solution)/shard_map/ppermute | solution.py:64
  693.0 93.9 %collective-permute-start.101 = (bf16[512,1024]{1,0:T(8,128)(2,1)S(1)}, bf16[512,1024]{1,0:T(8,128)(2,1)S(1)}, u32[]{:S(2)}, u32[]{:S(2)}) collective-permute-start(bf16[512,1024]{1,0:T(8,128)(2,1)S(1)} %dynamic-slice_convert_fusion.9), channel_id=1, source_target_pairs={{0,8},{2,10},{4,12},{6,14},{8,0},{10,2},{12,4},{14,6},{1,9},{3,11}... | collective-permute-start | bytes 3145736 | tf_op jit(solution)/shard_map/ppermute | solution.py:64
  696.6 31.3 %collective-permute-start.58 = (bf16[256,1024]{1,0:T(8,128)(2,1)S(1)}, bf16[256,1024]{1,0:T(8,128)(2,1)S(1)}, u32[]{:S(2)}, u32[]{:S(2)}) collective-permute-start(bf16[256,1024]{1,0:T(8,128)(2,1)S(1)} %get-tuple-element.61), channel_id=1, source_target_pairs={{0,4},{2,6},{4,0},{6,2},{8,12},{10,14},{12,8},{14,10},{1,5},{3,7},... | collective-permute-start | bytes 1572872 | tf_op jit(solution)/shard_map/ppermute | solution.py:64
  700.6 27.3 %collective-permute-start.57 = (bf16[256,1024]{1,0:T(8,128)(2,1)S(1)}, bf16[256,1024]{1,0:T(8,128)(2,1)S(1)}, u32[]{:S(2)}, u32[]{:S(2)}) collective-permute-start(bf16[256,1024]{1,0:T(8,128)(2,1)S(1)} %get-tuple-element.59), channel_id=1, source_target_pairs={{0,2},{2,0},{4,6},{6,4},{8,10},{10,8},{12,14},{14,12},{1,3},{3,1},... | collective-permute-start | bytes 1572872 | tf_op jit(solution)/shard_map/ppermute | solution.py:64
  700.9 108.5 %collective-permute-start.106 = (bf16[512,1024]{1,0:T(8,128)(2,1)S(1)}, bf16[512,1024]{1,0:T(8,128)(2,1)S(1)}, u32[]{:S(2)}, u32[]{:S(2)}) collective-permute-start(bf16[512,1024]{1,0:T(8,128)(2,1)S(1)} %dynamic-slice_convert_fusion.8), channel_id=1, source_target_pairs={{0,8},{2,10},{4,12},{6,14},{8,0},{10,2},{12,4},{14,6},{1,9},{3,11}... | collective-permute-start | bytes 3145736 | tf_op jit(solution)/shard_map/ppermute | solution.py:64
  702.5 128.6 %collective-permute-start.111 = (bf16[1024,512]{1,0:T(8,128)(2,1)S(1)}, bf16[1024,512]{1,0:T(8,128)(2,1)S(1)}, u32[]{:S(2)}, u32[]{:S(2)}) collective-permute-start(bf16[1024,512]{1,0:T(8,128)(2,1)S(1)} %dynamic-slice_convert_fusion.7), channel_id=1, source_target_pairs={{0,8},{2,10},{4,12},{6,14},{8,0},{10,2},{12,4},{14,6},{1,9},{3,11}... | collective-permute-start | bytes 3145736 | tf_op jit(solution)/shard_map/ppermute | solution.py:64
  727.9 104.5 %collective-permute-start.69 = (bf16[256,1024]{1,0:T(8,128)(2,1)S(1)}, bf16[256,1024]{1,0:T(8,128)(2,1)S(1)}, u32[]{:S(2)}, u32[]{:S(2)}) collective-permute-start(bf16[256,1024]{1,0:T(8,128)(2,1)S(1)} %fusion.30), channel_id=1, source_target_pairs={{0,1},{1,0},{2,3},{3,2},{4,5},{5,4},{6,7},{7,6},{8,9},{9,8},{10,11... | collective-permute-start | bytes 1572872 | tf_op jit(solution)/shard_map/ppermute | solution.py:64
  728.2 104.2 %collective-permute-start.60 = (bf16[256,1024]{1,0:T(8,128)(2,1)S(1)}, bf16[256,1024]{1,0:T(8,128)(2,1)S(1)}, u32[]{:S(2)}, u32[]{:S(2)}) collective-permute-start(bf16[256,1024]{1,0:T(8,128)(2,1)S(1)} %fusion.33), channel_id=1, source_target_pairs={{0,1},{1,0},{2,3},{3,2},{4,5},{5,4},{6,7},{7,6},{8,9},{9,8},{10,11... | collective-permute-start | bytes 1572872 | tf_op jit(solution)/shard_map/ppermute | solution.py:64
  787.6 52.5 %collective-permute-start.102 = (bf16[128,1024]{1,0:T(8,128)(2,1)S(1)}, bf16[128,1024]{1,0:T(8,128)(2,1)S(1)}, u32[]{:S(2)}, u32[]{:S(2)}) collective-permute-start(bf16[128,1024]{1,0:T(8,128)(2,1)S(1)} %get-tuple-element.51), channel_id=1, source_target_pairs={{0,2},{2,0},{4,6},{6,4},{8,10},{10,8},{12,14},{14,12},{1,3},{3,1},... | collective-permute-start | bytes 786440 | tf_op jit(solution)/shard_map/ppermute | solution.py:64
  809.5 30.7 %collective-permute-start.103 = (bf16[128,1024]{1,0:T(8,128)(2,1)S(1)}, bf16[128,1024]{1,0:T(8,128)(2,1)S(1)}, u32[]{:S(2)}, u32[]{:S(2)}) collective-permute-start(bf16[128,1024]{1,0:T(8,128)(2,1)S(1)} %get-tuple-element.50), channel_id=1, source_target_pairs={{0,4},{2,6},{4,0},{6,2},{8,12},{10,14},{12,8},{14,10},{1,5},{3,7},... | collective-permute-start | bytes 786440 | tf_op jit(solution)/shard_map/ppermute | solution.py:64
  831.2 35.3 %collective-permute-start.104 = (bf16[128,1024]{1,0:T(8,128)(2,1)S(1)}, bf16[128,1024]{1,0:T(8,128)(2,1)S(1)}, u32[]{:S(2)}, u32[]{:S(2)}) collective-permute-start(bf16[128,1024]{1,0:T(8,128)(2,1)S(1)} %get-tuple-element.49), channel_id=1, source_target_pairs={{0,6},{2,4},{4,2},{6,0},{8,14},{10,12},{12,10},{14,8},{1,7},{3,5},... | collective-permute-start | bytes 786440 | tf_op jit(solution)/shard_map/ppermute | solution.py:64
  836.0 26.0 %collective-permute-start.71 = (bf16[256,1024]{1,0:T(8,128)(2,1)S(1)}, bf16[256,1024]{1,0:T(8,128)(2,1)S(1)}, u32[]{:S(2)}, u32[]{:S(2)}) collective-permute-start(bf16[256,1024]{1,0:T(8,128)(2,1)S(1)} %constant_dynamic-slice_fusion.8), channel_id=1, source_target_pairs={{0,4},{2,6},{4,0},{6,2},{8,12},{10,14},{12,8},{14,10},{1,5},{3,7},... | collective-permute-start | bytes 1572872 | tf_op jit(solution)/shard_map/ppermute | solution.py:64
  840.1 24.1 %collective-permute-start.72 = (bf16[256,1024]{1,0:T(8,128)(2,1)S(1)}, bf16[256,1024]{1,0:T(8,128)(2,1)S(1)}, u32[]{:S(2)}, u32[]{:S(2)}) collective-permute-start(bf16[256,1024]{1,0:T(8,128)(2,1)S(1)} %constant_dynamic-slice_fusion.8), channel_id=1, source_target_pairs={{0,6},{2,4},{4,2},{6,0},{8,14},{10,12},{12,10},{14,8},{1,7},{3,5},... | collective-permute-start | bytes 1572872 | tf_op jit(solution)/shard_map/ppermute | solution.py:64
  840.1 30.6 %collective-permute-start.107 = (bf16[128,1024]{1,0:T(8,128)(2,1)S(1)}, bf16[128,1024]{1,0:T(8,128)(2,1)S(1)}, u32[]{:S(2)}, u32[]{:S(2)}) collective-permute-start(bf16[128,1024]{1,0:T(8,128)(2,1)S(1)} %get-tuple-element.48), channel_id=1, source_target_pairs={{0,2},{2,0},{4,6},{6,4},{8,10},{10,8},{12,14},{14,12},{1,3},{3,1},... | collective-permute-start | bytes 786440 | tf_op jit(solution)/shard_map/ppermute | solution.py:64
  852.9 20.0 %collective-permute-start.108 = (bf16[128,1024]{1,0:T(8,128)(2,1)S(1)}, bf16[128,1024]{1,0:T(8,128)(2,1)S(1)}, u32[]{:S(2)}, u32[]{:S(2)}) collective-permute-start(bf16[128,1024]{1,0:T(8,128)(2,1)S(1)} %get-tuple-element.47), channel_id=1, source_target_pairs={{0,4},{2,6},{4,0},{6,2},{8,12},{10,14},{12,8},{14,10},{1,5},{3,7},... | collective-permute-start | bytes 786440 | tf_op jit(solution)/shard_map/ppermute | solution.py:64
  866.5 20.2 %collective-permute-start.73 = (bf16[768,1024]{1,0:T(8,128)(2,1)S(1)}, bf16[768,1024]{1,0:T(8,128)(2,1)S(1)}, u32[]{:S(2)}, u32[]{:S(2)}) collective-permute-start(bf16[768,1024]{1,0:T(8,128)(2,1)S(1)} %constant_dynamic-update-slice_fusion.60), channel_id=1, source_target_pairs={{0,1},{1,0},{2,3},{3,2},{4,5},{5,4},{6,7},{7,6},{8,9},{9,8},{10,11... | collective-permute-start | bytes 4718600 | tf_op jit(solution)/shard_map/ppermute | solution.py:64
  937.4 56.5 %collective-permute-start.80 = (bf16[1024,256]{1,0:T(8,128)(2,1)}, bf16[1024,256]{1,0:T(8,128)(2,1)}, u32[]{:S(2)}, u32[]{:S(2)}) collective-permute-start(bf16[1024,256]{1,0:T(8,128)(2,1)} %dynamic-slice_convert_fusion.11), channel_id=1, source_target_pairs={{0,16},{16,0},{1,17},{17,1},{2,18},{18,2},{3,19},{19,3},{4,20},{20... | collective-permute-start | bytes 1572872 | tf_op jit(solution)/shard_map/ppermute | solution.py:64
  940.8 57.4 %collective-permute-start.95 = (bf16[256,1024]{1,0:T(8,128)(2,1)}, bf16[256,1024]{1,0:T(8,128)(2,1)}, u32[]{:S(2)}, u32[]{:S(2)}) collective-permute-start(bf16[256,1024]{1,0:T(8,128)(2,1)} %dynamic-slice_convert_fusion.10), channel_id=1, source_target_pairs={{0,16},{16,0},{1,17},{17,1},{2,18},{18,2},{3,19},{19,3},{4,20},{20... | collective-permute-start | bytes 1572872 | tf_op jit(solution)/shard_map/ppermute | solution.py:64
  963.5 56.1 %collective-permute-start.75 = (bf16[1024,1024]{1,0:T(8,128)(2,1)}, bf16[1024,1024]{1,0:T(8,128)(2,1)}, u32[]{:S(2)}, u32[]{:S(2)}) collective-permute-start(bf16[1024,1024]{1,0:T(8,128)(2,1)} %dynamic-slice_convert_fusion.3), channel_id=1, source_target_pairs={{0,1},{1,0},{2,3},{3,2},{4,5},{5,4},{6,7},{7,6},{8,9},{9,8},{10,11... | collective-permute-start | bytes 6291464 | tf_op jit(solution)/shard_map/ppermute | solution.py:64
  995.6 19.3 %collective-permute-start.81 = (bf16[512,256]{1,0:T(8,128)(2,1)S(1)}, bf16[512,256]{1,0:T(8,128)(2,1)S(1)}, u32[]{:S(2)}, u32[]{:S(2)}) collective-permute-start(bf16[512,256]{1,0:T(8,128)(2,1)S(1)} %dynamic-slice_convert_fusion.22), channel_id=1, source_target_pairs={{0,8},{2,10},{4,12},{6,14},{8,0},{10,2},{12,4},{14,6},{1,9},{3,11}... | collective-permute-start | bytes 786440 | tf_op jit(solution)/shard_map/ppermute | solution.py:64
  999.5 19.9 %collective-permute-start.96 = (bf16[256,512]{1,0:T(8,128)(2,1)S(1)}, bf16[256,512]{1,0:T(8,128)(2,1)S(1)}, u32[]{:S(2)}, u32[]{:S(2)}) collective-permute-start(bf16[256,512]{1,0:T(8,128)(2,1)S(1)} %dynamic-slice_convert_fusion.21), channel_id=1, source_target_pairs={{0,8},{2,10},{4,12},{6,14},{8,0},{10,2},{12,4},{14,6},{1,9},{3,11}... | collective-permute-start | bytes 786440 | tf_op jit(solution)/shard_map/ppermute | solution.py:64
  1023.5 26.4 %collective-permute-start.77 = (bf16[256,1024]{1,0:T(8,128)(2,1)S(1)}, bf16[256,1024]{1,0:T(8,128)(2,1)S(1)}, u32[]{:S(2)}, u32[]{:S(2)}) collective-permute-start(bf16[256,1024]{1,0:T(8,128)(2,1)S(1)} %get-tuple-element.54), channel_id=1, source_target_pairs={{0,4},{2,6},{4,0},{6,2},{8,12},{10,14},{12,8},{14,10},{1,5},{3,7},... | collective-permute-start | bytes 1572872 | tf_op jit(solution)/shard_map/ppermute | solution.py:64
  1026.1 23.8 %collective-permute-start.76 = (bf16[256,1024]{1,0:T(8,128)(2,1)S(1)}, bf16[256,1024]{1,0:T(8,128)(2,1)S(1)}, u32[]{:S(2)}, u32[]{:S(2)}) collective-permute-start(bf16[256,1024]{1,0:T(8,128)(2,1)S(1)} %get-tuple-element.52), channel_id=1, source_target_pairs={{0,2},{2,0},{4,6},{6,4},{8,10},{10,8},{12,14},{14,12},{1,3},{3,1},... | collective-permute-start | bytes 1572872 | tf_op jit(solution)/shard_map/ppermute | solution.py:64
  1027.1 23.3 %collective-permute-start.97 = (bf16[256,128]{1,0:T(8,128)(2,1)S(1)}, bf16[256,128]{1,0:T(8,128)(2,1)S(1)}, u32[]{:S(2)}, u32[]{:S(2)}) collective-permute-start(bf16[256,128]{1,0:T(8,128)(2,1)S(1)} %get-tuple-element.91), channel_id=1, source_target_pairs={{0,2},{2,0},{4,6},{6,4},{8,10},{10,8},{12,14},{14,12},{1,3},{3,1},... | collective-permute-start | bytes 196616 | tf_op jit(solution)/shard_map/ppermute | solution.py:64
  1028.2 22.4 %collective-permute-start.98 = (bf16[256,128]{1,0:T(8,128)(2,1)S(1)}, bf16[256,128]{1,0:T(8,128)(2,1)S(1)}, u32[]{:S(2)}, u32[]{:S(2)}) collective-permute-start(bf16[256,128]{1,0:T(8,128)(2,1)S(1)} %get-tuple-element.90), channel_id=1, source_target_pairs={{0,4},{2,6},{4,0},{6,2},{8,12},{10,14},{12,8},{14,10},{1,5},{3,7},... | collective-permute-start | bytes 196616 | tf_op jit(solution)/shard_map/ppermute | solution.py:64
  (130 other events, 2070.2 us)
Sparse Core Ops, SparseCore 0:
  1055.5 76.4 reduce-scatter.3

commit v2 on v1

--- a/solution.py
+++ b/solution.py
@@ -20,7 +20,7 @@
 LOW_FACTOR = 1.0
 HIGH_FACTOR = 4.0
 PRIOR_CONTEXT = 8192.0
-VMEM = 56 * 1024 * 1024
+VMEM = 62 * 1024 * 1024
 
 
 def inverse_freqs(head_dim):
@@ -296,6 +296,992 @@
     ).astype(jnp.float32)
 
 
+MESH = pl.DeviceIdType.MESH
+
+
+class Links:
+    def __init__(self, send_sem, recv_sem, local_sem, high_size):
+        self.send_sem, self.recv_sem, self.local_sem = send_sem, recv_sem, local_sem
+        self.x, self.seq, self.core = (lax.axis_index(a) for a in ("dp", "seq", "mp"))
+        self.high_size = high_size
+        self.low, self.high = self.seq % SQUARE, self.seq // SQUARE
+        self.count = self.local_count = 0
+        self.sent = []
+
+    def to(self, dx=0, dh=0, dl=0, dc=0):
+        seq = ((self.high + dh) % self.high_size) * SQUARE + (self.low + dl) % SQUARE
+        return ((self.x + dx) % 2, seq, (self.core + dc) % 2)
+
+    def copy(self, src, dst, **step):
+        k = self.count
+        self.count += 1
+        made = pltpu.make_async_remote_copy(
+            src_ref=src,
+            dst_ref=dst,
+            send_sem=self.send_sem.at[k],
+            recv_sem=self.recv_sem.at[k],
+            device_id=self.to(**step),
+            device_id_type=MESH,
+        )
+        made.start()
+        self.sent.append(made)
+        return made
+
+    def local(self, src, dst):
+        k = self.local_count
+        self.local_count += 1
+        made = pltpu.make_async_copy(src, dst, self.local_sem.at[k])
+        made.start()
+        return made
+
+    def greet(self, steps):
+        barrier = pltpu.get_barrier_semaphore()
+        for step in steps:
+            pl.semaphore_signal(barrier, inc=1, device_id=self.to(**step), device_id_type=MESH)
+        pl.semaphore_wait(barrier, len(steps))
+
+    def left(self, copies):
+        for made in copies:
+            made.wait_send()
+            self.sent = [one for one in self.sent if one is not made]
+
+    def finish(self):
+        for made in self.sent:
+            made.wait_send()
+
+
+def arrived(copies):
+    for made in copies:
+        made.wait_recv()
+
+
+class Weight:
+    def __init__(self, links, slice_of, spot):
+        self.links, self.spot = links, spot
+        l = links
+        self.own = l.local(slice_of(l.low), spot(l.x, l.high, l.low, 1))
+        self.near, self.far = [], []
+        for dh in range(2):
+            for dl in range(SQUARE):
+                if dh or dl:
+                    made = l.copy(
+                        slice_of((l.low + dl) % SQUARE),
+                        spot(l.x, l.high, l.low, 1),
+                        dh=dh,
+                        dl=dl,
+                    )
+                    (self.far if dh else self.near).append(made)
+
+    def pass_near(self):
+        self.own.wait()
+        arrived(self.near)
+        l = self.links
+        part = self.spot(l.x, l.high, 0, SQUARE)
+        self.across = [l.copy(part, part, dx=1)]
+
+    def pass_far(self):
+        arrived(self.far)
+        l = self.links
+        part = self.spot(l.x, 1 - l.high, 0, SQUARE)
+        self.across.append(l.copy(part, part, dx=1))
+
+    def wait(self):
+        arrived(self.across)
+
+
+def gather_rows(l, everyone, count, half_src):
+    return [
+        l.copy(half_src, everyone(l.core, l.low), dl=dl) for dl in range(1, SQUARE)
+    ]
+
+
+def gather_across(l, everyone, pushed):
+    handed = []
+    for dl in range(1, SQUARE):
+        pushed[dl - 1].wait_recv()
+        block = everyone(l.core, (l.low + SQUARE - dl) % SQUARE)
+        handed.append(l.copy(block, block, dc=1))
+    return handed
+
+
+def reduce_square(l, part, send_core, recv_core, send_block, recv_block, both):
+    handed = []
+    for j in range(SQUARE):
+        send_core[j] = part(j, 1 - l.core).astype(jnp.bfloat16)
+        handed.append(l.copy(send_core.at[j], recv_core.at[j], dc=1))
+    arrived(handed)
+    pushed = []
+    for dl in range(1, SQUARE):
+        j = (l.low + dl) % SQUARE
+        total = part(j, l.core) + recv_core[j].astype(jnp.float32)
+        send_block[dl] = total.astype(jnp.bfloat16)
+        pushed.append(l.copy(send_block.at[dl], recv_block.at[dl], dl=dl))
+    total = part(l.low, l.core) + recv_core[l.low].astype(jnp.float32)
+    for dl in range(1, SQUARE):
+        pushed[dl - 1].wait_recv()
+        total = total + recv_block[dl].astype(jnp.float32)
+    both[l.core] = total.astype(jnp.bfloat16)
+    l.copy(both.at[l.core], both.at[l.core], dc=1).wait_recv()
+
+
+def roll_heads(value):
+    width = value.shape[1]
+    lane = lax.broadcasted_iota(jnp.int32, value.shape, 1)
+    left = pltpu.roll(value, width - HD // 2, 1)
+    right = pltpu.roll(value, HD // 2, 1)
+    return jnp.where(lane % HD < HD // 2, left, right)
+
+
+def allowed_keys(l, ends, row, span, keys):
+    def segment_of(place):
+        total = jnp.zeros_like(place)
+        for doc in range(4):
+            total = total + (place >= ends[row * 4 + doc]).astype(jnp.int32)
+        return total
+
+    query = l.high * span + lax.broadcasted_iota(jnp.int32, (span, 1), 0)
+    key = lax.broadcasted_iota(jnp.int32, (1, keys), 1)
+    return (segment_of(query) == segment_of(key)) & (query >= key)
+
+
+def front_kernel(
+    sizes,
+    ends,
+    x_in,
+    g_in,
+    qkv_in,
+    gain_in,
+    wo_in,
+    wg_in,
+    wu_in,
+    wd_in,
+    cos_in,
+    sin_in,
+    qkv_out,
+    wo_out,
+    wg_out,
+    wu_out,
+    wd_out,
+    gain_out,
+    normed_one_out,
+    q_out,
+    kv_out,
+    attn_out,
+    residual_out,
+    normed_two_out,
+    g_out,
+    x_all,
+    normed,
+    wqkv,
+    wo,
+    gains,
+    gain_rows,
+    cos,
+    sin,
+    q,
+    kv,
+    attn,
+    low_attn,
+    send_core,
+    recv_core,
+    send_block,
+    recv_block,
+    both,
+    residual,
+    normed_two,
+    send_sem,
+    recv_sem,
+    local_sem,
+):
+    rows, local, model, high_size = sizes
+    own = rows * local
+    tokens = SQUARE * own
+    half = model // 2
+    block = qkv_in.shape[1]
+    heads = q.shape[2] // HD
+    span = SQUARE * local
+    keys = high_size * span
+    l = Links(send_sem, recv_sem, local_sem, high_size)
+    near = [dict(dl=dl) for dl in range(1, SQUARE)]
+    far = [dict(dh=1, dl=dl) for dl in range(SQUARE)]
+    l.greet(near + far + [dict(dx=1), dict(dc=1)])
+
+    def row_spot(ref):
+        def spot(x, h, low, n):
+            start = ((x * high_size + h) * SQUARE + low) * block
+            return ref.at[pl.ds(pl.multiple_of(start, block), n * block)]
+
+        return spot
+
+    def block_spot(ref):
+        return lambda x, h, low, n: ref.at[pl.ds((x * high_size + h) * SQUARE + low, n)]
+
+    def half_spot(ref):
+        def spot(x, h, low, n):
+            start = pl.multiple_of((h * SQUARE + low) * block, block)
+            return ref.at[x, :, pl.ds(start, n * block)]
+
+        return spot
+
+    def column_spot(ref):
+        def spot(x, h, low, n):
+            start = ((x * high_size + h) * SQUARE + low) * block
+            return ref.at[:, pl.ds(pl.multiple_of(start, block), n * block)]
+
+        return spot
+
+    def columns(ref, width):
+        return lambda j: ref.at[:, pl.ds(pl.multiple_of(j * width, width), width)]
+
+    def lines(ref, width):
+        return lambda j: ref.at[pl.ds(pl.multiple_of(j * width, width), width)]
+
+    def x_spot(side, low):
+        return x_all.at[side, pl.ds(pl.multiple_of(low * own, own), own)]
+
+    def g_spot(side, low):
+        return g_out.at[
+            pl.ds(pl.multiple_of(low * own, own), own),
+            pl.ds(pl.multiple_of(side * half, half), half),
+        ]
+
+    def normed_two_spot(side, low):
+        return normed_two.at[side, pl.ds(pl.multiple_of(low * own, own), own)]
+
+    def side_of(ref, side):
+        return ref.at[:, pl.ds(pl.multiple_of(side * half, half), half)]
+
+    loads = [l.local(side_of(x_in, side), x_spot(side, l.low)) for side in range(2)]
+    loads += [l.local(cos_in, cos), l.local(sin_in, sin)]
+    w_gain = Weight(l, lambda j: gain_in.at[pl.ds(0, 1)], block_spot(gains))
+    w_qkv = Weight(l, lambda j: qkv_in.at[j], row_spot(wqkv))
+    x_pushed = gather_rows(l, x_spot, 0, side_of(x_in, l.core))
+    w_o = Weight(l, lines(wo_in, wo.shape[1]), half_spot(wo))
+    w_gate = Weight(l, columns(wg_in, wg_out.shape[1]), row_spot(wg_out))
+
+    w_gain.pass_near()
+    w_qkv.pass_near()
+    w_gain.pass_far()
+    w_qkv.pass_far()
+    x_handed = gather_across(l, x_spot, x_pushed)
+    w_o.pass_near()
+    w_o.pass_far()
+    w_up = Weight(l, columns(wu_in, wu_out.shape[1]), row_spot(wu_out))
+    for made in loads:
+        made.wait()
+    w_gain.wait()
+    for b in range(gains.shape[0]):
+        tile = gains[b].astype(jnp.float32)
+        gain_rows[0:1, b * block : (b + 1) * block] = tile[0:1]
+        gain_rows[1:2, b * block : (b + 1) * block] = tile[1:2]
+    arrived(x_handed)
+
+    step = 128
+
+    def norm_step(i, carry):
+        at = pl.ds(pl.multiple_of(i * step, step), step)
+        first, second = x_all[0, at].astype(jnp.float32), x_all[1, at].astype(jnp.float32)
+        total = jnp.sum(first * first, axis=1, keepdims=True)
+        total = total + jnp.sum(second * second, axis=1, keepdims=True)
+        scale = lax.rsqrt(total / model + EPSILON)
+        normed[at, :half] = (first * scale * gain_rows[0:1, :half]).astype(jnp.bfloat16)
+        normed[at, half:] = (second * scale * gain_rows[0:1, half:]).astype(jnp.bfloat16)
+        return carry
+
+    lax.fori_loop(0, tokens // step, norm_step, 0)
+    stores = [l.local(normed, normed_one_out)]
+    w_qkv.wait()
+    stores += [l.local(wqkv, qkv_out), l.local(gain_rows, gain_out)]
+
+    def project_step(i, carry):
+        at = pl.ds(pl.multiple_of(i * local, local), local)
+        pre = dot(normed[at], wqkv[...])
+        times = heads // 2
+        cos_all = jnp.concatenate([cos[at, : 2 * HD]] * times + [cos[at, 2 * HD :]], axis=1)
+        sin_all = jnp.concatenate([sin[at, : 2 * HD]] * times + [sin[at, 2 * HD :]], axis=1)
+        turned = pre * cos_all + roll_heads(pre) * sin_all
+        spot = pl.ds(pl.multiple_of((i // rows) * local, local), local)
+        q[i % rows, spot] = (turned[:, : heads * HD].astype(jnp.bfloat16) * HD ** (-0.5)).astype(
+            jnp.bfloat16
+        )
+        kv[l.high, i % rows, spot] = turned[:, heads * HD :].astype(jnp.bfloat16)
+        return carry
+
+    lax.fori_loop(0, SQUARE * rows, project_step, 0)
+    kv_copy = l.copy(kv.at[l.high], kv.at[l.high], dh=1)
+    stores.append(l.local(q, q_out))
+    w_gate.pass_near()
+    kv_copy.wait_recv()
+    stores.append(l.local(kv, kv_out))
+
+    def attend_row(r, carry):
+        allowed = allowed_keys(l, ends, r, span, keys)
+        kv_row = kv[:, r].reshape(keys, 2 * HD)
+        k, v = kv_row[:, :HD], kv_row[:, HD:]
+        q_row = q[r]
+        outs = []
+        for head in range(heads):
+            score = dot(q_row[:, head * HD : (head + 1) * HD], k, ((1,), (1,)))
+            score = jnp.where(allowed, score, MASKED)
+            top = jnp.max(score, axis=1, keepdims=True)
+            grown = jnp.exp(score - top)
+            total = jnp.sum(grown, axis=1, keepdims=True)
+            probs = (grown * (1.0 / total)).astype(jnp.bfloat16)
+            outs.append(dot(probs, v))
+        out = jnp.concatenate(outs, axis=1)
+        for j in range(SQUARE):
+            at = pl.ds(pl.multiple_of(j * own + r * local, local), local)
+            part = out[j * local : (j + 1) * local]
+            attn[at] = part
+            low_attn[at] = part.astype(jnp.bfloat16)
+        return carry
+
+    lax.fori_loop(0, rows, attend_row, 0)
+    stores.append(l.local(attn, attn_out))
+    w_gate.pass_far()
+    w_down = Weight(l, lines(wd_in, wd_out.shape[0]), column_spot(wd_out))
+    w_o.wait()
+    stores.append(l.local(wo, wo_out))
+
+    def project_out(j, side):
+        at = pl.ds(pl.multiple_of(j * own, own), own)
+        return dot(low_attn[at], wo[side])
+
+    reduce_square(l, project_out, send_core, recv_core, send_block, recv_block, both)
+    at_own = pl.ds(pl.multiple_of(l.low * own, own), own)
+    total = jnp.zeros((own, 1), jnp.float32)
+    for side in range(2):
+        value = x_all[side, at_own].astype(jnp.float32) + both[side].astype(jnp.float32)
+        residual[:, side * half : (side + 1) * half] = value
+        total = total + jnp.sum(value * value, axis=1, keepdims=True)
+    scale = lax.rsqrt(total / model + EPSILON)
+    for side in range(2):
+        at = slice(side * half, (side + 1) * half)
+        normed_two[side, at_own] = (residual[:, at] * scale * gain_rows[1:2, at]).astype(
+            jnp.bfloat16
+        )
+    stores.append(l.local(residual, residual_out))
+    pushed = gather_rows(l, normed_two_spot, 0, normed_two_spot(l.core, l.low))
+    loads = [l.local(side_of(g_in, side), g_spot(side, l.low)) for side in range(2)]
+    g_pushed = gather_rows(l, g_spot, 0, side_of(g_in, l.core))
+    w_up.pass_near()
+    handed = gather_across(l, normed_two_spot, pushed)
+    arrived(handed)
+    for side in range(2):
+        stores.append(l.local(normed_two.at[side], side_of(normed_two_out, side)))
+    w_up.pass_far()
+    g_handed = gather_across(l, g_spot, g_pushed)
+    w_down.pass_near()
+    w_down.pass_far()
+    arrived(g_handed)
+    for weight in (w_gate, w_up, w_down):
+        weight.wait()
+    for made in loads + stores:
+        made.wait()
+    l.finish()
+
+
+def front(sizes, ends, x, g, qkv, gain, wo, wg, wu, wd, cos, sin):
+    rows, local, model, high_size = sizes
+    own = rows * local
+    tokens = SQUARE * own
+    half = model // 2
+    heads = wo.shape[0] // SQUARE // HD
+    width = qkv.shape[2]
+    ff = wg.shape[1] // SQUARE
+    blocks = model // qkv.shape[1]
+    span = SQUARE * local
+    low, f32 = jnp.bfloat16, jnp.float32
+    shape = jax.ShapeDtypeStruct
+    outs = (
+        shape((model, width), low),
+        shape((2, heads * HD, half), low),
+        shape((model, ff), low),
+        shape((model, ff), low),
+        shape((ff, model), low),
+        shape((8, model), f32),
+        shape((tokens, model), low),
+        shape((rows, span, heads * HD), low),
+        shape((high_size, rows, span, 2 * HD), low),
+        shape((tokens, heads * HD), f32),
+        shape((own, model), f32),
+        shape((tokens, model), low),
+        shape((tokens, model), low),
+    )
+    anywhere = pl.BlockSpec(memory_space=pl.ANY)
+    vmem = pltpu.VMEM
+    return pl.pallas_call(
+        functools.partial(front_kernel, sizes),
+        out_shape=outs,
+        in_specs=[pl.BlockSpec(memory_space=pltpu.SMEM)] + [anywhere] * 10,
+        out_specs=[anywhere] * len(outs),
+        scratch_shapes=[
+            vmem((2, tokens, half), low),
+            vmem((tokens, model), low),
+            vmem((model, width), low),
+            vmem((2, heads * HD, half), low),
+            vmem((blocks,) + gain.shape[1:], low),
+            vmem((8, model), f32),
+            vmem((tokens, 4 * HD), f32),
+            vmem((tokens, 4 * HD), f32),
+            vmem((rows, span, heads * HD), low),
+            vmem((high_size, rows, span, 2 * HD), low),
+            vmem((tokens, heads * HD), f32),
+            vmem((tokens, heads * HD), low),
+            vmem((SQUARE, own, half), low),
+            vmem((SQUARE, own, half), low),
+            vmem((SQUARE, own, half), low),
+            vmem((SQUARE, own, half), low),
+            vmem((2, own, half), low),
+            vmem((own, model), f32),
+            vmem((2, tokens, half), low),
+            pltpu.SemaphoreType.DMA((96,)),
+            pltpu.SemaphoreType.DMA((96,)),
+            pltpu.SemaphoreType.DMA((32,)),
+        ],
+        compiler_params=pltpu.CompilerParams(
+            collective_id=0, has_side_effects=True, vmem_limit_bytes=VMEM
+        ),
+        name="front",
+    )(ends, x, g, qkv, gain, wo, wg, wu, wd, cos, sin)
+
+
+class Grad:
+    def __init__(self, links, half_of, kept, crossed, block_of, landed):
+        self.links, self.kept, self.crossed = links, kept, crossed
+        self.block_of, self.landed = block_of, landed
+        self.placed = False
+        l = links
+        self.own = l.local(half_of(l.x), kept) if half_of else None
+        if half_of:
+            self.cross = l.copy(half_of(1 - l.x), crossed, dx=1)
+
+    def deal(self):
+        l = self.links
+        if self.own is not None:
+            self.own.wait()
+        self.cross.wait_recv()
+        kept, crossed = self.kept, self.crossed
+        lines = kept.shape[0]
+        step = min(128, lines)
+
+        def add(i, carry):
+            at = pl.ds(pl.multiple_of(i * step, step), step)
+            kept[at] = (kept[at].astype(jnp.float32) + crossed[at].astype(jnp.float32)).astype(
+                jnp.bfloat16
+            )
+            return carry
+
+        lax.fori_loop(0, lines // step, add, 0)
+        self.dealt = []
+        for dh in range(2):
+            for dl in range(SQUARE):
+                if dh or dl:
+                    block = self.block_of((l.high + dh) % 2, (l.low + dl) % SQUARE)
+                    self.dealt.append(
+                        l.copy(block, self.landed.at[l.high, l.low], dh=dh, dl=dl)
+                    )
+        mine = self.block_of(l.high, l.low)
+        self.mine = l.local(mine, self.landed.at[l.high, l.low])
+
+    def sum(self, stage, out_of):
+        l = self.links
+        if not self.placed:
+            self.mine.wait()
+        arrived(self.dealt)
+        stores = []
+        landed = self.landed
+        for j in range(SQUARE):
+            if j >= 2:
+                stores[j - 2].wait()
+            stage[j % 2] = landed[0, j].astype(jnp.float32) + landed[1, j].astype(jnp.float32)
+            stores.append(l.local(stage.at[j % 2], out_of(j)))
+        return stores[2:]
+
+
+def back_kernel(
+    sizes,
+    ends,
+    x_in,
+    g_in,
+    residual_in,
+    gain_in,
+    normed_two_part,
+    layer_part,
+    dwg_in,
+    dwu_in,
+    dwd_in,
+    qkv_in,
+    wo_in,
+    normed_one_in,
+    q_in,
+    kv_in,
+    attn_in,
+    cos_in,
+    sin_in,
+    layer_out,
+    input_out,
+    dqkv_out,
+    dwo_out,
+    dwg_out,
+    dwu_out,
+    dwd_out,
+    gains_out,
+    kept_g,
+    kept_d,
+    cross_g,
+    cross_d,
+    land_g,
+    land_u,
+    land_d,
+    kept_q,
+    cross_q,
+    land_q,
+    kept_o,
+    cross_o,
+    land_o,
+    send_q,
+    send_o,
+    stage_q,
+    stage_o,
+    stage,
+    stage_d,
+    own_a,
+    recv_core,
+    recv_block,
+    recv_block_b,
+    both,
+    both_b,
+    x_own,
+    g_own,
+    residual,
+    gain_rows,
+    low_all,
+    wqkv,
+    wo,
+    q,
+    kv,
+    attn,
+    attn_grad,
+    dkv,
+    dkv_send,
+    dkv_recv,
+    dqkv,
+    cos,
+    sin,
+    gain_send,
+    gain_recv,
+    out_low,
+    gain_sum,
+    send_sem,
+    recv_sem,
+    local_sem,
+):
+    rows, local, model, high_size = sizes
+    own = rows * local
+    tokens = SQUARE * own
+    half = model // 2
+    block = x_own.shape[1] // 16
+    heads = q.shape[2] // HD
+    span = SQUARE * local
+    keys = high_size * span
+    f32, b16 = jnp.float32, jnp.bfloat16
+    l = Links(send_sem, recv_sem, local_sem, high_size)
+    steps = [
+        dict(dx=dx, dh=dh, dl=dl)
+        for dx in range(2)
+        for dh in range(2)
+        for dl in range(SQUARE)
+        if dx or dh or dl
+    ]
+    l.greet(steps + [dict(dc=1)])
+
+    def side_of(ref, side):
+        return ref.at[:, pl.ds(pl.multiple_of(side * half, half), half)]
+
+    def row_half(ref):
+        return lambda x: ref.at[pl.ds(pl.multiple_of(x * half, half), half)]
+
+    def row_block(ref):
+        def at(h, low):
+            start = pl.multiple_of((h * SQUARE + low) * block, block)
+            return ref.at[pl.ds(start, block)]
+
+        return at
+
+    def column_block(ref):
+        def at(h, low):
+            start = pl.multiple_of((h * SQUARE + low) * block, block)
+            return ref.at[:, pl.ds(start, block)]
+
+        return at
+
+    def block_at(j):
+        return pl.ds(pl.multiple_of(j * own, own), own)
+
+    def part_at(ref, j, side):
+        return ref.at[block_at(j), pl.ds(pl.multiple_of(side * half, half), half)]
+
+    handed = [
+        l.copy(part_at(normed_two_part, j, 1 - l.core), recv_core.at[j], dc=1)
+        for j in range(SQUARE)
+    ]
+    owned = [l.local(part_at(normed_two_part, j, l.core), own_a.at[j]) for j in range(SQUARE)]
+    loads = [
+        l.local(residual_in, residual),
+        l.local(gain_in, gain_rows),
+        l.local(g_in, g_own),
+    ]
+    grad_d = Grad(l, lambda x: side_of(dwd_in, x), kept_d, cross_d, column_block(kept_d), land_d)
+    grad_g = Grad(l, row_half(dwg_in), kept_g, cross_g, row_block(kept_g), land_g)
+    later = [
+        l.local(x_in, x_own),
+        l.local(wo_in, wo),
+        l.local(attn_in, attn),
+        l.local(q_in, q),
+        l.local(kv_in, kv),
+        l.local(qkv_in, wqkv),
+        l.local(cos_in, cos),
+        l.local(sin_in, sin),
+    ]
+
+    def own_part(j):
+        return own_a[j].astype(f32)
+
+    def push_blocks(part, recv_b):
+        pushed = []
+        for dl in range(1, SQUARE):
+            j = (l.low + dl) % SQUARE
+            total = part(j) + recv_core[j].astype(f32)
+            own_a[j] = total.astype(b16)
+            pushed.append(l.copy(own_a.at[j], recv_b.at[dl - 1], dl=dl))
+        return pushed
+
+    def settle_block(part, recv_b, pushed, into):
+        total = part(l.low) + recv_core[l.low].astype(f32)
+        for dl in range(1, SQUARE):
+            pushed[dl - 1].wait_recv()
+            total = total + recv_b[dl - 1].astype(f32)
+        into[l.core] = total.astype(b16)
+        return l.copy(into.at[l.core], into.at[l.core], dc=1)
+
+    def norm_back(value_of, gain_row, grads):
+        squares = jnp.zeros((own, 1), f32)
+        inner = jnp.zeros((own, 1), f32)
+        for side in range(2):
+            at = slice(side * half, (side + 1) * half)
+            value = value_of(side)
+            squares = squares + jnp.sum(value * value, axis=1, keepdims=True)
+            weighted = grads[side].astype(f32) * gain_rows[gain_row : gain_row + 1, at]
+            inner = inner + jnp.sum(weighted * value, axis=1, keepdims=True)
+        scale = lax.rsqrt(squares / model + EPSILON)
+        pull = scale * scale * scale * (inner / model)
+        outs = []
+        for side in range(2):
+            at = slice(side * half, (side + 1) * half)
+            value = value_of(side)
+            grad = grads[side].astype(f32)
+            summed = jnp.sum(grad * (value * scale), axis=0, keepdims=True)
+            for b in range(half // block):
+                gain_send[gain_row, side * (half // block) + b, 0:1] = summed[
+                    :, b * block : (b + 1) * block
+                ]
+            weighted = grad * gain_rows[gain_row : gain_row + 1, at]
+            outs.append(weighted * scale - value * pull)
+        return outs
+
+    def push_gains(gain_row):
+        me = (l.x * 2 + l.high) * SQUARE + l.low
+        made = []
+        for step in steps:
+            to = ((l.x + step["dx"]) % 2 * 2 + (l.high + step["dh"]) % 2) * SQUARE + (
+                l.low + step["dl"]
+            ) % SQUARE
+            made.append(l.copy(gain_send.at[gain_row, to], gain_recv.at[gain_row, me], **step))
+        return made, l.local(gain_send.at[gain_row, me], gain_recv.at[gain_row, me])
+
+    for made in owned:
+        made.wait()
+    arrived(handed)
+
+    pushed = push_blocks(own_part, recv_block)
+    for made in loads:
+        made.wait()
+    swapped = settle_block(own_part, recv_block, pushed, both)
+    swapped.wait_recv()
+    l.left(pushed + [swapped])
+    outs = norm_back(
+        lambda side: residual[:, side * half : (side + 1) * half], 1, [both[0], both[1]]
+    )
+    for side in range(2):
+        at = slice(side * half, (side + 1) * half)
+        value = g_own[:, at].astype(f32) + outs[side]
+        residual[:, at] = value
+        low_all[side, block_at(l.low)] = value.astype(b16)
+
+    def low_spot(side, low):
+        return low_all.at[side, block_at(low)]
+
+    low_pushed = gather_rows(l, low_spot, 0, low_spot(l.core, l.low))
+    ffn_gains = push_gains(1)
+    handed_b = [
+        l.copy(part_at(layer_part, j, 1 - l.core), recv_core.at[j], dc=1) for j in range(SQUARE)
+    ]
+    owned = [l.local(part_at(layer_part, j, l.core), own_a.at[j]) for j in range(SQUARE)]
+    for made in later:
+        made.wait()
+    low_handed = gather_across(l, low_spot, low_pushed)
+    grad_d.deal()
+    arrived(low_handed)
+
+    def out_grad_step(j, carry):
+        at = block_at(j)
+        rows_at = attn[at].astype(b16)
+        low_out = dot(low_all[0, at], wo[0], ((1,), (1,)))
+        low_out = (low_out + dot(low_all[1, at], wo[1], ((1,), (1,)))).astype(b16)
+        for r in range(rows):
+            spot = pl.ds(pl.multiple_of(j * local, local), local)
+            attn_grad[r, spot] = low_out[r * local : (r + 1) * local]
+        out_low[at] = rows_at
+        return carry
+
+    lax.fori_loop(0, SQUARE, out_grad_step, 0)
+    send_o[...] = dot(out_low[...], low_all[1 - l.x], ((0,), (0,))).astype(b16)
+    grad_o = Grad(l, None, kept_o, cross_o, column_block(kept_o), land_o)
+    grad_o.cross = l.copy(send_o, cross_o, dx=1)
+    kept_o[...] = dot(out_low[...], low_all[l.x], ((0,), (0,))).astype(b16)
+
+    for made in owned:
+        made.wait()
+    arrived(handed_b)
+    pushed_b = push_blocks(own_part, recv_block_b)
+
+    def attend_row(r, carry):
+        allowed = allowed_keys(l, ends, r, span, keys)
+        kv_row = kv[:, r].reshape(keys, 2 * HD)
+        k, v = kv_row[:, :HD], kv_row[:, HD:]
+        q_row, go_row = q[r], attn_grad[r]
+        out_row = jnp.concatenate(
+            [
+                attn[pl.ds(pl.multiple_of(j * own + r * local, local), local)]
+                for j in range(SQUARE)
+            ],
+            axis=0,
+        )
+        grads = []
+        dk = jnp.zeros((keys, HD), f32)
+        dv = jnp.zeros((keys, HD), f32)
+        for head in range(heads):
+            at = slice(head * HD, (head + 1) * HD)
+            qh, go = q_row[:, at], go_row[:, at]
+            delta = jnp.sum(go.astype(f32) * out_row[:, at], axis=1, keepdims=True)
+            score = jnp.where(allowed, dot(qh, k, ((1,), (1,))), MASKED)
+            top = jnp.max(score, axis=1, keepdims=True)
+            grown = jnp.exp(score - top)
+            probs = grown * (1.0 / jnp.sum(grown, axis=1, keepdims=True))
+            dv = dv + dot(probs.astype(b16), go, ((0,), (0,)))
+            pull = dot(go, v, ((1,), (1,)))
+            score_grad = (probs * (pull - delta)).astype(b16)
+            grads.append(dot(score_grad, k) * HD ** (-0.5))
+            dk = dk + dot(score_grad, qh, ((0,), (0,)))
+        turned = jnp.concatenate(grads, axis=1)
+        for j in range(SQUARE):
+            at = pl.ds(pl.multiple_of(j * own + r * local, local), local)
+            value = turned[j * local : (j + 1) * local]
+            cos_q = jnp.concatenate([cos[at, : 2 * HD]] * (heads // 2), axis=1)
+            sin_q = jnp.concatenate([sin[at, : 2 * HD]] * (heads // 2), axis=1)
+            dqkv[at, : heads * HD] = (value * cos_q - roll_heads(value) * sin_q).astype(b16)
+        both_kv = jnp.concatenate([dk, dv], axis=1)
+        for part in range(high_size):
+            dkv[part, r] = both_kv[part * span : (part + 1) * span]
+        return carry
+
+    lax.fori_loop(0, 1, attend_row, 0)
+    grad_g.deal()
+    lax.fori_loop(1, rows, attend_row, 0)
+    dkv_send[...] = dkv[1 - l.high].astype(b16)
+    dkv_copy = l.copy(dkv_send, dkv_recv, dh=1)
+    l.left(low_pushed + low_handed)
+    normed = l.local(normed_one_in.at[:, pl.ds(0, half)], low_all.at[0])
+    normed_2 = l.local(normed_one_in.at[:, pl.ds(half, half)], low_all.at[1])
+    grad_o.deal()
+    l.left(grad_d.dealt)
+    grad_d.mine.wait()
+    grad_d.placed = True
+    grad_u = Grad(l, row_half(dwu_in), kept_d, cross_d, row_block(kept_d), land_u)
+    both_b_copy = settle_block(own_part, recv_block_b, pushed_b, both_b)
+    dkv_copy.wait_recv()
+
+    def unrotate_step(i, carry):
+        at = pl.ds(pl.multiple_of(i * local, local), local)
+        spot = pl.ds(pl.multiple_of((i // rows) * local, local), local)
+        kv_sum = dkv[l.high, i % rows, spot] + dkv_recv[i % rows, spot].astype(f32)
+        turned = kv_sum * cos[at, 2 * HD :] - roll_heads(kv_sum) * sin[at, 2 * HD :]
+        dqkv[at, heads * HD :] = turned.astype(b16)
+        return carry
+
+    lax.fori_loop(0, SQUARE * rows, unrotate_step, 0)
+
+    def project_back(j, side):
+        weight = wqkv[pl.ds(pl.multiple_of(side * half, half), half)]
+        return dot(dqkv[block_at(j)], weight, ((1,), (1,)))
+
+    both_b_copy.wait_recv()
+    l.left(pushed_b)
+    handed = []
+    for j in range(SQUARE):
+        own_a[j] = project_back(j, 1 - l.core).astype(b16)
+        handed.append(l.copy(own_a.at[j], recv_core.at[j], dc=1))
+    normed.wait()
+    normed_2.wait()
+    send_q[...] = dot(low_all[1 - l.x], dqkv[...], ((0,), (0,))).astype(b16)
+    arrived(handed)
+
+    def own_part_c(j):
+        return project_back(j, l.core)
+
+    l.left(handed)
+    pushed = push_blocks(own_part_c, recv_block)
+    grad_q = Grad(l, None, kept_q, cross_q, row_block(kept_q), land_q)
+    grad_q.cross = l.copy(send_q, cross_q, dx=1)
+    kept_q[...] = dot(low_all[l.x], dqkv[...], ((0,), (0,))).astype(b16)
+    settle_block(own_part_c, recv_block, pushed, both).wait_recv()
+    outs = norm_back(
+        lambda side: x_own[:, side * half : (side + 1) * half].astype(f32),
+        0,
+        [both[0], both[1]],
+    )
+    attn_gains = push_gains(0)
+    for side in range(2):
+        at = slice(side * half, (side + 1) * half)
+        x_own[:, at] = (residual[:, at] + outs[side]).astype(b16)
+    stores = [l.local(x_own, input_out)]
+    residual_load = l.local(residual_in, residual)
+    grad_q.deal()
+    grad_u.deal()
+
+    def wide(out, width):
+        return lambda j: out.at[:, pl.ds(j * width, width)]
+
+    def tall(out, lines):
+        return lambda j: out.at[pl.ds(j * lines, lines)]
+
+    def flush(made):
+        for one in made:
+            one.wait()
+
+    residual_load.wait()
+    for side in range(2):
+        at = slice(side * half, (side + 1) * half)
+        g_own[:, at] = (residual[:, at] + both_b[side].astype(f32)).astype(b16)
+    stores.append(l.local(g_own, layer_out))
+    stores += grad_d.sum(stage_d, tall(dwd_out, stage_d.shape[1]))
+    stores += grad_o.sum(stage_o, tall(dwo_out, stage_o.shape[1]))
+    done_g = grad_g.sum(stage, wide(dwg_out, stage.shape[2]))
+    stores += grad_q.sum(stage_q, lambda j: dqkv_out.at[j])
+    for made, kept in (ffn_gains, attn_gains):
+        arrived(made)
+        kept.wait()
+    for row in range(2):
+        total = jnp.zeros((8, block), f32)
+        for b in range(16):
+            total = total + gain_recv[row, b]
+        gain_sum[row : row + 1] = total[0:1]
+    stores.append(l.local(gain_sum, gains_out))
+    flush(done_g)
+    stores += grad_u.sum(stage, wide(dwu_out, stage.shape[2]))
+    flush(stores)
+    l.finish()
+
+
+def back(sizes, ends, *arrays):
+    rows, local, model, high_size = sizes
+    own = rows * local
+    tokens = SQUARE * own
+    half = model // 2
+    block = model // 16
+    ff = arrays[6].shape[1]
+    width = arrays[9].shape[1]
+    wide = width - 2 * HD
+    span = SQUARE * local
+    b16, f32 = jnp.bfloat16, jnp.float32
+    shape = jax.ShapeDtypeStruct
+    vmem = pltpu.VMEM
+    outs = (
+        shape((own, model), b16),
+        shape((own, model), b16),
+        shape((SQUARE, block, width), f32),
+        shape((SQUARE * wide, block), f32),
+        shape((block, SQUARE * ff), f32),
+        shape((block, SQUARE * ff), f32),
+        shape((SQUARE * ff, block), f32),
+        shape((8, block), f32),
+    )
+    anywhere = pl.BlockSpec(memory_space=pl.ANY)
+    scratch = [
+        vmem((half, ff), b16),
+        vmem((ff, half), b16),
+        vmem((half, ff), b16),
+        vmem((ff, half), b16),
+        vmem((2, SQUARE, block, ff), b16),
+        vmem((2, SQUARE, block, ff), b16),
+        vmem((2, SQUARE, ff, block), b16),
+        vmem((half, width), b16),
+        vmem((half, width), b16),
+        vmem((2, SQUARE, block, width), b16),
+        vmem((wide, half), b16),
+        vmem((wide, half), b16),
+        vmem((2, SQUARE, wide, block), b16),
+        vmem((half, width), b16),
+        vmem((wide, half), b16),
+        vmem((2, block, width), f32),
+        vmem((2, wide, block), f32),
+        vmem((2, block, ff), f32),
+        vmem((2, ff, block), f32),
+        vmem((SQUARE, own, half), b16),
+        vmem((SQUARE, own, half), b16),
+        vmem((SQUARE - 1, own, half), b16),
+        vmem((SQUARE - 1, own, half), b16),
+        vmem((2, own, half), b16),
+        vmem((2, own, half), b16),
+        vmem((own, model), b16),
+        vmem((own, model), b16),
+        vmem((own, model), f32),
+        vmem((8, model), f32),
+        vmem((2, tokens, half), b16),
+        vmem((model, width), b16),
+        vmem((2, wide, half), b16),
+        vmem((rows, span, wide), b16),
+        vmem((high_size, rows, span, 2 * HD), b16),
+        vmem((tokens, wide), f32),
+        vmem((rows, span, wide), b16),
+        vmem((high_size, rows, span, 2 * HD), f32),
+        vmem((rows, span, 2 * HD), b16),
+        vmem((rows, span, 2 * HD), b16),
+        vmem((tokens, width), b16),
+        vmem((tokens, 4 * HD), f32),
+        vmem((tokens, 4 * HD), f32),
+        vmem((2, 16, 8, block), f32),
+        vmem((2, 16, 8, block), f32),
+        vmem((tokens, wide), b16),
+        vmem((8, block), f32),
+        pltpu.SemaphoreType.DMA((128,)),
+        pltpu.SemaphoreType.DMA((128,)),
+        pltpu.SemaphoreType.DMA((64,)),
+    ]
+    return pl.pallas_call(
+        functools.partial(back_kernel, sizes),
+        out_shape=outs,
+        in_specs=[pl.BlockSpec(memory_space=pltpu.SMEM)] + [anywhere] * len(arrays),
+        out_specs=[anywhere] * len(outs),
+        scratch_shapes=scratch,
+        compiler_params=pltpu.CompilerParams(
+            collective_id=1, has_side_effects=True, vmem_limit_bytes=VMEM
+        ),
+        name="back",
+    )(ends, *arrays)
+
+
 def norm_back(values, scale, gain, grad):
     weighted = grad * gain
     gain_grad = jnp.sum(grad * values * scale, axis=0)
@@ -303,7 +1289,7 @@
     return (weighted * scale - values * scale**3 * inner, gain_grad)
 
 
-def shards(
+def shards_exchanged(
     hidden_in,
     doc_lengths,
     attn_gain,
@@ -435,6 +1421,158 @@
     )
 
 
+def shards(
+    hidden_in,
+    doc_lengths,
+    attn_gain,
+    query_weight,
+    key_weight,
+    value_weight,
+    output_weight,
+    ffn_gain,
+    gate_weight,
+    up_weight,
+    down_weight,
+    out_grad,
+):
+    rows, local, model = hidden_in.shape
+    tokens = rows * local
+    seq = lax.axis_index("seq")
+    high = seq // SQUARE
+    high_size = lax.axis_size("seq") // SQUARE
+    block = query_weight.shape[0]
+    if block % 128 or high_size != 2 or lax.axis_size("dp") != 2:
+        return shards_exchanged(
+            hidden_in,
+            doc_lengths,
+            attn_gain,
+            query_weight,
+            key_weight,
+            value_weight,
+            output_weight,
+            ffn_gain,
+            gate_weight,
+            up_weight,
+            down_weight,
+            out_grad,
+        )
+    group = H // KVH
+    span = SQUARE * local
+    width = (group + 2) * HD
+
+    ends = jnp.cumsum(doc_lengths, axis=-1).astype(jnp.int32)
+    spots = high * span + jnp.arange(span, dtype=jnp.int32).reshape(SQUARE, 1, local)
+    reached = spots[..., None] >= ends[None, :, None, :]
+    begin = jnp.max(jnp.where(reached, ends[None, :, None, :], 0), axis=-1)
+    position = (spots - begin).astype(jnp.float32).reshape(SQUARE * tokens)
+    angles = position[:, None] * inverse_freqs(HD)
+    cos, sin = jnp.cos(angles), jnp.sin(angles)
+    flat = jnp.zeros((SQUARE * tokens, HD), jnp.float32)
+    cos = jnp.concatenate([cos] * 6 + [flat + 1.0], axis=1)
+    sin = jnp.concatenate([-sin, sin] * 3 + [flat], axis=1)
+    qkv_shard = jnp.concatenate(
+        [
+            query_weight.reshape(block, SQUARE, group * HD),
+            key_weight.reshape(block, SQUARE, HD),
+            value_weight.reshape(block, SQUARE, HD),
+        ],
+        axis=2,
+    ).transpose(1, 0, 2)
+    gain_shard = jnp.zeros((1, 16, block), jnp.bfloat16)
+    gain_shard = gain_shard.at[0, 0].set(attn_gain).at[0, 1].set(ffn_gain)
+    own_in = hidden_in.reshape(tokens, model)
+    own_grad = out_grad.reshape(tokens, model)
+    (
+        qkv_own,
+        output_own,
+        gate_own,
+        up_own,
+        down_own,
+        gains,
+        normed_one,
+        queries,
+        kv,
+        attn,
+        residual,
+        normed_two,
+        all_grad,
+    ) = front(
+        (rows, local, model, high_size),
+        ends.reshape(-1),
+        own_in,
+        own_grad,
+        qkv_shard,
+        gain_shard,
+        output_weight,
+        gate_weight,
+        up_weight,
+        down_weight,
+        cos,
+        sin,
+    )
+    gate_proj = dot(normed_two, gate_own)
+    up_proj = dot(normed_two, up_own)
+    sigmoid_gate = jax.nn.sigmoid(gate_proj)
+    silu_gate = gate_proj * sigmoid_gate
+    hidden_units = (silu_gate * up_proj).astype(jnp.bfloat16)
+    hidden_grad = dot(all_grad, down_own, ((1,), (1,)))
+    gate_act = (
+        hidden_grad * up_proj * sigmoid_gate * (1.0 + gate_proj * (1.0 - sigmoid_gate))
+    ).astype(jnp.bfloat16)
+    up_act = (hidden_grad * silu_gate).astype(jnp.bfloat16)
+    down_part = dot(hidden_units, all_grad, ((0,), (0,))).astype(jnp.bfloat16)
+    gate_part = dot(normed_two, gate_act, ((0,), (0,))).astype(jnp.bfloat16)
+    up_part = dot(normed_two, up_act, ((0,), (0,))).astype(jnp.bfloat16)
+    normed_two_part = dot(gate_act, gate_own, ((1,), (1,))) + dot(up_act, up_own, ((1,), (1,)))
+    layer_part = dot(hidden_units, down_own).astype(jnp.bfloat16)
+    (
+        layer_out,
+        input_grad,
+        qkv_grad,
+        output_grad,
+        gate_grad,
+        up_grad,
+        down_grad,
+        gain_grads,
+    ) = back(
+        (rows, local, model, high_size),
+        ends.reshape(-1),
+        own_in,
+        own_grad,
+        residual,
+        gains,
+        normed_two_part.astype(jnp.bfloat16),
+        layer_part,
+        gate_part,
+        up_part,
+        down_part,
+        qkv_own,
+        output_own,
+        normed_one,
+        queries,
+        kv,
+        attn,
+        cos,
+        sin,
+    )
+    query_grad = qkv_grad[..., : group * HD].transpose(1, 0, 2).reshape(block, -1)
+    key_grad = qkv_grad[..., group * HD : (group + 1) * HD].transpose(1, 0, 2).reshape(block, -1)
+    value_grad = qkv_grad[..., (group + 1) * HD :].transpose(1, 0, 2).reshape(block, -1)
+    return (
+        layer_out.reshape(hidden_in.shape),
+        input_grad.reshape(hidden_in.shape),
+        gain_grads[0],
+        query_grad,
+        key_grad,
+        value_grad,
+        output_grad,
+        gain_grads[1],
+        gate_grad,
+        up_grad,
+        down_grad,
+    )
+
+
 def solution(mesh):
     return jax.shard_map(
         shards,

time: 1150 us -> 698 us (0.61)
  waiting for transfers between devices: 596 us -> 0 us
  Pallas kernels: 29.1 us -> 589 us
  starting transfers between devices: 130 us -> 0 us
  local copies, waits for them, and re-layouts: 134 us -> 30.4 us
  other arithmetic: 79.3 us -> 3.75 us
  blocking collectives: 53 us -> 0 us
  matrix products: 103 us -> 67 us
  between operations: 16.8 us -> 1.25 us
    pallas_call x2, Pallas kernels: 29.1 us -> 589 us  [the longest x1 302 us: front(): pl.pallas_call(functools.partial(front_kernel, sizes), out_shape=outs, in...]
    ppermute x115 -> x0, waiting for transfers between devices: 523 us -> none  [swap(): return lax.ppermute(value, axis, [(i, i ^ mask) for i in range(size)])]
    ppermute x115 -> x0, starting transfers between devices: 130 us -> none  [swap(): return lax.ppermute(value, axis, [(i, i ^ mask) for i in range(size)])]
    unnamed x2 -> x0, waiting for transfers between devices: 72.9 us -> none
    all_gather x1 -> x0, blocking collectives: 53 us -> none  [shards(): lax.all_gather(jnp.stack([attn_gain, ffn_gain]), ('dp', 'seq'), axis=1, t...]
    dot_general x21 -> x9, matrix products: 103 us -> 67 us  [dot(): lax.dot_general(left, right, (dims, ((), ())), preferred_element_type=jnp...]
    dynamic_update_slice x62 -> x0, local copies, waits for them, and re-layouts: 35.4 us -> none  [put(): return lax.dynamic_update_slice_in_dim(whole, part, start, axis)]
    convert_element_type x14 -> x1, other arithmetic: 24.2 us -> 0.01 us  [shards(): position = (spots - begin).astype(jnp.float32).reshape(SQUARE * tokens)]
  transfers between devices with their start and end apart: 116 -> 0, of which waited for: 58 -> 0; matrix products, arithmetic and copies ran while one was open for 15% -> 0% of each run, Pallas kernels for 0% -> 0%
where the time goes in v2:
time: 698 us; the launch traced here: 691 us
  Pallas kernels  589 us (84%)
  matrix products  67 us (10%)
  local copies, waits for them, and re-layouts  30.4 us (4%)
    pallas_call x1, Pallas kernels, front(): pl.pallas_call(functools.partial(front_kernel, sizes), out_shape=outs, in...  302 us
    pallas_call x1, Pallas kernels, back(): pl.pallas_call(functools.partial(back_kernel, sizes), out_shape=outs, in_...  287 us
    dot_general x9, matrix products, dot(): lax.dot_general(left, right, (dims, ((), ())), preferred_element_type=jnp...  67 us

profile of v2, /device:TPU:0, one launch (start us, length us, event | category | flops | bytes accessed | tf_op | source)
XLA Modules:
  0.0 691.0 jit_solution(8782785974676610306)
XLA Ops:
  0.6 0.9 reduce_window_sum.11
  1.5 0.6 reshape.186.ends
  2.1 0.9 copy.49
  3.0 0.1 copy.52
  3.2 1.0 copy.48
  4.1 0.1 copy.51
  4.3 1.1 copy.47
  5.4 0.2 copy.50
  5.6 0.9 maximum_bitcast_fusion.qkv_in
  6.4 0.7 scatter.6
  7.1 0.6 slice.58
  7.7 1.3 scatter.9.gain_in
  9.0 0.0 copy-start.5
  9.0 0.1 select_reduce_fusion
  9.2 1.9 multiply_sine_fusion
  11.1 3.7 concatenate.15.cos_in
  14.9 3.7 concatenate.16.sin_in
  18.6 0.0 copy-done.5
  18.6 301.7 %front.1 = (bf16[2048,384]{1,0:T(8,128)(2,1)}, bf16[2,256,1024]{2,1,0:T(8,128)(2,1)}, bf16[2048,1024]{1,0:T(8,128)(2,1)}, bf16[2048,1024]{1,0:T(8,128)(2,1)}, bf...) custom-call(s32[8]{0:T(128)} %reshape.186.ends, ...), custom_call_target="tpu_custom_call" | custom-call | tf_op jit(solution)/shard_map/front/pallas_call | solution.py:713
  320.4 0.0 copy-start.6
  320.4 0.0 copy-start.8
  320.4 10.0 %fusion.3 = f32[1024,1024]{1,0:T(8,128)} fusion(bf16[1024,2048]{1,0:T(8,128)(2,1)} %get-tuple-element.60, bf16[2048,1024]{1,0:T(8,128)(2,1)} %get-tuple-element.62), kind=kOutput, calls=%fused_computation.25 | convolution fusion | flops 4294967296 | bytes 12582912 | tf_op jit(solution)/shard_map/dot_general | solution.py:59
  330.4 0.0 copy-done.6
  330.4 0.0 copy-done.8
  330.4 0.0 copy-start.7
  330.4 0.0 copy-start.9
  330.4 6.1 fusion.2
  336.5 0.0 copy-done.7
  336.5 0.0 copy-done.9
  336.5 0.0 copy-start.10
  336.5 9.8 %multiply_convert_fusion = (bf16[1024,1024]{1,0:T(8,128)(2,1)S(1)}, bf16[1024,1024]{1,0:T(8,128)(2,1)S(1)}, bf16[1024,1024]{1,0:T(8,128)(2,1)}) fusion(f32[1024,1024]{1,0:T(8,128)} %fusion.3, f32[1024,1024]{1,0:T(8,128)} %fusion.2, bf16[1024,2048]{1,0:T(8,128)(2,1)S(1)} %copy-done.7, bf16[2048,1024]{1,0:T(8,128)(2,1)S(1)} %copy-done.9), kind=kOutput, calls=%fused_computation.1 | convolution fusion | flops 4310695936 | bytes 23068672 | tf_op jit(solution)/shard_map/dot_general | solution.py:59
  346.3 0.0 copy-done.10
  346.3 7.3 %fusion.4 = f32[1024,2048]{1,0:T(8,128)} fusion(bf16[1024,1024]{1,0:T(8,128)(2,1)S(1)} %get-tuple-element.111, bf16[2048,1024]{1,0:T(8,128)(2,1)S(1)} %copy-done.10), kind=kOutput, calls=%fused_computation.26 | convolution fusion | flops 4294967296 | bytes 14680064 | tf_op jit(solution)/shard_map/dot_general | solution.py:59
  353.6 9.1 %add_convert_fusion.normed_two_part = bf16[1024,2048]{1,0:T(8,128)(2,1)} fusion(f32[1024,2048]{1,0:T(8,128)} %fusion.4, bf16[1024,1024]{1,0:T(8,128)(2,1)} %get-tuple-element.112, bf16[2048,1024]{1,0:T(8,128)(2,1)S(1)} %copy-done.9), kind=kOutput, calls=%fused_computation | convolution fusion | flops 4299161600 | bytes 18874368 | tf_op jit(solution)/shard_map/dot_general | solution.py:59
  362.7 6.0 convolution_convert_fusion.3.layer_part
  368.7 0.0 copy-start.11
  368.7 6.2 convolution_convert_fusion.2.dwg_in
  374.9 0.0 copy-done.11
  374.9 6.2 convolution_convert_fusion.1.dwu_in
  381.1 6.2 convolution_convert_fusion.dwd_in
  387.4 286.9 %back.1 = (bf16[256,2048]{1,0:T(8,128)(2,1)}, bf16[256,2048]{1,0:T(8,128)(2,1)}, f32[4,128,384]{2,1,0:T(8,128)}, f32[1024,128]{1,0:T(8,128)}, f32[128,4096]{1,0:...) custom-call(s32[8]{0:T(128)} %reshape.186.ends, bf16[256,2048]{1,0:T(8,128)(2,1)} %bitcast.45, ...), custom_call_target="tpu_custom_call" | custom-call | tf_op jit(solution)/shard_map/back/pallas_call | solution.py:1272
  674.3 1.3 slice_bitcast_fusion.3
  675.6 1.1 slice_bitcast_fusion
  676.7 0.2 copy.54
  676.9 0.0 copy-start.2
  676.9 1.0 copy.57
  677.9 0.0 copy-start.3
  677.9 1.9 slice_bitcast_fusion.1
  679.8 1.1 copy.55
  680.8 0.8 copy.58
  681.6 0.1 copy.56
  681.7 0.8 copy.59
  682.5 0.0 copy-start.4
  682.5 2.4 copy.67
  684.8 0.0 copy-done.3
  684.8 1.0 copy.68
  685.8 0.0 copy-done.4
  685.8 0.8 copy.69
  686.6 0.0 copy-done.2
  686.6 1.3 copy.70
  687.9 0.0 copy-done.1
  687.9 1.3 copy.71
  689.2 0.0 copy-done
  689.2 1.3 copy.72
  (8 shorter events, 0.1 us)
Async XLA Ops:
  9.0 9.6 %copy-start.5 = (bf16[1,16,128]{2,1,0:T(8,128)(2,1)}, bf16[1,16,128]{2,1,0:T(8,128)(2,1)S(1)}, u32[]{:S(2)}) copy-start(bf16[1,16,128]{2,1,0:T(8,128)(2,1)S(1)} %scatter.9.gain_in) | copy-start | bytes 12292
  320.4 10.1 %copy-start.6 = (bf16[1024,2048]{1,0:T(8,128)(2,1)S(1)}, bf16[1024,2048]{1,0:T(8,128)(2,1)}, u32[]{:S(2)}) copy-start(bf16[1024,2048]{1,0:T(8,128)(2,1)} %get-tuple-element.58) | copy-start | bytes 12582916
  320.4 10.1 %copy-start.8 = (bf16[1024,2048]{1,0:T(8,128)(2,1)S(1)}, bf16[1024,2048]{1,0:T(8,128)(2,1)}, u32[]{:S(2)}) copy-start(bf16[1024,2048]{1,0:T(8,128)(2,1)} %get-tuple-element.59) | copy-start | bytes 12582916
  330.4 6.1 copy-start.7
  330.4 6.1 copy-start.9
  336.5 9.8 %copy-start.10 = (bf16[2048,1024]{1,0:T(8,128)(2,1)S(1)}, bf16[2048,1024]{1,0:T(8,128)(2,1)}, u32[]{:S(2)}) copy-start(bf16[2048,1024]{1,0:T(8,128)(2,1)} %get-tuple-element.62) | copy-start | bytes 12582916
  368.7 6.2 copy-start.11
  676.9 9.7 %copy-start.2 = (f32[128,4096]{1,0:T(8,128)S(1)}, f32[128,4096]{1,0:T(8,128)}, u32[]{:S(2)}) copy-start(f32[128,4096]{1,0:T(8,128)} %get-tuple-element.139) | copy-start | bytes 6291460
  677.9 7.0 %copy-start.3 = (bf16[256,2048]{1,0:T(8,128)(2,1)S(1)}, bf16[256,2048]{1,0:T(8,128)(2,1)}, u32[]{:S(2)}) copy-start(bf16[256,2048]{1,0:T(8,128)(2,1)} %get-tuple-element.70) | copy-start | bytes 3145732
  682.5 3.3 copy-start.4
  684.8 3.1 copy-start.1
  686.6 2.6 copy-start

commit v3 on v2

--- a/solution.py
+++ b/solution.py
@@ -308,8 +308,14 @@
         self.count = self.local_count = 0
         self.sent = []
 
-    def to(self, dx=0, dh=0, dl=0, dc=0):
-        seq = ((self.high + dh) % self.high_size) * SQUARE + (self.low + dl) % SQUARE
+    def beside(self, flip):
+        if flip == 1:
+            return self.low + 1 - 2 * (self.low % 2)
+        return (self.low + 2) % SQUARE if flip == 2 else SQUARE - 1 - self.low
+
+    def to(self, dx=0, dh=0, dl=0, dc=0, flip=0):
+        low = self.beside(flip) if flip else (self.low + dl) % SQUARE
+        seq = ((self.high + dh) % self.high_size) * SQUARE + low
         return ((self.x + dx) % 2, seq, (self.core + dc) % 2)
 
     def copy(self, src, dst, **step):
@@ -389,39 +395,58 @@
         arrived(self.across)
 
 
-def gather_rows(l, everyone, count, half_src):
+def gather_push(l, everyone, source):
     return [
-        l.copy(half_src, everyone(l.core, l.low), dl=dl) for dl in range(1, SQUARE)
+        l.copy(source(part), everyone(l.core, l.low, part), flip=flip)
+        for flip, part in ((1, 0), (2, 1), (1, 1), (2, 0))
     ]
 
 
 def gather_across(l, everyone, pushed):
-    handed = []
-    for dl in range(1, SQUARE):
-        pushed[dl - 1].wait_recv()
-        block = everyone(l.core, (l.low + SQUARE - dl) % SQUARE)
+    handed, corner = [], []
+    for k, (flip, part) in enumerate(((1, 0), (2, 1), (1, 1), (2, 0))):
+        pushed[k].wait_recv()
+        block = everyone(l.core, l.beside(flip), part)
+        if k < 2:
+            corner.append(l.copy(block, block, flip=3 - flip))
         handed.append(l.copy(block, block, dc=1))
-    return handed
-
-
-def reduce_square(l, part, send_core, recv_core, send_block, recv_block, both):
-    handed = []
-    for j in range(SQUARE):
-        send_core[j] = part(j, 1 - l.core).astype(jnp.bfloat16)
-        handed.append(l.copy(send_core.at[j], recv_core.at[j], dc=1))
-    arrived(handed)
-    pushed = []
-    for dl in range(1, SQUARE):
-        j = (l.low + dl) % SQUARE
-        total = part(j, l.core) + recv_core[j].astype(jnp.float32)
-        send_block[dl] = total.astype(jnp.bfloat16)
-        pushed.append(l.copy(send_block.at[dl], recv_block.at[dl], dl=dl))
-    total = part(l.low, l.core) + recv_core[l.low].astype(jnp.float32)
-    for dl in range(1, SQUARE):
-        pushed[dl - 1].wait_recv()
-        total = total + recv_block[dl].astype(jnp.float32)
+    for part in range(2):
+        corner[part].wait_recv()
+        block = everyone(l.core, l.beside(3), part)
+        handed.append(l.copy(block, block, dc=1))
+    return handed, corner
+
+
+def square_push(l, total_of, send, relay, landed):
+    lines = send.shape[1]
+    first, second = pl.ds(0, lines // 2), pl.ds(lines // 2, lines // 2)
+    one, two, corner = (l.beside(flip) for flip in (1, 2, 3))
+    send[corner] = total_of(corner).astype(jnp.bfloat16)
+    made = [
+        l.copy(send.at[corner, first], relay.at[0], flip=1),
+        l.copy(send.at[corner, second], relay.at[1], flip=2),
+    ]
+    send[one] = total_of(one).astype(jnp.bfloat16)
+    made.append(l.copy(send.at[one, first], landed.at[0, first], flip=1))
+    send[two] = total_of(two).astype(jnp.bfloat16)
+    made.append(l.copy(send.at[two, second], landed.at[1, second], flip=2))
+    made[0].wait_recv()
+    value = send[two, first].astype(jnp.float32) + relay[0].astype(jnp.float32)
+    send[two, first] = value.astype(jnp.bfloat16)
+    made.append(l.copy(send.at[two, first], landed.at[1, first], flip=2))
+    made[1].wait_recv()
+    value = send[one, second].astype(jnp.float32) + relay[1].astype(jnp.float32)
+    send[one, second] = value.astype(jnp.bfloat16)
+    made.append(l.copy(send.at[one, second], landed.at[0, second], flip=1))
+    return made
+
+
+def square_settle(l, total_of, made, landed, both):
+    total = total_of(l.low)
+    arrived(made[2:])
+    total = total + landed[0].astype(jnp.float32) + landed[1].astype(jnp.float32)
     both[l.core] = total.astype(jnp.bfloat16)
-    l.copy(both.at[l.core], both.at[l.core], dc=1).wait_recv()
+    return l.copy(both.at[l.core], both.at[l.core], dc=1)
 
 
 def roll_heads(value):
@@ -486,6 +511,7 @@
     recv_core,
     send_block,
     recv_block,
+    relay,
     both,
     residual,
     normed_two,
@@ -536,17 +562,24 @@
     def lines(ref, width):
         return lambda j: ref.at[pl.ds(pl.multiple_of(j * width, width), width)]
 
-    def x_spot(side, low):
-        return x_all.at[side, pl.ds(pl.multiple_of(low * own, own), own)]
-
-    def g_spot(side, low):
-        return g_out.at[
-            pl.ds(pl.multiple_of(low * own, own), own),
-            pl.ds(pl.multiple_of(side * half, half), half),
+    def part_at(low, part):
+        if part is None:
+            return pl.ds(pl.multiple_of(low * own, own), own)
+        return pl.ds(pl.multiple_of(low * own + part * (own // 2), own // 2), own // 2)
+
+    def x_spot(side, low, part=None):
+        return x_all.at[side, part_at(low, part)]
+
+    def g_spot(side, low, part=None):
+        return g_out.at[part_at(low, part), pl.ds(pl.multiple_of(side * half, half), half)]
+
+    def normed_two_spot(side, low, part=None):
+        return normed_two.at[side, part_at(low, part)]
+
+    def own_part_of(ref):
+        return lambda part: ref.at[
+            pl.ds(part * (own // 2), own // 2), pl.ds(pl.multiple_of(l.core * half, half), half)
         ]
-
-    def normed_two_spot(side, low):
-        return normed_two.at[side, pl.ds(pl.multiple_of(low * own, own), own)]
 
     def side_of(ref, side):
         return ref.at[:, pl.ds(pl.multiple_of(side * half, half), half)]
@@ -555,18 +588,17 @@
     loads += [l.local(cos_in, cos), l.local(sin_in, sin)]
     w_gain = Weight(l, lambda j: gain_in.at[pl.ds(0, 1)], block_spot(gains))
     w_qkv = Weight(l, lambda j: qkv_in.at[j], row_spot(wqkv))
-    x_pushed = gather_rows(l, x_spot, 0, side_of(x_in, l.core))
+    x_pushed = gather_push(l, x_spot, own_part_of(x_in))
     w_o = Weight(l, lines(wo_in, wo.shape[1]), half_spot(wo))
     w_gate = Weight(l, columns(wg_in, wg_out.shape[1]), row_spot(wg_out))
 
     w_gain.pass_near()
     w_qkv.pass_near()
+    x_handed, _ = gather_across(l, x_spot, x_pushed)
     w_gain.pass_far()
     w_qkv.pass_far()
-    x_handed = gather_across(l, x_spot, x_pushed)
     w_o.pass_near()
     w_o.pass_far()
-    w_up = Weight(l, columns(wu_in, wu_out.shape[1]), row_spot(wu_out))
     for made in loads:
         made.wait()
     w_gain.wait()
@@ -611,6 +643,7 @@
     kv_copy = l.copy(kv.at[l.high], kv.at[l.high], dh=1)
     stores.append(l.local(q, q_out))
     w_gate.pass_near()
+    w_up = Weight(l, columns(wu_in, wu_out.shape[1]), row_spot(wu_out))
     kv_copy.wait_recv()
     stores.append(l.local(kv, kv_out))
 
@@ -639,7 +672,6 @@
     lax.fori_loop(0, rows, attend_row, 0)
     stores.append(l.local(attn, attn_out))
     w_gate.pass_far()
-    w_down = Weight(l, lines(wd_in, wd_out.shape[0]), column_spot(wd_out))
     w_o.wait()
     stores.append(l.local(wo, wo_out))
 
@@ -647,7 +679,19 @@
         at = pl.ds(pl.multiple_of(j * own, own), own)
         return dot(low_attn[at], wo[side])
 
-    reduce_square(l, project_out, send_core, recv_core, send_block, recv_block, both)
+    handed = []
+    for j in range(SQUARE):
+        send_core[j] = project_out(j, 1 - l.core).astype(jnp.bfloat16)
+        handed.append(l.copy(send_core.at[j], recv_core.at[j], dc=1))
+    arrived(handed)
+
+    def total_out(j):
+        return project_out(j, l.core) + recv_core[j].astype(jnp.float32)
+
+    pushed = square_push(l, total_out, send_block, relay, recv_block)
+    w_up.pass_near()
+    w_down = Weight(l, lines(wd_in, wd_out.shape[0]), column_spot(wd_out))
+    square_settle(l, total_out, pushed, recv_block, both).wait_recv()
     at_own = pl.ds(pl.multiple_of(l.low * own, own), own)
     total = jnp.zeros((own, 1), jnp.float32)
     for side in range(2):
@@ -661,17 +705,18 @@
             jnp.bfloat16
         )
     stores.append(l.local(residual, residual_out))
-    pushed = gather_rows(l, normed_two_spot, 0, normed_two_spot(l.core, l.low))
+    pushed = gather_push(
+        l, normed_two_spot, lambda part: normed_two_spot(l.core, l.low, part)
+    )
     loads = [l.local(side_of(g_in, side), g_spot(side, l.low)) for side in range(2)]
-    g_pushed = gather_rows(l, g_spot, 0, side_of(g_in, l.core))
-    w_up.pass_near()
-    handed = gather_across(l, normed_two_spot, pushed)
+    g_pushed = gather_push(l, g_spot, own_part_of(g_in))
+    w_up.pass_far()
+    handed, _ = gather_across(l, normed_two_spot, pushed)
+    w_down.pass_near()
     arrived(handed)
     for side in range(2):
         stores.append(l.local(normed_two.at[side], side_of(normed_two_out, side)))
-    w_up.pass_far()
-    g_handed = gather_across(l, g_spot, g_pushed)
-    w_down.pass_near()
+    g_handed, _ = gather_across(l, g_spot, g_pushed)
     w_down.pass_far()
     arrived(g_handed)
     for weight in (w_gate, w_up, w_down):
@@ -731,12 +776,13 @@
             vmem((SQUARE, own, half), low),
             vmem((SQUARE, own, half), low),
             vmem((SQUARE, own, half), low),
-            vmem((SQUARE, own, half), low),
+            vmem((2, own, half), low),
+            vmem((2, own // 2, half), low),
             vmem((2, own, half), low),
             vmem((own, model), f32),
             vmem((2, tokens, half), low),
-            pltpu.SemaphoreType.DMA((96,)),
-            pltpu.SemaphoreType.DMA((96,)),
+            pltpu.SemaphoreType.DMA((128,)),
+            pltpu.SemaphoreType.DMA((128,)),
             pltpu.SemaphoreType.DMA((32,)),
         ],
         compiler_params=pltpu.CompilerParams(
@@ -750,7 +796,6 @@
     def __init__(self, links, half_of, kept, crossed, block_of, landed):
         self.links, self.kept, self.crossed = links, kept, crossed
         self.block_of, self.landed = block_of, landed
-        self.placed = False
         l = links
         self.own = l.local(half_of(l.x), kept) if half_of else None
         if half_of:
@@ -779,24 +824,9 @@
                 if dh or dl:
                     block = self.block_of((l.high + dh) % 2, (l.low + dl) % SQUARE)
                     self.dealt.append(
-                        l.copy(block, self.landed.at[l.high, l.low], dh=dh, dl=dl)
+                        l.copy(block, self.landed(l.high, l.low), dh=dh, dl=dl)
                     )
-        mine = self.block_of(l.high, l.low)
-        self.mine = l.local(mine, self.landed.at[l.high, l.low])
-
-    def sum(self, stage, out_of):
-        l = self.links
-        if not self.placed:
-            self.mine.wait()
-        arrived(self.dealt)
-        stores = []
-        landed = self.landed
-        for j in range(SQUARE):
-            if j >= 2:
-                stores[j - 2].wait()
-            stage[j % 2] = landed[0, j].astype(jnp.float32) + landed[1, j].astype(jnp.float32)
-            stores.append(l.local(stage.at[j % 2], out_of(j)))
-        return stores[2:]
+        self.mine = l.local(self.block_of(l.high, l.low), self.landed(l.high, l.low))
 
 
 def back_kernel(
@@ -821,35 +851,30 @@
     sin_in,
     layer_out,
     input_out,
-    dqkv_out,
-    dwo_out,
-    dwg_out,
-    dwu_out,
-    dwd_out,
-    gains_out,
-    kept_g,
-    kept_d,
-    cross_g,
-    cross_d,
+    land_q,
+    land_o,
     land_g,
     land_u,
     land_d,
+    gains_out,
+    kept_g,
+    kept_u,
+    kept_d,
+    cross_g,
+    cross_u,
+    cross_d,
     kept_q,
     cross_q,
-    land_q,
     kept_o,
     cross_o,
-    land_o,
     send_q,
     send_o,
-    stage_q,
-    stage_o,
-    stage,
-    stage_d,
     own_a,
     recv_core,
     recv_block,
+    relay,
     recv_block_b,
+    relay_b,
     both,
     both_b,
     x_own,
@@ -916,6 +941,14 @@
 
         return at
 
+    def tall(ref):
+        lines = ref.shape[1] // SQUARE
+        return lambda h, low: ref.at[h, pl.ds(pl.multiple_of(low * lines, lines), lines)]
+
+    def broad(ref):
+        wide = ref.shape[2] // SQUARE
+        return lambda h, low: ref.at[h, :, pl.ds(pl.multiple_of(low * wide, wide), wide)]
+
     def block_at(j):
         return pl.ds(pl.multiple_of(j * own, own), own)
 
@@ -932,8 +965,9 @@
         l.local(gain_in, gain_rows),
         l.local(g_in, g_own),
     ]
-    grad_d = Grad(l, lambda x: side_of(dwd_in, x), kept_d, cross_d, column_block(kept_d), land_d)
-    grad_g = Grad(l, row_half(dwg_in), kept_g, cross_g, row_block(kept_g), land_g)
+    grad_d = Grad(
+        l, lambda x: side_of(dwd_in, x), kept_d, cross_d, column_block(kept_d), tall(land_d)
+    )
     later = [
         l.local(x_in, x_own),
         l.local(wo_in, wo),
@@ -945,25 +979,8 @@
         l.local(sin_in, sin),
     ]
 
-    def own_part(j):
-        return own_a[j].astype(f32)
-
-    def push_blocks(part, recv_b):
-        pushed = []
-        for dl in range(1, SQUARE):
-            j = (l.low + dl) % SQUARE
-            total = part(j) + recv_core[j].astype(f32)
-            own_a[j] = total.astype(b16)
-            pushed.append(l.copy(own_a.at[j], recv_b.at[dl - 1], dl=dl))
-        return pushed
-
-    def settle_block(part, recv_b, pushed, into):
-        total = part(l.low) + recv_core[l.low].astype(f32)
-        for dl in range(1, SQUARE):
-            pushed[dl - 1].wait_recv()
-            total = total + recv_b[dl - 1].astype(f32)
-        into[l.core] = total.astype(b16)
-        return l.copy(into.at[l.core], into.at[l.core], dc=1)
+    def own_total(j):
+        return own_a[j].astype(f32) + recv_core[j].astype(f32)
 
     def norm_back(value_of, gain_row, grads):
         squares = jnp.zeros((own, 1), f32)
@@ -1004,10 +1021,10 @@
         made.wait()
     arrived(handed)
 
-    pushed = push_blocks(own_part, recv_block)
+    pushed = square_push(l, own_total, own_a, relay, recv_block)
     for made in loads:
         made.wait()
-    swapped = settle_block(own_part, recv_block, pushed, both)
+    swapped = square_settle(l, own_total, pushed, recv_block, both)
     swapped.wait_recv()
     l.left(pushed + [swapped])
     outs = norm_back(
@@ -1019,10 +1036,12 @@
         residual[:, at] = value
         low_all[side, block_at(l.low)] = value.astype(b16)
 
-    def low_spot(side, low):
-        return low_all.at[side, block_at(low)]
-
-    low_pushed = gather_rows(l, low_spot, 0, low_spot(l.core, l.low))
+    def low_spot(side, low, part):
+        start = pl.multiple_of(low * own + part * (own // 2), own // 2)
+        return low_all.at[side, pl.ds(start, own // 2)]
+
+    low_pushed = gather_push(l, low_spot, lambda part: low_spot(l.core, l.low, part))
+    grad_g = Grad(l, row_half(dwg_in), kept_g, cross_g, row_block(kept_g), broad(land_g))
     ffn_gains = push_gains(1)
     handed_b = [
         l.copy(part_at(layer_part, j, 1 - l.core), recv_core.at[j], dc=1) for j in range(SQUARE)
@@ -1030,9 +1049,10 @@
     owned = [l.local(part_at(layer_part, j, l.core), own_a.at[j]) for j in range(SQUARE)]
     for made in later:
         made.wait()
-    low_handed = gather_across(l, low_spot, low_pushed)
+    low_handed, low_corner = gather_across(l, low_spot, low_pushed)
     grad_d.deal()
     arrived(low_handed)
+    grad_u = Grad(l, row_half(dwu_in), kept_u, cross_u, row_block(kept_u), broad(land_u))
 
     def out_grad_step(j, carry):
         at = block_at(j)
@@ -1047,14 +1067,14 @@
 
     lax.fori_loop(0, SQUARE, out_grad_step, 0)
     send_o[...] = dot(out_low[...], low_all[1 - l.x], ((0,), (0,))).astype(b16)
-    grad_o = Grad(l, None, kept_o, cross_o, column_block(kept_o), land_o)
+    grad_o = Grad(l, None, kept_o, cross_o, column_block(kept_o), tall(land_o))
     grad_o.cross = l.copy(send_o, cross_o, dx=1)
     kept_o[...] = dot(out_low[...], low_all[l.x], ((0,), (0,))).astype(b16)
 
     for made in owned:
         made.wait()
     arrived(handed_b)
-    pushed_b = push_blocks(own_part, recv_block_b)
+    pushed_b = square_push(l, own_total, own_a, relay_b, recv_block_b)
 
     def attend_row(r, carry):
         allowed = allowed_keys(l, ends, r, span, keys)
@@ -1101,15 +1121,11 @@
     lax.fori_loop(1, rows, attend_row, 0)
     dkv_send[...] = dkv[1 - l.high].astype(b16)
     dkv_copy = l.copy(dkv_send, dkv_recv, dh=1)
-    l.left(low_pushed + low_handed)
+    l.left(low_pushed + low_handed + low_corner)
     normed = l.local(normed_one_in.at[:, pl.ds(0, half)], low_all.at[0])
     normed_2 = l.local(normed_one_in.at[:, pl.ds(half, half)], low_all.at[1])
     grad_o.deal()
-    l.left(grad_d.dealt)
-    grad_d.mine.wait()
-    grad_d.placed = True
-    grad_u = Grad(l, row_half(dwu_in), kept_d, cross_d, row_block(kept_d), land_u)
-    both_b_copy = settle_block(own_part, recv_block_b, pushed_b, both_b)
+    both_b_copy = square_settle(l, own_total, pushed_b, recv_block_b, both_b)
     dkv_copy.wait_recv()
 
     def unrotate_step(i, carry):
@@ -1137,15 +1153,16 @@
     send_q[...] = dot(low_all[1 - l.x], dqkv[...], ((0,), (0,))).astype(b16)
     arrived(handed)
 
-    def own_part_c(j):
-        return project_back(j, l.core)
+    def own_total_c(j):
+        return project_back(j, l.core) + recv_core[j].astype(f32)
 
     l.left(handed)
-    pushed = push_blocks(own_part_c, recv_block)
-    grad_q = Grad(l, None, kept_q, cross_q, row_block(kept_q), land_q)
+    pushed = square_push(l, own_total_c, own_a, relay, recv_block)
+    grad_q = Grad(l, None, kept_q, cross_q, row_block(kept_q), lambda h, low: land_q.at[h, low])
     grad_q.cross = l.copy(send_q, cross_q, dx=1)
     kept_q[...] = dot(low_all[l.x], dqkv[...], ((0,), (0,))).astype(b16)
-    settle_block(own_part_c, recv_block, pushed, both).wait_recv()
+    grad_u.deal()
+    square_settle(l, own_total_c, pushed, recv_block, both).wait_recv()
     outs = norm_back(
         lambda side: x_own[:, side * half : (side + 1) * half].astype(f32),
         0,
@@ -1158,27 +1175,11 @@
     stores = [l.local(x_own, input_out)]
     residual_load = l.local(residual_in, residual)
     grad_q.deal()
-    grad_u.deal()
-
-    def wide(out, width):
-        return lambda j: out.at[:, pl.ds(j * width, width)]
-
-    def tall(out, lines):
-        return lambda j: out.at[pl.ds(j * lines, lines)]
-
-    def flush(made):
-        for one in made:
-            one.wait()
-
     residual_load.wait()
     for side in range(2):
         at = slice(side * half, (side + 1) * half)
         g_own[:, at] = (residual[:, at] + both_b[side].astype(f32)).astype(b16)
     stores.append(l.local(g_own, layer_out))
-    stores += grad_d.sum(stage_d, tall(dwd_out, stage_d.shape[1]))
-    stores += grad_o.sum(stage_o, tall(dwo_out, stage_o.shape[1]))
-    done_g = grad_g.sum(stage, wide(dwg_out, stage.shape[2]))
-    stores += grad_q.sum(stage_q, lambda j: dqkv_out.at[j])
     for made, kept in (ffn_gains, attn_gains):
         arrived(made)
         kept.wait()
@@ -1188,9 +1189,11 @@
             total = total + gain_recv[row, b]
         gain_sum[row : row + 1] = total[0:1]
     stores.append(l.local(gain_sum, gains_out))
-    flush(done_g)
-    stores += grad_u.sum(stage, wide(dwu_out, stage.shape[2]))
-    flush(stores)
+    for grad in (grad_d, grad_o, grad_g, grad_u, grad_q):
+        grad.mine.wait()
+        arrived(grad.dealt)
+    for made in stores:
+        made.wait()
     l.finish()
 
 
@@ -1210,38 +1213,33 @@
     outs = (
         shape((own, model), b16),
         shape((own, model), b16),
-        shape((SQUARE, block, width), f32),
-        shape((SQUARE * wide, block), f32),
-        shape((block, SQUARE * ff), f32),
-        shape((block, SQUARE * ff), f32),
-        shape((SQUARE * ff, block), f32),
+        shape((2, SQUARE, block, width), b16),
+        shape((2, SQUARE * wide, block), b16),
+        shape((2, block, SQUARE * ff), b16),
+        shape((2, block, SQUARE * ff), b16),
+        shape((2, SQUARE * ff, block), b16),
         shape((8, block), f32),
     )
     anywhere = pl.BlockSpec(memory_space=pl.ANY)
     scratch = [
         vmem((half, ff), b16),
+        vmem((half, ff), b16),
         vmem((ff, half), b16),
         vmem((half, ff), b16),
+        vmem((half, ff), b16),
         vmem((ff, half), b16),
-        vmem((2, SQUARE, block, ff), b16),
-        vmem((2, SQUARE, block, ff), b16),
-        vmem((2, SQUARE, ff, block), b16),
         vmem((half, width), b16),
         vmem((half, width), b16),
-        vmem((2, SQUARE, block, width), b16),
         vmem((wide, half), b16),
         vmem((wide, half), b16),
-        vmem((2, SQUARE, wide, block), b16),
         vmem((half, width), b16),
         vmem((wide, half), b16),
-        vmem((2, block, width), f32),
-        vmem((2, wide, block), f32),
-        vmem((2, block, ff), f32),
-        vmem((2, ff, block), f32),
         vmem((SQUARE, own, half), b16),
         vmem((SQUARE, own, half), b16),
-        vmem((SQUARE - 1, own, half), b16),
-        vmem((SQUARE - 1, own, half), b16),
+        vmem((2, own, half), b16),
+        vmem((2, own // 2, half), b16),
+        vmem((2, own, half), b16),
+        vmem((2, own // 2, half), b16),
         vmem((2, own, half), b16),
         vmem((2, own, half), b16),
         vmem((own, model), b16),
@@ -1528,11 +1526,7 @@
     (
         layer_out,
         input_grad,
-        qkv_grad,
-        output_grad,
-        gate_grad,
-        up_grad,
-        down_grad,
+        *landed,
         gain_grads,
     ) = back(
         (rows, local, model, high_size),
@@ -1554,6 +1548,9 @@
         attn,
         cos,
         sin,
+    )
+    qkv_grad, output_grad, gate_grad, up_grad, down_grad = (
+        part[0].astype(jnp.float32) + part[1].astype(jnp.float32) for part in landed
     )
     query_grad = qkv_grad[..., : group * HD].transpose(1, 0, 2).reshape(block, -1)
     key_grad = qkv_grad[..., group * HD : (group + 1) * HD].transpose(1, 0, 2).reshape(block, -1)

time: 698 us -> 628 us (0.90)
  Pallas kernels: 589 us -> 520 us
  local copies, waits for them, and re-layouts: 30.4 us -> 20.5 us
  other arithmetic: 3.75 us -> 12.7 us
    pallas_call x1, Pallas kernels: 302 us -> 263 us  [front(): pl.pallas_call(functools.partial(front_kernel, sizes), out_shape=outs, in...]
    pallas_call x1, Pallas kernels: 287 us -> 257 us  [back(): pl.pallas_call(functools.partial(back_kernel, sizes), out_shape=outs, in_...]
    add x0 -> x4, other arithmetic: none -> 8.99 us  [shards(): part[0].astype(jnp.float32) + part[1].astype(jnp.float32)]
where the time goes in v3:
time: 628 us; the launch traced here: 621 us
  Pallas kernels  520 us (83%)
  matrix products  66.7 us (11%)
  local copies, waits for them, and re-layouts  20.5 us (3%)
  other arithmetic  12.7 us (2%)
    pallas_call x1, Pallas kernels, front(): pl.pallas_call(functools.partial(front_kernel, sizes), out_shape=outs, in...  263 us
    pallas_call x1, Pallas kernels, back(): pl.pallas_call(functools.partial(back_kernel, sizes), out_shape=outs, in_...  257 us
    dot_general x9, matrix products, dot(): lax.dot_general(left, right, (dims, ((), ())), preferred_element_type=jnp...  66.7 us

profile of v3, /device:TPU:0, one launch (start us, length us, event | category | flops | bytes accessed | tf_op | source)
XLA Modules:
  0.0 621.0 jit_solution(15381045290487366123)
XLA Ops:
  0.6 0.9 reduce_window_sum.11
  1.5 0.6 reshape.201.ends
  2.1 0.9 copy.49
  3.0 0.1 copy.52
  3.2 1.0 copy.48
  4.1 0.1 copy.51
  4.3 1.1 copy.47
  5.4 0.1 copy.50
  5.6 0.9 maximum_bitcast_fusion.qkv_in
  6.4 0.7 scatter.6
  7.1 0.6 slice.88
  7.7 1.3 scatter.9.gain_in
  9.0 0.0 copy-start.4
  9.0 0.1 select_reduce_fusion
  9.1 1.9 multiply_sine_fusion
  11.1 3.7 concatenate.15.cos_in
  14.9 3.7 concatenate.16.sin_in
  18.6 0.0 copy-done.4
  18.6 263.0 %front.1 = (bf16[2048,384]{1,0:T(8,128)(2,1)}, bf16[2,256,1024]{2,1,0:T(8,128)(2,1)}, bf16[2048,1024]{1,0:T(8,128)(2,1)}, bf16[2048,1024]{1,0:T(8,128)(2,1)}, bf...) custom-call(s32[8]{0:T(128)} %reshape.201.ends, ...), custom_call_target="tpu_custom_call" | custom-call | tf_op jit(solution)/shard_map/front/pallas_call | solution.py:758
  281.6 0.0 copy-start.5
  281.6 0.0 copy-start.7
  281.6 10.0 %fusion.3 = f32[1024,1024]{1,0:T(8,128)} fusion(bf16[1024,2048]{1,0:T(8,128)(2,1)} %get-tuple-element.60, bf16[2048,1024]{1,0:T(8,128)(2,1)} %get-tuple-element.62), kind=kOutput, calls=%fused_computation.30 | convolution fusion | flops 4294967296 | bytes 12582912 | tf_op jit(solution)/shard_map/dot_general | solution.py:59
  291.7 0.0 copy-done.5
  291.7 0.0 copy-done.7
  291.7 0.0 copy-start.6
  291.7 0.0 copy-start.8
  291.7 6.1 fusion.2
  297.8 0.0 copy-done.6
  297.8 0.0 copy-done.8
  297.8 0.0 copy-start.9
  297.8 9.8 %multiply_convert_fusion = (bf16[1024,1024]{1,0:T(8,128)(2,1)S(1)}, bf16[1024,1024]{1,0:T(8,128)(2,1)S(1)}, bf16[1024,1024]{1,0:T(8,128)(2,1)}) fusion(f32[1024,1024]{1,0:T(8,128)} %fusion.3, f32[1024,1024]{1,0:T(8,128)} %fusion.2, bf16[1024,2048]{1,0:T(8,128)(2,1)S(1)} %copy-done.6, bf16[2048,1024]{1,0:T(8,128)(2,1)S(1)} %copy-done.8), kind=kOutput, calls=%fused_computation.1 | convolution fusion | flops 4310695936 | bytes 23068672 | tf_op jit(solution)/shard_map/dot_general | solution.py:59
  307.6 0.0 copy-done.9
  307.6 7.0 %fusion.4 = f32[1024,2048]{1,0:T(8,128)} fusion(bf16[1024,1024]{1,0:T(8,128)(2,1)S(1)} %get-tuple-element.111, bf16[2048,1024]{1,0:T(8,128)(2,1)S(1)} %copy-done.9), kind=kOutput, calls=%fused_computation.31 | convolution fusion | flops 4294967296 | bytes 14680064 | tf_op jit(solution)/shard_map/dot_general | solution.py:59
  314.6 9.1 %add_convert_fusion.normed_two_part = bf16[1024,2048]{1,0:T(8,128)(2,1)} fusion(f32[1024,2048]{1,0:T(8,128)} %fusion.4, bf16[1024,1024]{1,0:T(8,128)(2,1)} %get-tuple-element.112, bf16[2048,1024]{1,0:T(8,128)(2,1)S(1)} %copy-done.8), kind=kOutput, calls=%fused_computation | convolution fusion | flops 4299161600 | bytes 18874368 | tf_op jit(solution)/shard_map/dot_general | solution.py:59
  323.6 6.0 convolution_convert_fusion.3.layer_part
  329.7 0.0 copy-start.10
  329.7 6.2 %convolution_convert_fusion.2.dwg_in = bf16[2048,1024]{1,0:T(8,128)(2,1)} fusion(bf16[1024,2048]{1,0:T(8,128)(2,1)S(1)} %copy-done.6, bf16[1024,1024]{1,0:T(8,128)(2,1)S(1)} %get-tuple-element.111), kind=kOutput, calls=%fused_computation.8 | convolution fusion | flops 4297064448 | bytes 10485760 | tf_op jit(solution)/shard_map/dot_general | solution.py:59
  335.9 0.0 copy-done.10
  335.9 6.2 convolution_convert_fusion.1.dwu_in
  342.1 6.2 %convolution_convert_fusion.dwd_in = bf16[1024,2048]{1,0:T(8,128)(2,1)} fusion(bf16[1024,1024]{1,0:T(8,128)(2,1)S(1)} %get-tuple-element.110, bf16[1024,2048]{1,0:T(8,128)(2,1)S(1)} %copy-done.5), kind=kOutput, calls=%fused_computation.6 | convolution fusion | flops 4297064448 | bytes 10485760 | tf_op jit(solution)/shard_map/dot_general | solution.py:59
  348.4 257.1 %back.1 = (bf16[256,2048]{1,0:T(8,128)(2,1)}, bf16[256,2048]{1,0:T(8,128)(2,1)}, bf16[2,4,128,384]{3,2,1,0:T(8,128)(2,1)}, bf16[2,1024,128]{2,1,0:T(8,128)(2,1)}...) custom-call(s32[8]{0:T(128)} %reshape.201.ends, ...), custom_call_target="tpu_custom_call" | custom-call | tf_op jit(solution)/shard_map/back/pallas_call | solution.py:1270
  605.4 1.3 slice_bitcast_fusion.3
  606.7 1.2 add_bitcast_fusion.3
  607.9 0.2 copy.54
  608.1 0.0 copy-start.1
  608.1 1.0 copy.57
  609.1 0.1 slice_bitcast_fusion.1
  609.3 0.1 copy.55
  609.4 0.8 copy.58
  610.2 0.1 copy.56
  610.3 0.8 copy.59
  611.0 1.9 add_bitcast_fusion.4
  612.9 0.0 copy-done.1
  612.9 0.0 copy-start
  612.9 4.4 add_bitcast_fusion.1
  617.3 0.0 copy-start.3
  617.3 0.0 copy-start.2
  617.3 0.0 copy-done
  617.3 1.5 add_bitcast_fusion
  618.8 0.0 copy-done.3
  618.8 1.0 copy.63
  619.8 0.0 copy-done.2
  619.8 1.0 copy.64
  (7 shorter events, 0.1 us)
Async XLA Ops:
  9.0 9.6 %copy-start.4 = (bf16[1,16,128]{2,1,0:T(8,128)(2,1)}, bf16[1,16,128]{2,1,0:T(8,128)(2,1)S(1)}, u32[]{:S(2)}) copy-start(bf16[1,16,128]{2,1,0:T(8,128)(2,1)S(1)} %scatter.9.gain_in) | copy-start | bytes 12292
  281.6 10.1 %copy-start.5 = (bf16[1024,2048]{1,0:T(8,128)(2,1)S(1)}, bf16[1024,2048]{1,0:T(8,128)(2,1)}, u32[]{:S(2)}) copy-start(bf16[1024,2048]{1,0:T(8,128)(2,1)} %get-tuple-element.58) | copy-start | bytes 12582916
  281.6 10.1 %copy-start.7 = (bf16[1024,2048]{1,0:T(8,128)(2,1)S(1)}, bf16[1024,2048]{1,0:T(8,128)(2,1)}, u32[]{:S(2)}) copy-start(bf16[1024,2048]{1,0:T(8,128)(2,1)} %get-tuple-element.59) | copy-start | bytes 12582916
  291.7 6.1 copy-start.6
  291.7 6.1 copy-start.8
  297.8 9.8 %copy-start.9 = (bf16[2048,1024]{1,0:T(8,128)(2,1)S(1)}, bf16[2048,1024]{1,0:T(8,128)(2,1)}, u32[]{:S(2)}) copy-start(bf16[2048,1024]{1,0:T(8,128)(2,1)} %get-tuple-element.62) | copy-start | bytes 12582916
  329.7 6.2 %copy-start.10 = (bf16[1024,1024]{1,0:T(8,128)(2,1)S(1)}, bf16[1024,1024]{1,0:T(8,128)(2,1)}, u32[]{:S(2)}) copy-start(bf16[1024,1024]{1,0:T(8,128)(2,1)} %get-tuple-element.112) | copy-start | bytes 6291460
  608.1 4.8 copy-start.1
  612.9 4.4 copy-start
  617.3 1.5 copy-start.3
  617.3 2.5 copy-start.2

commit v4 on v3

--- a/solution.py
+++ b/solution.py
@@ -457,11 +457,26 @@
     return jnp.where(lane % HD < HD // 2, left, right)
 
 
-def allowed_keys(l, ends, row, span, keys):
+def rope_rows(cos, sin, at, copies):
+    return (
+        jnp.concatenate([cos[at]] * copies, axis=1),
+        jnp.concatenate([sin[at]] * copies, axis=1),
+    )
+
+
+def rope_key_rows(cos, sin, at):
+    lane = lax.broadcasted_iota(jnp.int32, (1, 2 * HD), 1)
+    return (jnp.where(lane < HD, cos[at], 1.0), jnp.where(lane < HD, sin[at], 0.0))
+
+
+def allowed_keys(l, lengths, row, span, keys):
     def segment_of(place):
         total = jnp.zeros_like(place)
+        end = lengths[row * 4]
         for doc in range(4):
-            total = total + (place >= ends[row * 4 + doc]).astype(jnp.int32)
+            if doc:
+                end = end + lengths[row * 4 + doc]
+            total = total + (place >= end).astype(jnp.int32)
         return total
 
     query = l.high * span + lax.broadcasted_iota(jnp.int32, (span, 1), 0)
@@ -471,7 +486,7 @@
 
 def front_kernel(
     sizes,
-    ends,
+    lengths,
     x_in,
     g_in,
     qkv_in,
@@ -484,17 +499,17 @@
     sin_in,
     qkv_out,
     wo_out,
-    wg_out,
-    wu_out,
-    wd_out,
     gain_out,
     normed_one_out,
     q_out,
     kv_out,
     attn_out,
     residual_out,
-    normed_two_out,
-    g_out,
+    dwg_out,
+    dwu_out,
+    dwd_out,
+    normed_two_part,
+    layer_part,
     x_all,
     normed,
     wqkv,
@@ -515,6 +530,13 @@
     both,
     residual,
     normed_two,
+    g_all,
+    wg,
+    wu,
+    wd,
+    hidden,
+    gate_act,
+    up_act,
     send_sem,
     recv_sem,
     local_sem,
@@ -523,7 +545,7 @@
     own = rows * local
     tokens = SQUARE * own
     half = model // 2
-    block = qkv_in.shape[1]
+    block = qkv_in.shape[0]
     heads = q.shape[2] // HD
     span = SQUARE * local
     keys = high_size * span
@@ -549,10 +571,10 @@
 
         return spot
 
-    def column_spot(ref):
+    def row_half_spot(ref):
         def spot(x, h, low, n):
-            start = ((x * high_size + h) * SQUARE + low) * block
-            return ref.at[:, pl.ds(pl.multiple_of(start, block), n * block)]
+            start = pl.multiple_of((h * SQUARE + low) * block, block)
+            return ref.at[x, pl.ds(start, n * block)]
 
         return spot
 
@@ -571,7 +593,7 @@
         return x_all.at[side, part_at(low, part)]
 
     def g_spot(side, low, part=None):
-        return g_out.at[part_at(low, part), pl.ds(pl.multiple_of(side * half, half), half)]
+        return g_all.at[side, part_at(low, part)]
 
     def normed_two_spot(side, low, part=None):
         return normed_two.at[side, part_at(low, part)]
@@ -587,10 +609,10 @@
     loads = [l.local(side_of(x_in, side), x_spot(side, l.low)) for side in range(2)]
     loads += [l.local(cos_in, cos), l.local(sin_in, sin)]
     w_gain = Weight(l, lambda j: gain_in.at[pl.ds(0, 1)], block_spot(gains))
-    w_qkv = Weight(l, lambda j: qkv_in.at[j], row_spot(wqkv))
+    w_qkv = Weight(l, columns(qkv_in, wqkv.shape[1]), row_spot(wqkv))
     x_pushed = gather_push(l, x_spot, own_part_of(x_in))
     w_o = Weight(l, lines(wo_in, wo.shape[1]), half_spot(wo))
-    w_gate = Weight(l, columns(wg_in, wg_out.shape[1]), row_spot(wg_out))
+    w_gate = Weight(l, columns(wg_in, wg.shape[2]), row_half_spot(wg))
 
     w_gain.pass_near()
     w_qkv.pass_near()
@@ -616,21 +638,23 @@
         total = jnp.sum(first * first, axis=1, keepdims=True)
         total = total + jnp.sum(second * second, axis=1, keepdims=True)
         scale = lax.rsqrt(total / model + EPSILON)
-        normed[at, :half] = (first * scale * gain_rows[0:1, :half]).astype(jnp.bfloat16)
-        normed[at, half:] = (second * scale * gain_rows[0:1, half:]).astype(jnp.bfloat16)
+        normed[0, at] = (first * scale * gain_rows[0:1, :half]).astype(jnp.bfloat16)
+        normed[1, at] = (second * scale * gain_rows[0:1, half:]).astype(jnp.bfloat16)
         return carry
 
     lax.fori_loop(0, tokens // step, norm_step, 0)
-    stores = [l.local(normed, normed_one_out)]
+    normed_store = l.local(normed, normed_one_out)
+    stores = []
     w_qkv.wait()
     stores += [l.local(wqkv, qkv_out), l.local(gain_rows, gain_out)]
 
     def project_step(i, carry):
         at = pl.ds(pl.multiple_of(i * local, local), local)
-        pre = dot(normed[at], wqkv[...])
-        times = heads // 2
-        cos_all = jnp.concatenate([cos[at, : 2 * HD]] * times + [cos[at, 2 * HD :]], axis=1)
-        sin_all = jnp.concatenate([sin[at, : 2 * HD]] * times + [sin[at, 2 * HD :]], axis=1)
+        pre = dot(normed[0, at], wqkv[:half]) + dot(normed[1, at], wqkv[half:])
+        cos_q, sin_q = rope_rows(cos, sin, at, heads // 2)
+        cos_k, sin_k = rope_key_rows(cos, sin, at)
+        cos_all = jnp.concatenate([cos_q, cos_k], axis=1)
+        sin_all = jnp.concatenate([sin_q, sin_k], axis=1)
         turned = pre * cos_all + roll_heads(pre) * sin_all
         spot = pl.ds(pl.multiple_of((i // rows) * local, local), local)
         q[i % rows, spot] = (turned[:, : heads * HD].astype(jnp.bfloat16) * HD ** (-0.5)).astype(
@@ -643,12 +667,12 @@
     kv_copy = l.copy(kv.at[l.high], kv.at[l.high], dh=1)
     stores.append(l.local(q, q_out))
     w_gate.pass_near()
-    w_up = Weight(l, columns(wu_in, wu_out.shape[1]), row_spot(wu_out))
+    w_up = Weight(l, columns(wu_in, wu.shape[2]), row_half_spot(wu))
     kv_copy.wait_recv()
     stores.append(l.local(kv, kv_out))
 
     def attend_row(r, carry):
-        allowed = allowed_keys(l, ends, r, span, keys)
+        allowed = allowed_keys(l, lengths, r, span, keys)
         kv_row = kv[:, r].reshape(keys, 2 * HD)
         k, v = kv_row[:, :HD], kv_row[:, HD:]
         q_row = q[r]
@@ -690,7 +714,6 @@
 
     pushed = square_push(l, total_out, send_block, relay, recv_block)
     w_up.pass_near()
-    w_down = Weight(l, lines(wd_in, wd_out.shape[0]), column_spot(wd_out))
     square_settle(l, total_out, pushed, recv_block, both).wait_recv()
     at_own = pl.ds(pl.multiple_of(l.low * own, own), own)
     total = jnp.zeros((own, 1), jnp.float32)
@@ -708,50 +731,115 @@
     pushed = gather_push(
         l, normed_two_spot, lambda part: normed_two_spot(l.core, l.low, part)
     )
+    w_up.pass_far()
+    w_down = Weight(l, lines(wd_in, wd.shape[1]), half_spot(wd))
+    handed, _ = gather_across(l, normed_two_spot, pushed)
     loads = [l.local(side_of(g_in, side), g_spot(side, l.low)) for side in range(2)]
     g_pushed = gather_push(l, g_spot, own_part_of(g_in))
-    w_up.pass_far()
-    handed, _ = gather_across(l, normed_two_spot, pushed)
     w_down.pass_near()
     arrived(handed)
-    for side in range(2):
-        stores.append(l.local(normed_two.at[side], side_of(normed_two_out, side)))
+    normed_store.wait()
+    w_gate.wait()
+    w_up.wait()
+
+    def unit_step(j, carry):
+        at = part_at(j, None)
+        first, second = normed_two[0, at], normed_two[1, at]
+        gate = dot(first, wg[0]) + dot(second, wg[1])
+        up = dot(first, wu[0]) + dot(second, wu[1])
+        sigmoid = jax.nn.sigmoid(gate)
+        silu = gate * sigmoid
+        hidden[at] = (silu * up).astype(jnp.bfloat16)
+        gate_act[at] = (up * sigmoid * (1.0 + gate * (1.0 - sigmoid))).astype(jnp.bfloat16)
+        up_act[at] = silu.astype(jnp.bfloat16)
+        return carry
+
+    lax.fori_loop(0, SQUARE, unit_step, 0)
     g_handed, _ = gather_across(l, g_spot, g_pushed)
     w_down.pass_far()
+    for made in loads:
+        made.wait()
     arrived(g_handed)
-    for weight in (w_gate, w_up, w_down):
-        weight.wait()
-    for made in loads + stores:
+    busy = [(0, None), (1, None)]
+
+    def fill(product, out):
+        k, made = busy.pop(0)
+        if made is not None:
+            made.wait()
+        buffer = normed.at[k]
+
+        def step(i, carry):
+            at = pl.ds(pl.multiple_of(i * own, own), own)
+            buffer[at] = product(at).astype(jnp.bfloat16)
+            return carry
+
+        lax.fori_loop(0, half // own, step, 0)
+        busy.append((k, l.local(buffer, out)))
+
+    for side in range(2):
+        fill(
+            lambda at, side=side: dot(hidden[:, at], g_all[side], ((0,), (0,))),
+            dwd_out.at[side],
+        )
+    w_down.wait()
+
+    def act_step(j, carry):
+        at = part_at(j, None)
+        grad = dot(g_all[0, at], wd[0], ((1,), (1,))) + dot(g_all[1, at], wd[1], ((1,), (1,)))
+        gate_act[at] = (grad * gate_act[at].astype(jnp.float32)).astype(jnp.bfloat16)
+        up_act[at] = (grad * up_act[at].astype(jnp.float32)).astype(jnp.bfloat16)
+        return carry
+
+    lax.fori_loop(0, SQUARE, act_step, 0)
+    for side in range(2):
+        fill(
+            lambda at, side=side: dot(gate_act[at], wg[side], ((1,), (1,)))
+            + dot(up_act[at], wu[side], ((1,), (1,))),
+            normed_two_part.at[side],
+        )
+    for side in range(2):
+        fill(lambda at, side=side: dot(hidden[at], wd[side]), layer_part.at[side])
+    for act, out in ((gate_act, dwg_out), (up_act, dwu_out)):
+        for side in range(2):
+            fill(
+                lambda at, side=side, act=act: dot(
+                    normed_two[side, :, at], act[...], ((0,), (0,))
+                ),
+                out.at[side],
+            )
+    for _, made in busy:
+        made.wait()
+    for made in stores:
         made.wait()
     l.finish()
 
 
-def front(sizes, ends, x, g, qkv, gain, wo, wg, wu, wd, cos, sin):
+def front(sizes, lengths, x, g, qkv, gain, wo, wg, wu, wd, cos, sin):
     rows, local, model, high_size = sizes
     own = rows * local
     tokens = SQUARE * own
     half = model // 2
     heads = wo.shape[0] // SQUARE // HD
-    width = qkv.shape[2]
+    width = qkv.shape[1] // SQUARE
     ff = wg.shape[1] // SQUARE
-    blocks = model // qkv.shape[1]
+    blocks = model // qkv.shape[0]
     span = SQUARE * local
     low, f32 = jnp.bfloat16, jnp.float32
     shape = jax.ShapeDtypeStruct
     outs = (
         shape((model, width), low),
         shape((2, heads * HD, half), low),
-        shape((model, ff), low),
-        shape((model, ff), low),
-        shape((ff, model), low),
         shape((8, model), f32),
-        shape((tokens, model), low),
+        shape((2, tokens, half), low),
         shape((rows, span, heads * HD), low),
         shape((high_size, rows, span, 2 * HD), low),
         shape((tokens, heads * HD), f32),
         shape((own, model), f32),
-        shape((tokens, model), low),
-        shape((tokens, model), low),
+        shape((2, half, ff), low),
+        shape((2, half, ff), low),
+        shape((2, ff, half), low),
+        shape((2, tokens, half), low),
+        shape((2, tokens, half), low),
     )
     anywhere = pl.BlockSpec(memory_space=pl.ANY)
     vmem = pltpu.VMEM
@@ -762,13 +850,13 @@
         out_specs=[anywhere] * len(outs),
         scratch_shapes=[
             vmem((2, tokens, half), low),
-            vmem((tokens, model), low),
+            vmem((2, tokens, half), low),
             vmem((model, width), low),
             vmem((2, heads * HD, half), low),
             vmem((blocks,) + gain.shape[1:], low),
             vmem((8, model), f32),
-            vmem((tokens, 4 * HD), f32),
-            vmem((tokens, 4 * HD), f32),
+            vmem((tokens, 2 * HD), f32),
+            vmem((tokens, 2 * HD), f32),
             vmem((rows, span, heads * HD), low),
             vmem((high_size, rows, span, 2 * HD), low),
             vmem((tokens, heads * HD), f32),
@@ -781,6 +869,13 @@
             vmem((2, own, half), low),
             vmem((own, model), f32),
             vmem((2, tokens, half), low),
+            vmem((2, tokens, half), low),
+            vmem((2, half, ff), low),
+            vmem((2, half, ff), low),
+            vmem((2, ff, half), low),
+            vmem((tokens, ff), low),
+            vmem((tokens, ff), low),
+            vmem((tokens, ff), low),
             pltpu.SemaphoreType.DMA((128,)),
             pltpu.SemaphoreType.DMA((128,)),
             pltpu.SemaphoreType.DMA((32,)),
@@ -789,7 +884,7 @@
             collective_id=0, has_side_effects=True, vmem_limit_bytes=VMEM
         ),
         name="front",
-    )(ends, x, g, qkv, gain, wo, wg, wu, wd, cos, sin)
+    )(lengths, x, g, qkv, gain, wo, wg, wu, wd, cos, sin)
 
 
 class Grad:
@@ -831,7 +926,7 @@
 
 def back_kernel(
     sizes,
-    ends,
+    lengths,
     x_in,
     g_in,
     residual_in,
@@ -921,12 +1016,6 @@
     ]
     l.greet(steps + [dict(dc=1)])
 
-    def side_of(ref, side):
-        return ref.at[:, pl.ds(pl.multiple_of(side * half, half), half)]
-
-    def row_half(ref):
-        return lambda x: ref.at[pl.ds(pl.multiple_of(x * half, half), half)]
-
     def row_block(ref):
         def at(h, low):
             start = pl.multiple_of((h * SQUARE + low) * block, block)
@@ -953,7 +1042,7 @@
         return pl.ds(pl.multiple_of(j * own, own), own)
 
     def part_at(ref, j, side):
-        return ref.at[block_at(j), pl.ds(pl.multiple_of(side * half, half), half)]
+        return ref.at[side, block_at(j)]
 
     handed = [
         l.copy(part_at(normed_two_part, j, 1 - l.core), recv_core.at[j], dc=1)
@@ -966,7 +1055,7 @@
         l.local(g_in, g_own),
     ]
     grad_d = Grad(
-        l, lambda x: side_of(dwd_in, x), kept_d, cross_d, column_block(kept_d), tall(land_d)
+        l, lambda x: dwd_in.at[x], kept_d, cross_d, column_block(kept_d), tall(land_d)
     )
     later = [
         l.local(x_in, x_own),
@@ -1041,7 +1130,7 @@
         return low_all.at[side, pl.ds(start, own // 2)]
 
     low_pushed = gather_push(l, low_spot, lambda part: low_spot(l.core, l.low, part))
-    grad_g = Grad(l, row_half(dwg_in), kept_g, cross_g, row_block(kept_g), broad(land_g))
+    grad_g = Grad(l, lambda x: dwg_in.at[x], kept_g, cross_g, row_block(kept_g), broad(land_g))
     ffn_gains = push_gains(1)
     handed_b = [
         l.copy(part_at(layer_part, j, 1 - l.core), recv_core.at[j], dc=1) for j in range(SQUARE)
@@ -1052,7 +1141,7 @@
     low_handed, low_corner = gather_across(l, low_spot, low_pushed)
     grad_d.deal()
     arrived(low_handed)
-    grad_u = Grad(l, row_half(dwu_in), kept_u, cross_u, row_block(kept_u), broad(land_u))
+    grad_u = Grad(l, lambda x: dwu_in.at[x], kept_u, cross_u, row_block(kept_u), broad(land_u))
 
     def out_grad_step(j, carry):
         at = block_at(j)
@@ -1077,7 +1166,7 @@
     pushed_b = square_push(l, own_total, own_a, relay_b, recv_block_b)
 
     def attend_row(r, carry):
-        allowed = allowed_keys(l, ends, r, span, keys)
+        allowed = allowed_keys(l, lengths, r, span, keys)
         kv_row = kv[:, r].reshape(keys, 2 * HD)
         k, v = kv_row[:, :HD], kv_row[:, HD:]
         q_row, go_row = q[r], attn_grad[r]
@@ -1108,8 +1197,7 @@
         for j in range(SQUARE):
             at = pl.ds(pl.multiple_of(j * own + r * local, local), local)
             value = turned[j * local : (j + 1) * local]
-            cos_q = jnp.concatenate([cos[at, : 2 * HD]] * (heads // 2), axis=1)
-            sin_q = jnp.concatenate([sin[at, : 2 * HD]] * (heads // 2), axis=1)
+            cos_q, sin_q = rope_rows(cos, sin, at, heads // 2)
             dqkv[at, : heads * HD] = (value * cos_q - roll_heads(value) * sin_q).astype(b16)
         both_kv = jnp.concatenate([dk, dv], axis=1)
         for part in range(high_size):
@@ -1122,8 +1210,7 @@
     dkv_send[...] = dkv[1 - l.high].astype(b16)
     dkv_copy = l.copy(dkv_send, dkv_recv, dh=1)
     l.left(low_pushed + low_handed + low_corner)
-    normed = l.local(normed_one_in.at[:, pl.ds(0, half)], low_all.at[0])
-    normed_2 = l.local(normed_one_in.at[:, pl.ds(half, half)], low_all.at[1])
+    normed = l.local(normed_one_in, low_all)
     grad_o.deal()
     both_b_copy = square_settle(l, own_total, pushed_b, recv_block_b, both_b)
     dkv_copy.wait_recv()
@@ -1132,7 +1219,8 @@
         at = pl.ds(pl.multiple_of(i * local, local), local)
         spot = pl.ds(pl.multiple_of((i // rows) * local, local), local)
         kv_sum = dkv[l.high, i % rows, spot] + dkv_recv[i % rows, spot].astype(f32)
-        turned = kv_sum * cos[at, 2 * HD :] - roll_heads(kv_sum) * sin[at, 2 * HD :]
+        cos_k, sin_k = rope_key_rows(cos, sin, at)
+        turned = kv_sum * cos_k - roll_heads(kv_sum) * sin_k
         dqkv[at, heads * HD :] = turned.astype(b16)
         return carry
 
@@ -1149,7 +1237,6 @@
         own_a[j] = project_back(j, 1 - l.core).astype(b16)
         handed.append(l.copy(own_a.at[j], recv_core.at[j], dc=1))
     normed.wait()
-    normed_2.wait()
     send_q[...] = dot(low_all[1 - l.x], dqkv[...], ((0,), (0,))).astype(b16)
     arrived(handed)
 
@@ -1197,13 +1284,13 @@
     l.finish()
 
 
-def back(sizes, ends, *arrays):
+def back(sizes, lengths, *arrays):
     rows, local, model, high_size = sizes
     own = rows * local
     tokens = SQUARE * own
     half = model // 2
     block = model // 16
-    ff = arrays[6].shape[1]
+    ff = arrays[6].shape[2]
     width = arrays[9].shape[1]
     wide = width - 2 * HD
     span = SQUARE * local
@@ -1257,8 +1344,8 @@
         vmem((rows, span, 2 * HD), b16),
         vmem((rows, span, 2 * HD), b16),
         vmem((tokens, width), b16),
-        vmem((tokens, 4 * HD), f32),
-        vmem((tokens, 4 * HD), f32),
+        vmem((tokens, 2 * HD), f32),
+        vmem((tokens, 2 * HD), f32),
         vmem((2, 16, 8, block), f32),
         vmem((2, 16, 8, block), f32),
         vmem((tokens, wide), b16),
@@ -1277,7 +1364,7 @@
             collective_id=1, has_side_effects=True, vmem_limit_bytes=VMEM
         ),
         name="back",
-    )(ends, *arrays)
+    )(lengths, *arrays)
 
 
 def norm_back(values, scale, gain, grad):
@@ -1458,16 +1545,15 @@
     span = SQUARE * local
     width = (group + 2) * HD
 
-    ends = jnp.cumsum(doc_lengths, axis=-1).astype(jnp.int32)
     spots = high * span + jnp.arange(span, dtype=jnp.int32).reshape(SQUARE, 1, local)
-    reached = spots[..., None] >= ends[None, :, None, :]
-    begin = jnp.max(jnp.where(reached, ends[None, :, None, :], 0), axis=-1)
-    position = (spots - begin).astype(jnp.float32).reshape(SQUARE * tokens)
-    angles = position[:, None] * inverse_freqs(HD)
-    cos, sin = jnp.cos(angles), jnp.sin(angles)
-    flat = jnp.zeros((SQUARE * tokens, HD), jnp.float32)
-    cos = jnp.concatenate([cos] * 6 + [flat + 1.0], axis=1)
-    sin = jnp.concatenate([-sin, sin] * 3 + [flat], axis=1)
+    begin, end = jnp.zeros((1, rows, 1), jnp.int32), jnp.zeros((1, rows, 1), jnp.int32)
+    for doc in range(doc_lengths.shape[1]):
+        end = end + doc_lengths[:, doc].reshape(1, rows, 1)
+        begin = jnp.where(spots >= end, end, begin)
+    position = (spots - begin).astype(jnp.float32).reshape(SQUARE * tokens, 1)
+    angles = position * jnp.tile(inverse_freqs(HD), 4)[None, :]
+    sign = jnp.where(jnp.arange(2 * HD) % HD < HD // 2, -1.0, 1.0)[None, :]
+    cos, sin = jnp.cos(angles), jnp.sin(angles) * sign
     qkv_shard = jnp.concatenate(
         [
             query_weight.reshape(block, SQUARE, group * HD),
@@ -1475,28 +1561,31 @@
             value_weight.reshape(block, SQUARE, HD),
         ],
         axis=2,
-    ).transpose(1, 0, 2)
-    gain_shard = jnp.zeros((1, 16, block), jnp.bfloat16)
-    gain_shard = gain_shard.at[0, 0].set(attn_gain).at[0, 1].set(ffn_gain)
+    ).reshape(block, SQUARE * width)
+    gain_shard = jnp.concatenate(
+        [attn_gain[None, None], ffn_gain[None, None], jnp.zeros((1, 14, block), jnp.bfloat16)],
+        axis=1,
+    )
+    lengths = doc_lengths.reshape(-1)
     own_in = hidden_in.reshape(tokens, model)
     own_grad = out_grad.reshape(tokens, model)
     (
         qkv_own,
         output_own,
-        gate_own,
-        up_own,
-        down_own,
         gains,
         normed_one,
         queries,
         kv,
         attn,
         residual,
-        normed_two,
-        all_grad,
+        gate_part,
+        up_part,
+        down_part,
+        normed_two_part,
+        layer_part,
     ) = front(
         (rows, local, model, high_size),
-        ends.reshape(-1),
+        lengths,
         own_in,
         own_grad,
         qkv_shard,
@@ -1508,21 +1597,6 @@
         cos,
         sin,
     )
-    gate_proj = dot(normed_two, gate_own)
-    up_proj = dot(normed_two, up_own)
-    sigmoid_gate = jax.nn.sigmoid(gate_proj)
-    silu_gate = gate_proj * sigmoid_gate
-    hidden_units = (silu_gate * up_proj).astype(jnp.bfloat16)
-    hidden_grad = dot(all_grad, down_own, ((1,), (1,)))
-    gate_act = (
-        hidden_grad * up_proj * sigmoid_gate * (1.0 + gate_proj * (1.0 - sigmoid_gate))
-    ).astype(jnp.bfloat16)
-    up_act = (hidden_grad * silu_gate).astype(jnp.bfloat16)
-    down_part = dot(hidden_units, all_grad, ((0,), (0,))).astype(jnp.bfloat16)
-    gate_part = dot(normed_two, gate_act, ((0,), (0,))).astype(jnp.bfloat16)
-    up_part = dot(normed_two, up_act, ((0,), (0,))).astype(jnp.bfloat16)
-    normed_two_part = dot(gate_act, gate_own, ((1,), (1,))) + dot(up_act, up_own, ((1,), (1,)))
-    layer_part = dot(hidden_units, down_own).astype(jnp.bfloat16)
     (
         layer_out,
         input_grad,
@@ -1530,12 +1604,12 @@
         gain_grads,
     ) = back(
         (rows, local, model, high_size),
-        ends.reshape(-1),
+        lengths,
         own_in,
         own_grad,
         residual,
         gains,
-        normed_two_part.astype(jnp.bfloat16),
+        normed_two_part,
         layer_part,
         gate_part,
         up_part,

time: 628 us -> 588 us (0.936)
  matrix products: 66.7 us -> 0 us
  Pallas kernels: 520 us -> 550 us
    dot_general x9 -> x0, matrix products: 66.7 us -> none  [dot(): lax.dot_general(left, right, (dims, ((), ())), preferred_element_type=jnp...]
    pallas_call x1, Pallas kernels: 263 us -> 299 us  [front(): pl.pallas_call(functools.partial(front_kernel, sizes), out_shape=outs, in...]
    concatenate x2 -> x1, local copies, waits for them, and re-layouts: 7.48 us -> 0.08 us  [shards(): jnp.concatenate([attn_gain[None, None], ffn_gain[None, None], jnp.zeros((...]
where the time goes in v4:
time: 588 us; the launch traced here: 579 us
  Pallas kernels  550 us (94%)
  local copies, waits for them, and re-layouts  15.3 us (3%)
  other arithmetic  12.1 us (2%)
    pallas_call x1, Pallas kernels, front(): pl.pallas_call(functools.partial(front_kernel, sizes), out_shape=outs, in...  299 us
    pallas_call x1, Pallas kernels, back(): pl.pallas_call(functools.partial(back_kernel, sizes), out_shape=outs, in_...  251 us

profile of v4, /device:TPU:0, one launch (start us, length us, event | category | flops | bytes accessed | tf_op | source)
XLA Modules:
  0.0 578.6 jit_solution(9358382340453864780)
XLA Ops:
  0.7 1.3 reshape.260.lengths
  1.9 0.1 pad.2.clone
  2.1 0.1 mul.46
  2.2 1.0 slice_reduce_fusion
  3.2 0.1 ge.68
  3.3 0.1 ge.77
  3.3 1.3 maximum_maximum_fusion.gain_in
  4.7 0.1 ge.71
  4.8 0.1 ge.74
  4.8 0.9 copy.23
  5.8 0.1 copy.25
  5.9 1.0 copy.24
  6.9 0.1 copy.26
  7.1 1.1 reshape.263
  8.2 0.3 pad_maximum_fusion
  8.5 0.8 copy.33
  9.3 3.0 fusion
  12.3 299.1 %front.1 = (bf16[2048,384]{1,0:T(8,128)(2,1)}, bf16[2,256,1024]{2,1,0:T(8,128)(2,1)}, f32[8,2048]{1,0:T(8,128)}, bf16[2,1024,1024]{2,1,0:T(8,128)(2,1)}, bf16[2,...) custom-call(s32[8]{0:T(128)} %reshape.260.lengths, ...), custom_call_target="tpu_custom_call" | custom-call | tf_op jit(solution)/shard_map/front/pallas_call | solution.py:846
  311.4 250.9 %back.1 = (bf16[256,2048]{1,0:T(8,128)(2,1)}, bf16[256,2048]{1,0:T(8,128)(2,1)}, bf16[2,4,128,384]{3,2,1,0:T(8,128)(2,1)}, bf16[2,1024,128]{2,1,0:T(8,128)(2,1)}...) custom-call(s32[8]{0:T(128)} %reshape.260.lengths, ...), custom_call_target="tpu_custom_call" | custom-call | tf_op jit(solution)/shard_map/back/pallas_call | solution.py:1357
  562.3 1.3 slice_bitcast_fusion.3
  563.6 1.9 add_bitcast_fusion.4
  565.5 1.2 add_bitcast_fusion.3
  566.7 0.0 copy-start
  566.7 0.1 slice_bitcast_fusion.1
  566.9 0.1 copy.29
  567.0 0.8 copy.32
  567.8 0.2 copy.27
  568.0 1.0 copy.30
  569.0 0.1 copy.28
  569.1 0.8 copy.31
  569.8 0.0 copy-done
  569.8 0.0 copy-start.1
  569.8 0.0 copy-start.2
  569.8 1.5 add_bitcast_fusion
  571.4 0.8 copy-done.1
  572.2 0.6 copy-done.2
  572.8 0.0 copy-start.4
  572.8 2.7 add_bitcast_fusion.1
  575.5 0.0 copy-start.3
  575.5 0.0 copy-done.4
  575.5 1.0 copy.36
  576.5 0.6 copy-done.3
  577.1 1.0 copy.37
  (9 shorter events, 0.1 us)
Async XLA Ops:
  566.7 3.1 copy-start
  569.8 2.3 copy-start.1
  569.8 3.0 copy-start.2
  572.8 2.7 copy-start.4
  575.5 1.6 copy-start.3

commit v5 on v4

--- a/solution.py
+++ b/solution.py
@@ -417,7 +417,7 @@
     return handed, corner
 
 
-def square_push(l, total_of, send, relay, landed):
+def square_push(l, total_of, send, relay, landed, split=False):
     lines = send.shape[1]
     first, second = pl.ds(0, lines // 2), pl.ds(lines // 2, lines // 2)
     one, two, corner = (l.beside(flip) for flip in (1, 2, 3))
@@ -430,6 +430,15 @@
     made.append(l.copy(send.at[one, first], landed.at[0, first], flip=1))
     send[two] = total_of(two).astype(jnp.bfloat16)
     made.append(l.copy(send.at[two, second], landed.at[1, second], flip=2))
+    if not split:
+        square_relay(l, made, send, relay, landed)
+    return made
+
+
+def square_relay(l, made, send, relay, landed):
+    lines = send.shape[1]
+    first, second = pl.ds(0, lines // 2), pl.ds(lines // 2, lines // 2)
+    one, two = l.beside(1), l.beside(2)
     made[0].wait_recv()
     value = send[two, first].astype(jnp.float32) + relay[0].astype(jnp.float32)
     send[two, first] = value.astype(jnp.bfloat16)
@@ -438,7 +447,6 @@
     value = send[one, second].astype(jnp.float32) + relay[1].astype(jnp.float32)
     send[one, second] = value.astype(jnp.bfloat16)
     made.append(l.copy(send.at[one, second], landed.at[0, second], flip=1))
-    return made
 
 
 def square_settle(l, total_of, made, landed, both):
@@ -472,10 +480,10 @@
 def allowed_keys(l, lengths, row, span, keys):
     def segment_of(place):
         total = jnp.zeros_like(place)
-        end = lengths[row * 4]
+        end = lengths[row, 0]
         for doc in range(4):
             if doc:
-                end = end + lengths[row * 4 + doc]
+                end = end + lengths[row, doc]
             total = total + (place >= end).astype(jnp.int32)
         return total
 
@@ -1163,7 +1171,7 @@
     for made in owned:
         made.wait()
     arrived(handed_b)
-    pushed_b = square_push(l, own_total, own_a, relay_b, recv_block_b)
+    pushed_b = square_push(l, own_total, own_a, relay_b, recv_block_b, split=True)
 
     def attend_row(r, carry):
         allowed = allowed_keys(l, lengths, r, span, keys)
@@ -1204,16 +1212,19 @@
             dkv[part, r] = both_kv[part * span : (part + 1) * span]
         return carry
 
-    lax.fori_loop(0, 1, attend_row, 0)
-    grad_g.deal()
-    lax.fori_loop(1, rows, attend_row, 0)
-    dkv_send[...] = dkv[1 - l.high].astype(b16)
-    dkv_copy = l.copy(dkv_send, dkv_recv, dh=1)
+    dkv_copies = []
+    for r in range(rows):
+        lax.fori_loop(r, r + 1, attend_row, 0)
+        dkv_send[r] = dkv[1 - l.high, r].astype(b16)
+        dkv_copies.append(l.copy(dkv_send.at[r], dkv_recv.at[r], dh=1))
+        if r == 0:
+            square_relay(l, pushed_b, own_a, relay_b, recv_block_b)
+            grad_g.deal()
     l.left(low_pushed + low_handed + low_corner)
     normed = l.local(normed_one_in, low_all)
     grad_o.deal()
     both_b_copy = square_settle(l, own_total, pushed_b, recv_block_b, both_b)
-    dkv_copy.wait_recv()
+    arrived(dkv_copies)
 
     def unrotate_step(i, carry):
         at = pl.ds(pl.multiple_of(i * local, local), local)
@@ -1566,7 +1577,7 @@
         [attn_gain[None, None], ffn_gain[None, None], jnp.zeros((1, 14, block), jnp.bfloat16)],
         axis=1,
     )
-    lengths = doc_lengths.reshape(-1)
+    lengths = doc_lengths
     own_in = hidden_in.reshape(tokens, model)
     own_grad = out_grad.reshape(tokens, model)
     (

time: 588 us -> 583 us (level)
  no operation moved by 1% of the time
where the time goes in v5:
time: 583 us; the launch traced here: 573 us
  Pallas kernels  546 us (94%)
  local copies, waits for them, and re-layouts  14 us (2%)
  other arithmetic  12.1 us (2%)
    pallas_call x1, Pallas kernels, front(): pl.pallas_call(functools.partial(front_kernel, sizes), out_shape=outs, in...  299 us
    pallas_call x1, Pallas kernels, back(): pl.pallas_call(functools.partial(back_kernel, sizes), out_shape=outs, in_...  247 us

profile of v5, /device:TPU:0, one launch (start us, length us, event | category | flops | bytes accessed | tf_op | source)
XLA Modules:
  0.0 573.4 jit_solution(15569124608383405112)
XLA Ops:
  0.7 0.1 pad.2.clone
  0.8 0.1 mul.46
  0.9 1.0 slice_reduce_fusion
  1.9 0.1 ge.68
  2.0 0.1 ge.77
  2.1 1.3 maximum_maximum_fusion.gain_in
  3.4 0.1 ge.71
  3.5 0.1 ge.74
  3.6 0.9 copy.23
  4.5 0.1 copy.25
  4.7 1.0 copy.24
  5.6 0.1 copy.26
  5.8 1.1 reshape.259
  6.9 0.3 pad_maximum_fusion
  7.2 0.8 copy.33
  8.0 3.0 fusion
  11.1 299.1 %front.1 = (bf16[2048,384]{1,0:T(8,128)(2,1)}, bf16[2,256,1024]{2,1,0:T(8,128)(2,1)}, f32[8,2048]{1,0:T(8,128)}, bf16[2,1024,1024]{2,1,0:T(8,128)(2,1)}, bf16[2,...) custom-call(s32[2,4]{1,0:T(2,128)} %lengths.3, ...), custom_call_target="tpu_custom_call" | custom-call | tf_op jit(solution)/shard_map/front/pallas_call | solution.py:854
  310.2 247.0 %back.1 = (bf16[256,2048]{1,0:T(8,128)(2,1)}, bf16[256,2048]{1,0:T(8,128)(2,1)}, bf16[2,4,128,384]{3,2,1,0:T(8,128)(2,1)}, bf16[2,1024,128]{2,1,0:T(8,128)(2,1)}...) custom-call(s32[2,4]{1,0:T(2,128)} %lengths.3, ...), custom_call_target="tpu_custom_call" | custom-call | tf_op jit(solution)/shard_map/back/pallas_call | solution.py:1368
  557.2 1.3 slice_bitcast_fusion.3
  558.5 1.9 add_bitcast_fusion.4
  560.3 1.2 add_bitcast_fusion.3
  561.6 0.0 copy-start
  561.6 0.1 slice_bitcast_fusion.1
  561.7 0.1 copy.29
  561.8 0.8 copy.32
  562.6 0.2 copy.27
  562.8 1.0 copy.30
  563.8 0.1 copy.28
  563.9 0.8 copy.31
  564.7 0.0 copy-done
  564.7 0.0 copy-start.1
  564.7 0.0 copy-start.2
  564.7 1.5 add_bitcast_fusion
  566.2 0.8 copy-done.1
  567.0 0.6 copy-done.2
  567.7 0.0 copy-start.4
  567.7 2.7 add_bitcast_fusion.1
  570.4 0.0 copy-start.3
  570.4 0.0 copy-done.4
  570.4 1.0 copy.36
  571.4 0.6 copy-done.3
  572.0 1.0 copy.37
  (9 shorter events, 0.1 us)
Async XLA Ops:
  561.6 3.1 copy-start
  564.7 2.3 copy-start.1
  564.7 3.0 copy-start.2
  567.7 2.7 copy-start.4
  570.4 1.6 copy-start.3

commit v6 on v5

--- a/solution.py
+++ b/solution.py
@@ -1260,6 +1260,7 @@
     grad_q.cross = l.copy(send_q, cross_q, dx=1)
     kept_q[...] = dot(low_all[l.x], dqkv[...], ((0,), (0,))).astype(b16)
     grad_u.deal()
+    grad_q.deal()
     square_settle(l, own_total_c, pushed, recv_block, both).wait_recv()
     outs = norm_back(
         lambda side: x_own[:, side * half : (side + 1) * half].astype(f32),
@@ -1272,7 +1273,6 @@
         x_own[:, at] = (residual[:, at] + outs[side]).astype(b16)
     stores = [l.local(x_own, input_out)]
     residual_load = l.local(residual_in, residual)
-    grad_q.deal()
     residual_load.wait()
     for side in range(2):
         at = slice(side * half, (side + 1) * half)

time: 583 us -> 583 us (level)
  no operation moved by 1% of the time
where the time goes in v6:
time: 583 us; the launch traced here: 574 us
  Pallas kernels  546 us (94%)
  local copies, waits for them, and re-layouts  14 us (2%)
  other arithmetic  12.1 us (2%)
    pallas_call x1, Pallas kernels, front(): pl.pallas_call(functools.partial(front_kernel, sizes), out_shape=outs, in...  299 us
    pallas_call x1, Pallas kernels, back(): pl.pallas_call(functools.partial(back_kernel, sizes), out_shape=outs, in_...  247 us

profile of v6, /device:TPU:0, one launch (start us, length us, event | category | flops | bytes accessed | tf_op | source)
XLA Modules:
  0.0 573.7 jit_solution(17307045107469901523)
XLA Ops:
  0.7 0.1 pad.2.clone
  0.8 0.1 mul.46
  0.9 1.0 slice_reduce_fusion
  1.9 0.1 ge.68
  2.0 0.1 ge.77
  2.1 1.3 maximum_maximum_fusion.gain_in
  3.4 0.1 ge.71
  3.5 0.1 ge.74
  3.6 0.9 copy.23
  4.5 0.1 copy.25
  4.7 1.0 copy.24
  5.6 0.1 copy.26
  5.8 1.1 reshape.259
  6.9 0.3 pad_maximum_fusion
  7.2 0.8 copy.33
  8.0 3.0 fusion
  11.1 299.1 %front.1 = (bf16[2048,384]{1,0:T(8,128)(2,1)}, bf16[2,256,1024]{2,1,0:T(8,128)(2,1)}, f32[8,2048]{1,0:T(8,128)}, bf16[2,1024,1024]{2,1,0:T(8,128)(2,1)}, bf16[2,...) custom-call(s32[2,4]{1,0:T(2,128)} %lengths.3, ...), custom_call_target="tpu_custom_call" | custom-call | tf_op jit(solution)/shard_map/front/pallas_call | solution.py:854
  310.2 247.2 %back.1 = (bf16[256,2048]{1,0:T(8,128)(2,1)}, bf16[256,2048]{1,0:T(8,128)(2,1)}, bf16[2,4,128,384]{3,2,1,0:T(8,128)(2,1)}, bf16[2,1024,128]{2,1,0:T(8,128)(2,1)}...) custom-call(s32[2,4]{1,0:T(2,128)} %lengths.3, ...), custom_call_target="tpu_custom_call" | custom-call | tf_op jit(solution)/shard_map/back/pallas_call | solution.py:1368
  557.4 1.3 slice_bitcast_fusion.3
  558.7 1.9 add_bitcast_fusion.4
  560.6 1.2 add_bitcast_fusion.3
  561.8 0.0 copy-start
  561.8 0.1 slice_bitcast_fusion.1
  562.0 0.1 copy.29
  562.1 0.8 copy.32
  562.9 0.2 copy.27
  563.1 1.0 copy.30
  564.1 0.1 copy.28
  564.2 0.8 copy.31
  564.9 0.0 copy-done
  564.9 0.0 copy-start.1
  564.9 0.0 copy-start.2
  564.9 1.5 add_bitcast_fusion
  566.5 0.8 copy-done.1
  567.3 0.6 copy-done.2
  567.9 0.0 copy-start.4
  567.9 2.7 add_bitcast_fusion.1
  570.6 0.0 copy-start.3
  570.6 0.0 copy-done.4
  570.6 1.0 copy.36
  571.6 0.6 copy-done.3
  572.2 1.0 copy.37
  (9 shorter events, 0.1 us)
Async XLA Ops:
  561.8 3.1 copy-start
  564.9 2.3 copy-start.1
  564.9 3.0 copy-start.2
  567.9 2.7 copy-start.4
  570.6 1.6 copy-start.3
